TPU v7x, 1024 devices: a whole 4x4x32 slice. The times are simulated.
1024 devices in a mesh: grp: 32 (over z), ep: 32 (over y, x, core).
Axes of the slice: x: 4, y: 4, z: 32, core: 2. Of those that a mesh axis runs over, the one named last changes fastest.
Arguments:
- tokens: bfloat16 [1024, 7168], P(('grp', 'ep')), may hold values from -6 to 6
- expert_ids: int32 [32, 32, 8], P('grp', 'ep'), may hold values from 0 to 31, all different within a row; in each aligned block of 32 rows (0 to 31, 32 to 63, ..., all dimensions but the last counted through in order) at most 8 rows name the same one
- affinity: bfloat16 [32, 32, 8], P('grp', 'ep'), may hold values from 0.3984375 to 1
- gate_up_blocks: bfloat16 [32, 32, 3584, 256], P('grp', 'ep'), may hold values from -0.0625 to 0.0625
- down_blocks: bfloat16 [32, 32, 128, 3584], P('grp', 'ep'), may hold values from -0.125 to 0.125
- queries: bfloat16 [1024, 128, 576], P(('grp', 'ep')), may hold values from -10 to 10
- latent_pool: bfloat16 [8192, 64, 576], P(('grp', 'ep')), may hold values from -6 to 6
- page_moves: int32 [1024, 4], P(('grp', 'ep')), may hold values from 0 to 7, as said below
- page_list: int32 [1024, 8], P(('grp', 'ep')), may hold values from 0 to 11, as said below
- lengths: int32 [1024], P(('grp', 'ep')), may hold values from 257 to 512, as said below
Outputs:
- attention_latent: bfloat16 [1024, 128, 512], P(('grp', 'ep'))
- expert_mix: bfloat16 [1024, 7168], P(('grp', 'ep'))
Inputs may be any that keep to these rules, and one draw needn't show every extreme that they name: `expert_ids`: each token names 8 distinct experts; the 32 tokens of one grp index name every expert exactly 8 times. `page_moves`: distinct local page numbers in each row. `page_list`: distinct numbers in each row; page numbers 8 and above are the received pages (2 from below, then 2 from above), and they fill the first 4 entries in some order; the rest are local pages that the device does not hand over. `lengths`: every received page is read in full; some request reaches 512.
All inputs are finite; a program needn't handle non-finite values.
Results may differ from a plain program's by a relative error of at most 0.024.
Values may be sent and summed in bfloat16 or wider, within the bound.
No kernel may reach another device: no remote copies, remote signals or barrier semaphores. Data moves between devices by JAX's collectives and lax.ppermute only.
A program may use at most 64 MiB of HBM per device.

v0:
```python
import jax
import jax.numpy as jnp
from jax import lax
from jax.sharding import PartitionSpec as P

KVL = 512


softmax_scale = 192.0 ** (-0.5)
routed_scale = 2.5


def with_halo(block, sides, width):
    for axis, dim in sides:
        count = lax.axis_size(axis)
        forward = [(i, i + 1) for i in range(count - 1)]
        forward.append((count - 1, 0))
        backward = [(target, source) for source, target in forward]
        low = lax.ppermute(
            lax.slice_in_dim(block, block.shape[dim] - width, None, axis=dim), axis, forward
        )
        high = lax.ppermute(lax.slice_in_dim(block, 0, width, axis=dim), axis, backward)
        block = jnp.concatenate([low, block, high], axis=dim)
    return block


def swapped(value, axis, apart):
    mask = 2**apart
    pairs = [(source, source ^ mask) for source in range(lax.axis_size(axis))]
    return lax.ppermute(value, axis, pairs)


def attention_part(queries, latent_pool, page_moves, page_list, lengths):
    outgoing = page_moves.reshape(-1)
    moving = outgoing.shape[0] // 2
    departing = jnp.take(latent_pool, outgoing, axis=0)
    bordered = with_halo(departing, (("ep", 0),), moving)
    extended = jnp.concatenate([latent_pool, bordered[:moving], bordered[3 * moving :]], axis=0)
    latent_rows = jnp.take(extended, page_list.reshape(-1), axis=0)
    latent_rows = latent_rows.reshape(-1, latent_pool.shape[2])
    query_rows = queries.reshape(queries.shape[1], queries.shape[2])
    scores = jnp.dot(query_rows, latent_rows.T, preferred_element_type=jnp.float32) * softmax_scale
    in_range = jnp.arange(latent_rows.shape[0]) < lengths[0]
    scores = jnp.where(in_range[None, :], scores, -1e30)
    attention_weights = jax.nn.softmax(scores, axis=-1).astype(jnp.bfloat16)
    mixed_latent = jnp.dot(
        attention_weights, latent_rows[:, :KVL], preferred_element_type=jnp.float32
    )
    return mixed_latent.astype(jnp.bfloat16).reshape(1, query_rows.shape[0], KVL)


def expert_part(tokens, expert_ids, affinity, gate_up_blocks, down_blocks):
    group_size = lax.axis_size("ep")
    group_count = lax.axis_size("grp")
    half_split = group_size // 2
    half_index = lax.axis_index("ep") // half_split
    model_width = tokens.shape[1]
    half_width = model_width // 2
    chosen_local = expert_ids.reshape(1, -1)
    affinity_local = affinity.reshape(1, -1)
    gate_up = gate_up_blocks.reshape(gate_up_blocks.shape[2], gate_up_blocks.shape[3])
    unit_count = gate_up.shape[1] // 2
    down_matrix = down_blocks.reshape(down_blocks.shape[2], down_blocks.shape[3])
    swap_bit = half_split.bit_length() - 1
    token_rows, chosen_all, affinity_all = (
        lax.all_gather(tokens, "ep", axis=0, tiled=True),
        lax.all_gather(chosen_local, "ep", axis=0, tiled=True),
        lax.all_gather(affinity_local, "ep", axis=0, tiled=True),
    )
    token_block = lax.dynamic_slice_in_dim(token_rows, half_index * half_width, half_width, 1)
    affinity_float = affinity_all.astype(jnp.float32)
    route_weights = routed_scale * affinity_float / jnp.sum(affinity_float, axis=1, keepdims=True)
    expert_number = jnp.arange(group_count, dtype=jnp.int32)
    matches = chosen_all[:, :, None] == expert_number[None, None, :]
    member = jnp.any(matches, axis=1).astype(jnp.int32)
    weight_of = jnp.sum(jnp.where(matches, route_weights[:, :, None], 0.0), axis=1)
    position = jnp.cumsum(member, axis=0) - member
    capacity = group_size * chosen_local.shape[1] // group_count
    slot_number = jnp.arange(capacity, dtype=jnp.int32)
    selector = (member.T[:, None, :] == 1) & (position.T[:, None, :] == slot_number[None, :, None])
    selector_matrix = selector.astype(jnp.bfloat16)
    outgoing_rows = jnp.einsum(
        "esn,nc->esc", selector_matrix, token_block, preferred_element_type=jnp.float32
    ).astype(jnp.bfloat16)
    arrived = lax.all_to_all(outgoing_rows, "grp", split_axis=0, concat_axis=0, tiled=True)
    partial_sum = jnp.dot(
        arrived.reshape(-1, half_width), gate_up, preferred_element_type=jnp.float32
    )
    layout = arrived.shape
    partner_sum = swapped(partial_sum.astype(jnp.bfloat16), "ep", swap_bit).astype(
        partial_sum.dtype
    )
    combined = partial_sum + partner_sum
    activation = (jax.nn.silu(combined[:, :unit_count]) * combined[:, unit_count:]).astype(
        jnp.bfloat16
    )
    partial_out = jnp.dot(activation, down_matrix, preferred_element_type=jnp.float32).astype(
        jnp.bfloat16
    )
    partial_out = partial_out.reshape(layout[0], layout[1], half_width)
    returned_rows = lax.all_to_all(partial_out, "grp", split_axis=0, concat_axis=0, tiled=True)
    weighted = jnp.where(selector, weight_of.T[:, None, :], 0.0)
    contribution = jnp.einsum(
        "esn,esc->nc", weighted, returned_rows.astype(jnp.float32), precision=lax.Precision.HIGHEST
    )
    spread = jnp.zeros((group_size, model_width), jnp.float32)
    spread = lax.dynamic_update_slice_in_dim(spread, contribution, half_index * half_width, 1)
    summed = lax.psum_scatter(spread.astype(jnp.bfloat16), "ep", scatter_dimension=0, tiled=True)
    return summed


def shards(
    tokens,
    expert_ids,
    affinity,
    gate_up_blocks,
    down_blocks,
    queries,
    latent_pool,
    page_moves,
    page_list,
    lengths,
):
    attention_latent = attention_part(queries, latent_pool, page_moves, page_list, lengths)
    expert_mix = expert_part(tokens, expert_ids, affinity, gate_up_blocks, down_blocks)
    return (attention_latent, expert_mix)


def solution(mesh):
    placed = (
        P(("grp", "ep"), None),
        P("grp", "ep", None),
        P("grp", "ep", None),
        P("grp", "ep", None, None),
        P("grp", "ep", None, None),
        P(("grp", "ep"), None, None),
        P(("grp", "ep"), None, None),
        P(("grp", "ep"), None),
        P(("grp", "ep"), None),
        P(("grp", "ep")),
    )
    return jax.shard_map(
        shards,
        mesh=mesh,
        in_specs=placed,
        out_specs=(P(("grp", "ep"), None, None), P(("grp", "ep"), None)),
        check_vma=False,
    )
```

profile of v0, /device:TPU:1, one launch (start us, length us, event | category | flops | bytes accessed | tf_op | source)
XLA Modules:
  0.0 621.2 jit_solution(12796455067844390362)
XLA Ops:
  7.2 0.0 copy-start
  7.2 36.8 %all-gather.2 = bf16[32,1,7168]{2,1,0:T(2,128)(2,1)S(1)} all-gather(bf16[1,1,7168]{2,1,0:T(2,128)(2,1)} %bitcast.62), channel_id=1, replica_groups=mesh['grp'=32,'ep'=32] {'ep'}, dimensions={0}, use_global_device_ids=true | all-gather | bytes 473088 | tf_op jit(solution)/shard_map/all_gather | solution.py:66
  44.0 20.5 %all-gather = s32[32,1,8]{2,1,0:T(1,128)S(1)} all-gather(s32[1,1,8]{2,1,0:T(1,128)} %param.11), channel_id=2, replica_groups=mesh['grp'=32,'ep'=32] {'ep'}, dimensions={0}, use_global_device_ids=true | all-gather | bytes 1056 | tf_op jit(solution)/shard_map/all_gather | solution.py:67
  64.5 0.1 copy.26
  64.6 0.1 copy.27
  64.7 0.1 reduce_window_sum.11
  64.8 0.1 copy.31
  64.9 0.5 constant_dynamic-slice_fusion.1
  65.4 0.6 convolution_convert_fusion.1
  66.1 194.9 %all_to_all.10 = bf16[32,8,3584]{2,1,0:T(8,128)(2,1)S(1)} all-to-all(bf16[32,8,3584]{2,1,0:T(8,128)(2,1)S(1)} %convolution_convert_fusion.1), channel_id=1, replica_groups=mesh['grp'=32,'ep'=32] {'grp'}, dimensions={0} | all-to-all | bytes 3670016 | tf_op jit(solution)/shard_map/all_to_all | solution.py:85
  261.0 0.0 copy-done
  261.0 0.0 copy-start.3
  261.0 0.6 fusion.31
  261.6 3.9 collective-permute-start.2
  265.6 3.3 collective-permute-done.2
  268.9 0.0 copy-done.3
  268.9 1.9 fusion
  270.7 0.0 copy-start.6
  270.7 0.0 copy-start.2
  270.7 4.9 all-to-all-start.1
  275.6 0.0 copy-start.5
  275.6 0.0 copy-start.7
  275.6 0.0 all-reduce.3.cloned.1.call-start
  275.7 0.0 copy-done.6
  275.7 0.0 copy-done.2
  275.7 0.6 gather_fusion
  276.4 0.1 broadcast_select_fusion.1
  276.5 4.6 collective-permute-start
  281.1 1.9 collective-permute-start.1
  283.1 0.0 copy-done.5
  283.1 23.0 %all-gather.1 = bf16[32,1,8]{2,1,0:T(2,128)(2,1)S(1)} all-gather(bf16[1,1,8]{2,1,0:T(2,128)(2,1)S(1)} %copy-done.5), channel_id=3, replica_groups=mesh['grp'=32,'ep'=32] {'ep'}, dimensions={0}, use_global_device_ids=true | all-gather | bytes 528 | tf_op jit(solution)/shard_map/all_gather | solution.py:68
  306.0 0.3 convert_reduce_fusion
  306.4 0.1 broadcast_divide_fusion
  306.4 0.1 copy.28
  307.2 0.0 copy-done.7
  307.3 0.1 copy.29
  307.3 0.1 broadcast_in_dim.82
  307.4 0.1 broadcast_in_dim.83
  307.5 1.3 dynamic-slice.1
  308.8 0.0 collective-permute-done
  308.8 0.0 copy-start.4
  308.8 0.6 copy-done.4
  309.5 0.0 collective-permute-done.1
  309.5 1.2 pad_maximum_fusion
  310.7 0.7 gather_fusion.1
  311.3 0.1 broadcast_select_fusion
  311.5 1.3 fusion.30
  312.7 133.0 %all-to-all-done.1 = bf16[32,8,3584]{2,1,0:T(8,128)(2,1)} async-done(((bf16[32,8,3584]{2,1,0:T(8,128)(2,1)}), bf16[32,8,3584]{2,1,0:T(8,128)(2,1)}, u32[]{:S(2)}, u32[]{:S(2)}) %all-to-all-start.1) | async-done | bytes 1835040 | tf_op jit(solution)/shard_map/all_to_all | solution.py:101
  445.8 3.3 fusion.1
  449.0 0.0 copy-start.1
  449.0 0.8 copy-done.1
  449.8 0.0 all-reduce.3.cloned.1.call-update
  449.8 0.1 fusion.11
  449.9 1.0 fusion.7
  450.9 161.3 %all-reduce.3.cloned.1.call-done = bf16[32,7168]{1,0:T(8,128)(2,1)} async-done(((bf16[32,7168]{1,0:T(8,128)(2,1)}), bf16[32,7168]{1,0:T(8,128)(2,1)}) %all-reduce.3.cloned.1.call-update) | async-done | bytes 458768
  612.2 2.2 constant_dynamic-slice_fusion
  (15 shorter events, 0.2 us)
Async XLA Ops:
  7.2 253.8 %copy-start = (bf16[1,1,3584,256]{3,2,1,0:T(8,128)(2,1)S(1)}, bf16[1,1,3584,256]{3,2,1,0:T(8,128)(2,1)}, u32[]{:S(2)}) copy-start(bf16[1,1,3584,256]{3,2,1,0:T(8,128)(2,1)} %param.13) | copy-start | bytes 5505028
  261.0 7.9 %copy-start.3 = (bf16[1,1,128,3584]{3,2,1,0:T(8,128)(2,1)S(1)}, bf16[1,1,128,3584]{3,2,1,0:T(8,128)(2,1)}, u32[]{:S(2)}) copy-start(bf16[1,1,128,3584]{3,2,1,0:T(8,128)(2,1)} %param.14) | copy-start | bytes 2752516
  261.6 7.2 %collective-permute-start.2 = (bf16[256,256]{1,0:T(8,128)(2,1)S(1)}, bf16[256,256]{1,0:T(8,128)(2,1)S(1)}, u32[]{:S(2)}, u32[]{:S(2)}) collective-permute-start(bf16[256,256]{1,0:T(8,128)(2,1)S(1)} %get-tuple-element.10), channel_id=1, source_target_pairs={{0,16},{1,17},{2,18},{3,19},{4,20},{5,21},{6,22},{7,23},{8,24},{9,... | collective-permute-start | bytes 393224 | tf_op jit(solution)/shard_map/ppermute | solution.py:30
  270.7 4.9 copy-start.6
  270.7 5.0 copy-start.2
  270.7 175.0 %all-to-all-start.1 = ((bf16[32,8,3584]{2,1,0:T(8,128)(2,1)}), bf16[32,8,3584]{2,1,0:T(8,128)(2,1)}, u32[]{:S(2)}, u32[]{:S(2)}) async-start(bf16[32,8,3584]{2,1,0:T(8,128)(2,1)} %fusion), calls=%async_computation.1 | async-start | bytes 3670016 | tf_op jit(solution)/shard_map/all_to_all | solution.py:101
  275.6 7.5 %copy-start.5 = (bf16[1,1,8]{2,1,0:T(2,128)(2,1)S(1)}, bf16[1,1,8]{2,1,0:T(2,128)(2,1)}, u32[]{:S(2)}) copy-start(bf16[1,1,8]{2,1,0:T(2,128)(2,1)} %param.12) | copy-start | bytes 52
  275.6 31.6 %copy-start.7 = (s32[1,8]{1,0:T(1,128)S(1)}, s32[1,8]{1,0:T(1,128)}, u32[]{:S(2)}) copy-start(s32[1,8]{1,0:T(1,128)} %param.18) | copy-start | bytes 100
  275.6 336.6 %all-reduce.3.cloned.1.call-start = ((), (), s32[]{:S(2)}) async-start(), calls=%async_computation.2 | async-start | bytes 917504
  276.5 32.3 %collective-permute-start = (bf16[2,64,576]{2,1,0:T(8,128)(2,1)S(1)}, bf16[2,64,576]{2,1,0:T(8,128)(2,1)S(1)}, u32[]{:S(2)}, u32[]{:S(2)}) collective-permute-start(bf16[2,64,576]{2,1,0:T(8,128)(2,1)S(1)} %get-tuple-element.2), channel_id=1, source_target_pairs={{0,1},{1,2},{2,3},{3,4},{4,5},{5,6},{6,7},{7,8},{8,9},{9,10},{10,1... | collective-permute-start | bytes 442376 | tf_op jit(solution)/shard_map/ppermute | solution.py:19
  281.1 28.4 %collective-permute-start.1 = (bf16[2,64,576]{2,1,0:T(8,128)(2,1)S(1)}, bf16[2,64,576]{2,1,0:T(8,128)(2,1)}, u32[]{:S(2)}, u32[]{:S(2)}) collective-permute-start(bf16[2,64,576]{2,1,0:T(8,128)(2,1)S(1)} %get-tuple-element.3), channel_id=1, source_target_pairs={{1,0},{2,1},{3,2},{4,3},{5,4},{6,5},{7,6},{8,7},{9,8},{10,9},{11,1... | collective-permute-start | bytes 442376 | tf_op jit(solution)/shard_map/ppermute | solution.py:22
  308.8 0.7 copy-start.4
  449.0 0.8 copy-start.1
Sparse Core Ops, SparseCore 0:
  450.0 162.2 all-reduce.2
where the time goes:
time: 622 us; the launch traced here: 621 us
  waiting for transfers between devices  298 us (48%)
  blocking collectives  275 us (44%)
  starting transfers between devices  15.4 us (2%)
  between operations  15 us (2%)
  matrix products  8.64 us (1%)
  local copies, waits for them, and re-layouts  7.34 us (1%)
    all_to_all x1, blocking collectives, expert_part(): lax.all_to_all(outgoing_rows, 'grp', split_axis=0, concat_axis=0, tiled=T...  195 us
    unnamed x2, waiting for transfers between devices  161 us
    all_to_all x1, waiting for transfers between devices, expert_part(): lax.all_to_all(partial_out, 'grp', split_axis=0, concat_axis=0, tiled=True)  133 us
    all_gather x1, blocking collectives, expert_part(): lax.all_gather(tokens, 'ep', axis=0, tiled=True)  36.8 us
    all_gather x1, blocking collectives, expert_part(): lax.all_gather(affinity_local, 'ep', axis=0, tiled=True)  23 us
    all_gather x1, blocking collectives, expert_part(): lax.all_gather(chosen_local, 'ep', axis=0, tiled=True)  20.5 us
  transfers between devices with their start and end apart: 5, of which 3 were waited for; matrix products, arithmetic and copies ran while one was open for 1% of the time, Pallas kernels for 0%

commit v1 on v0

v1 whole, which is shorter than its diff:
```python
import jax
import jax.numpy as jnp
from jax import lax
from jax.sharding import Mesh, PartitionSpec as P

KVL = 512
SLICE = 224
WIDE = 256
HALF = ("y", "x", "c")
EP = ("h",) + HALF


softmax_scale = 192.0 ** (-0.5)
routed_scale = 2.5


def exchanged(value, axes):
    return lax.all_to_all(value, axes, split_axis=0, concat_axis=0, tiled=True)


def attention_part(queries, latent_pool, page_moves, page_list, lengths):
    outgoing = page_moves.reshape(-1)
    moving = outgoing.shape[0] // 2
    departing = jnp.take(latent_pool, outgoing, axis=0)
    count = lax.axis_size(EP)
    forward = [(i, (i + 1) % count) for i in range(count)]
    backward = [(target, source) for source, target in forward]
    low = lax.ppermute(departing[moving:], EP, forward)
    high = lax.ppermute(departing[:moving], EP, backward)
    extended = jnp.concatenate([latent_pool, low, high], axis=0)
    latent_rows = jnp.take(extended, page_list.reshape(-1), axis=0)
    latent_rows = latent_rows.reshape(-1, latent_pool.shape[2])
    query_rows = queries.reshape(queries.shape[1], queries.shape[2])
    scores = jnp.dot(query_rows, latent_rows.T, preferred_element_type=jnp.float32) * softmax_scale
    in_range = jnp.arange(latent_rows.shape[0]) < lengths[0]
    scores = jnp.where(in_range[None, :], scores, -1e30)
    attention_weights = jax.nn.softmax(scores, axis=-1).astype(jnp.bfloat16)
    mixed_latent = jnp.dot(
        attention_weights, latent_rows[:, :KVL], preferred_element_type=jnp.float32
    )
    return mixed_latent.astype(jnp.bfloat16).reshape(1, query_rows.shape[0], KVL)


def expert_part(tokens, expert_ids, affinity, gate_up_blocks, down_blocks):
    members = lax.axis_size(EP)
    groups = lax.axis_size("z")
    parts = lax.axis_size(HALF)
    choices = expert_ids.shape[2]
    capacity = members * choices // groups
    gate_up = gate_up_blocks.reshape(parts, SLICE, gate_up_blocks.shape[3])
    units = gate_up.shape[2] // 2
    down = down_blocks.reshape(units, parts, SLICE)
    down = jnp.pad(down.transpose(1, 0, 2), ((0, 0), (0, 0), (0, WIDE - SLICE)))
    routing = jnp.concatenate(
        [expert_ids.reshape(1, choices).astype(jnp.bfloat16), affinity.reshape(1, choices)], axis=1
    )
    routing = jnp.pad(routing, ((0, 0), (0, WIDE - SLICE - 2 * choices)))
    outgoing = jnp.concatenate(
        [tokens.reshape(members, SLICE), jnp.broadcast_to(routing, (members, WIDE - SLICE))], axis=1
    )
    held = exchanged(outgoing, EP)
    chosen = held[:, SLICE : SLICE + choices].astype(jnp.float32)
    affinity_all = held[:, SLICE + choices : SLICE + 2 * choices].astype(jnp.float32)
    route_weights = routed_scale * affinity_all / jnp.sum(affinity_all, axis=1, keepdims=True)
    matches = chosen[:, :, None] == jnp.arange(groups, dtype=jnp.float32)[None, None, :]
    member = jnp.any(matches, axis=1)
    weight_of = jnp.sum(jnp.where(matches, route_weights[:, :, None], 0.0), axis=1)
    earlier = jnp.arange(members)[:, None] > jnp.arange(members)[None, :]
    position = jnp.dot(
        earlier.astype(jnp.bfloat16),
        member.astype(jnp.bfloat16),
        preferred_element_type=jnp.float32,
    )
    slot_number = jnp.arange(capacity, dtype=jnp.float32)
    selector = member.T[:, None, :] & (position.T[:, None, :] == slot_number[None, :, None])
    rows = groups * capacity
    sent_rows = jnp.dot(
        selector.astype(jnp.bfloat16).reshape(rows, members),
        held,
        preferred_element_type=jnp.float32,
    ).astype(jnp.bfloat16)
    arrived = exchanged(sent_rows.reshape(groups, capacity, WIDE), "z").reshape(rows, WIDE)
    gathered = lax.all_gather(arrived, HALF, axis=0, tiled=False)
    partial_sum = jnp.einsum(
        "urk,ukn->rn", gathered[:, :, :SLICE], gate_up, preferred_element_type=jnp.float32
    )
    partner_sum = lax.ppermute(partial_sum.astype(jnp.bfloat16), "h", [(0, 1), (1, 0)])
    combined = partial_sum + partner_sum.astype(jnp.float32)
    activation = (jax.nn.silu(combined[:, :units]) * combined[:, units:]).astype(jnp.bfloat16)
    partial_out = jnp.einsum(
        "ru,cuk->crk", activation, down, preferred_element_type=jnp.float32
    ).astype(jnp.bfloat16)
    summed = jnp.sum(exchanged(partial_out, HALF).astype(jnp.float32), axis=0)
    summed = summed.astype(jnp.bfloat16).reshape(groups, capacity, WIDE)
    returned = exchanged(summed, "z").reshape(rows, WIDE)
    weighted = jnp.where(selector, weight_of.T[:, None, :], 0.0).reshape(rows, members)
    mixed = jnp.einsum(
        "rn,rk->nk", weighted, returned.astype(jnp.float32), precision=lax.Precision.HIGHEST
    )
    own = exchanged(mixed.astype(jnp.bfloat16), EP)
    return own[:, :SLICE].reshape(1, -1)


def shards(
    tokens,
    expert_ids,
    affinity,
    gate_up_blocks,
    down_blocks,
    queries,
    latent_pool,
    page_moves,
    page_list,
    lengths,
):
    attention_latent = attention_part(queries, latent_pool, page_moves, page_list, lengths)
    expert_mix = expert_part(tokens, expert_ids, affinity, gate_up_blocks, down_blocks)
    return (attention_latent, expert_mix)


def solution(mesh):
    fine = Mesh(mesh.devices.reshape(32, 2, 2, 4, 2), ("z",) + EP)
    both = ("z",) + EP
    placed = (
        P(both, None),
        P("z", EP, None),
        P("z", EP, None),
        P("z", EP, None, None),
        P("z", EP, None, None),
        P(both, None, None),
        P(both, None, None),
        P(both, None),
        P(both, None),
        P(both),
    )
    return jax.shard_map(
        shards,
        mesh=fine,
        in_specs=placed,
        out_specs=(P(both, None, None), P(both, None)),
        check_vma=False,
    )
```

time: 622 us -> 244 us (0.39)
  waiting for transfers between devices: 298 us -> 85.3 us
  blocking collectives: 275 us -> 73.3 us
  starting transfers between devices: 15.4 us -> 47.3 us
    unnamed x2 -> x1, waiting for transfers between devices: 161 us -> 0.02 us
    all_to_all x1 -> x2, blocking collectives: 195 us -> 73.3 us  [exchanged(): return lax.all_to_all(value, axes, split_axis=0, concat_axis=0, tiled=True)]
    all_to_all x1 -> x3, waiting for transfers between devices: 133 us -> 51.2 us  [exchanged(): return lax.all_to_all(value, axes, split_axis=0, concat_axis=0, tiled=True)]
    all_gather x3 -> x0, blocking collectives: 80.3 us -> none  [the longest x1 36.8 us: expert_part(): lax.all_gather(tokens, 'ep', axis=0, tiled=True)]
    all_to_all x1 -> x3, starting transfers between devices: 4.86 us -> 37.4 us  [exchanged(): return lax.all_to_all(value, axes, split_axis=0, concat_axis=0, tiled=True)]
    all_gather x0 -> x1, waiting for transfers between devices: none -> 31.8 us  [expert_part(): gathered = lax.all_gather(arrived, HALF, axis=0, tiled=False)]
  transfers between devices with their start and end apart: 5 -> 7, of which waited for: 3 -> 5; matrix products, arithmetic and copies ran while one was open for 1% -> 4% of each run, Pallas kernels for 0% -> 0%
where the time goes in v1:
time: 244 us; the launch traced here: 243 us
  waiting for transfers between devices  85.3 us (35%)
  blocking collectives  73.3 us (30%)
  starting transfers between devices  47.3 us (19%)
  between operations  14.9 us (6%)
  matrix products  8.08 us (3%)
  other arithmetic  7.54 us (3%)
  local copies, waits for them, and re-layouts  6.67 us (3%)
    all_to_all x2, blocking collectives, exchanged(): return lax.all_to_all(value, axes, split_axis=0, concat_axis=0, tiled=True)  73.3 us
    all_to_all x3, waiting for transfers between devices, exchanged(): return lax.all_to_all(value, axes, split_axis=0, concat_axis=0, tiled=True)  51.2 us
    all_to_all x3, starting transfers between devices, exchanged(): return lax.all_to_all(value, axes, split_axis=0, concat_axis=0, tiled=True)  37.4 us
    all_gather x1, waiting for transfers between devices, expert_part(): gathered = lax.all_gather(arrived, HALF, axis=0, tiled=False)  31.8 us
  transfers between devices with their start and end apart: 7, of which 5 were waited for; matrix products, arithmetic and copies ran while one was open for 4% of the time, Pallas kernels for 0%

profile of v1, /device:TPU:1, one launch (start us, length us, event | category | flops | bytes accessed | tf_op | source)
XLA Modules:
  0.0 243.1 jit_solution(17611572434738633104)
XLA Ops:
  7.2 0.0 copy-start
  7.2 0.0 all-gather.2.cloned.1.call-start
  7.2 1.0 reduce.3
  8.2 0.1 reshape.217
  8.3 0.7 convert_bitcast_fusion.1
  8.9 0.7 fusion.38
  9.7 0.1 pad.11.clone
  9.8 0.5 broadcast.173
  10.3 0.6 reduce.4
  10.9 23.8 %all_to_all.39 = bf16[32,2,128]{2,1,0:T(2,128)(2,1)S(1)} all-to-all(bf16[32,2,128]{2,1,0:T(2,128)(2,1)S(1)} %reshape.245), channel_id=1, replica_groups=mesh['z'=32,'h'=2,'y'=2,'x'=4,'c'=2] {'h','y','x','c'}, dimensions={0} | all-to-all | bytes 32768 | tf_op jit(solution)/shard_map/all_to_all | solution.py:18
  34.7 0.1 slice_convert_fusion
  34.8 0.1 fusion.18
  34.9 0.2 fusion.33
  35.1 0.1 copy.30
  35.2 0.2 fusion.7
  35.4 49.5 %all_to_all.40 = bf16[32,8,256]{2,1,0:T(8,128)(2,1)} all-to-all(bf16[32,8,256]{2,1,0:T(8,128)(2,1)S(1)} %fusion.7), channel_id=1, replica_groups=mesh['z'=32,'h'=2,'y'=2,'x'=4,'c'=2] {'z'}, dimensions={0} | all-to-all | bytes 262144 | tf_op jit(solution)/shard_map/all_to_all | solution.py:18
  84.8 0.0 all-gather.2.cloned.1.call-update
  84.9 31.8 %all-gather.2.cloned.1.call-done = bf16[16,256,256]{2,1,0:T(8,128)(2,1)} async-done(((bf16[1,256,256]{2,1,0:T(8,128)(2,1)}), bf16[16,256,256]{2,1,0:T(8,128)(2,1)}) %all-gather.2.cloned.1.call-update) | async-done | bytes 2097168 | tf_op jit(solution)/shard_map/all_gather | solution.py:83
  116.6 0.0 copy-done
  116.6 2.3 fusion.45
  118.9 4.4 %collective-permute-start.2 = (bf16[256,256]{1,0:T(8,128)(2,1)S(1)}, bf16[256,256]{1,0:T(8,128)(2,1)S(1)}, u32[]{:S(2)}, u32[]{:S(2)}) collective-permute-start(bf16[256,256]{1,0:T(8,128)(2,1)S(1)} %get-tuple-element.6), channel_id=1, source_target_pairs={{0,16},{16,0},{1,17},{17,1},{2,18},{18,2},{3,19},{19,3},{4,20},{20... | collective-permute-start | bytes 393224 | tf_op jit(solution)/shard_map/ppermute | solution.py:87
  123.3 1.6 copy.32
  124.9 2.2 collective-permute-done.2
  127.2 2.0 convert_bitcast_fusion
  129.2 0.0 copy-start.3
  129.2 0.0 copy-start.1
  129.2 0.0 copy-start.4
  129.2 6.4 %all-to-all-start.2 = ((bf16[16,256,256]{1,2,0:T(8,128)(2,1)}), bf16[16,256,256]{1,2,0:T(8,128)(2,1)}, u32[]{:S(2)}, u32[]{:S(2)}) async-start(bf16[16,256,256]{1,2,0:T(8,128)(2,1)} %convert_bitcast_fusion), calls=%async_computation.2 | async-start | bytes 4194304 | tf_op jit(solution)/shard_map/all_to_all | solution.py:18
  135.6 0.0 copy-done.3
  135.6 0.0 copy-done.1
  135.6 0.6 gather_fusion
  136.2 0.1 broadcast_select_fusion.1
  136.4 3.5 %collective-permute-start = (bf16[2,64,576]{2,1,0:T(8,128)(2,1)S(1)}, bf16[2,64,576]{2,1,0:T(8,128)(2,1)S(1)}, u32[]{:S(2)}, u32[]{:S(2)}) collective-permute-start(bf16[2,64,576]{2,1,0:T(8,128)(2,1)S(1)} %get-tuple-element.2), channel_id=1, source_target_pairs={{0,1},{1,2},{2,3},{3,4},{4,5},{5,6},{6,7},{7,8},{8,9},{9,10},{10,1... | collective-permute-start | bytes 442376 | tf_op jit(solution)/shard_map/ppermute | solution.py:28
  139.9 1.9 collective-permute-start.1
  142.5 0.0 copy-done.4
  142.5 0.1 broadcast_in_dim.88
  142.6 0.1 broadcast_in_dim.89
  142.7 0.2 convert_reduce_fusion
  142.9 20.4 %all-to-all-done.2 = bf16[16,256,256]{1,2,0:T(8,128)(2,1)} async-done(((bf16[16,256,256]{1,2,0:T(8,128)(2,1)}), bf16[16,256,256]{1,2,0:T(8,128)(2,1)}, u32[]{:S(2)}, u32[]{:S(2)}) %all-to-all-start.2) | async-done | bytes 2097184 | tf_op jit(solution)/shard_map/all_to_all | solution.py:18
  163.3 1.9 reduce_sum.42
  165.2 0.8 copy.34
  165.9 21.7 %all-to-all-start.3 = ((bf16[32,8,256]{2,1,0:T(8,128)(2,1)}), bf16[32,8,256]{2,1,0:T(8,128)(2,1)}, u32[]{:S(2)}, u32[]{:S(2)}) async-start(bf16[32,8,256]{2,1,0:T(8,128)(2,1)} %bitcast.26), calls=%async_computation.3 | async-start | bytes 262144 | tf_op jit(solution)/shard_map/all_to_all | solution.py:18
  187.7 0.1 fusion.32
  187.8 0.1 select_reduce_fusion
  187.9 0.1 copy.31
  188.0 0.0 collective-permute-done
  188.0 0.0 copy-start.2
  188.0 0.7 copy-done.2
  188.7 0.0 collective-permute-done.1
  188.7 1.2 pad_maximum_fusion
  189.8 0.7 gather_fusion.1
  190.5 0.1 broadcast_select_fusion
  190.6 1.3 fusion.44
  191.9 0.1 fusion.13
  192.0 25.0 %all-to-all-done.3 = bf16[32,8,256]{2,1,0:T(8,128)(2,1)} async-done(((bf16[32,8,256]{2,1,0:T(8,128)(2,1)}), bf16[32,8,256]{2,1,0:T(8,128)(2,1)}, u32[]{:S(2)}, u32[]{:S(2)}) %all-to-all-start.3) | async-done | bytes 131104 | tf_op jit(solution)/shard_map/all_to_all | solution.py:18
  217.0 1.2 fusion.9
  218.1 0.6 reduce.5
  218.7 0.6 reshape.247
  219.3 9.3 %all-to-all-start.4 = ((bf16[32,2,128]{2,1,0:T(2,128)(2,1)}), bf16[32,2,128]{2,1,0:T(2,128)(2,1)S(1)}, u32[]{:S(2)}, u32[]{:S(2)}) async-start(bf16[32,2,128]{2,1,0:T(2,128)(2,1)} %reshape.247), calls=%async_computation.4 | async-start | bytes 32768 | tf_op jit(solution)/shard_map/all_to_all | solution.py:18
  228.7 1.0 fusion.6
  229.7 5.9 %all-to-all-done.4 = bf16[32,2,128]{2,1,0:T(2,128)(2,1)S(1)} async-done(((bf16[32,2,128]{2,1,0:T(2,128)(2,1)}), bf16[32,2,128]{2,1,0:T(2,128)(2,1)S(1)}, u32[]{:S(2)}, u32[]{:S(2)}) %all-to-all-start.4) | async-done | bytes 16416 | tf_op jit(solution)/shard_map/all_to_all | solution.py:18
  235.6 0.7 reshape.223
  (15 shorter events, 0.2 us)
Async XLA Ops:
  7.2 109.5 %copy-start = (bf16[1,1,3584,256]{3,2,1,0:T(8,128)(2,1)S(1)}, bf16[1,1,3584,256]{3,2,1,0:T(8,128)(2,1)}, u32[]{:S(2)}) copy-start(bf16[1,1,3584,256]{3,2,1,0:T(8,128)(2,1)} %param.13) | copy-start | bytes 5505028
  7.2 109.5 %all-gather.2.cloned.1.call-start = ((), (), s32[]{:S(2)}) async-start(), calls=%async_computation.5 | async-start | bytes 2228224 | tf_op jit(solution)/shard_map/all_gather | solution.py:83
  118.9 8.2 %collective-permute-start.2 = (bf16[256,256]{1,0:T(8,128)(2,1)S(1)}, bf16[256,256]{1,0:T(8,128)(2,1)S(1)}, u32[]{:S(2)}, u32[]{:S(2)}) collective-permute-start(bf16[256,256]{1,0:T(8,128)(2,1)S(1)} %get-tuple-element.6), channel_id=1, source_target_pairs={{0,16},{16,0},{1,17},{17,1},{2,18},{18,2},{3,19},{19,3},{4,20},{20... | collective-permute-start | bytes 393224 | tf_op jit(solution)/shard_map/ppermute | solution.py:87
  129.2 6.4 %copy-start.3 = (s32[1,4]{1,0:T(1,128)S(1)}, s32[1,4]{1,0:T(1,128)}, u32[]{:S(2)}) copy-start(s32[1,4]{1,0:T(1,128)} %param.17) | copy-start | bytes 52
  129.2 6.4 %copy-start.1 = (bf16[8,64,576]{2,1,0:T(8,128)(2,1)S(1)}, bf16[8,64,576]{2,1,0:T(8,128)(2,1)}, u32[]{:S(2)}) copy-start(bf16[8,64,576]{2,1,0:T(8,128)(2,1)} %param.16) | copy-start | bytes 1769476
  129.2 13.3 %copy-start.4 = (s32[1,8]{1,0:T(1,128)S(1)}, s32[1,8]{1,0:T(1,128)}, u32[]{:S(2)}) copy-start(s32[1,8]{1,0:T(1,128)} %param.18) | copy-start | bytes 100
  129.2 34.1 %all-to-all-start.2 = ((bf16[16,256,256]{1,2,0:T(8,128)(2,1)}), bf16[16,256,256]{1,2,0:T(8,128)(2,1)}, u32[]{:S(2)}, u32[]{:S(2)}) async-start(bf16[16,256,256]{1,2,0:T(8,128)(2,1)} %convert_bitcast_fusion), calls=%async_computation.2 | async-start | bytes 4194304 | tf_op jit(solution)/shard_map/all_to_all | solution.py:18
  136.4 51.6 %collective-permute-start = (bf16[2,64,576]{2,1,0:T(8,128)(2,1)S(1)}, bf16[2,64,576]{2,1,0:T(8,128)(2,1)S(1)}, u32[]{:S(2)}, u32[]{:S(2)}) collective-permute-start(bf16[2,64,576]{2,1,0:T(8,128)(2,1)S(1)} %get-tuple-element.2), channel_id=1, source_target_pairs={{0,1},{1,2},{2,3},{3,4},{4,5},{5,6},{6,7},{7,8},{8,9},{9,10},{10,1... | collective-permute-start | bytes 442376 | tf_op jit(solution)/shard_map/ppermute | solution.py:28
  139.9 48.7 %collective-permute-start.1 = (bf16[2,64,576]{2,1,0:T(8,128)(2,1)S(1)}, bf16[2,64,576]{2,1,0:T(8,128)(2,1)}, u32[]{:S(2)}, u32[]{:S(2)}) collective-permute-start(bf16[2,64,576]{2,1,0:T(8,128)(2,1)S(1)} %get-tuple-element.3), channel_id=1, source_target_pairs={{1,0},{2,1},{3,2},{4,3},{5,4},{6,5},{7,6},{8,7},{9,8},{10,9},{11,1... | collective-permute-start | bytes 442376 | tf_op jit(solution)/shard_map/ppermute | solution.py:29
  165.9 51.0 %all-to-all-start.3 = ((bf16[32,8,256]{2,1,0:T(8,128)(2,1)}), bf16[32,8,256]{2,1,0:T(8,128)(2,1)}, u32[]{:S(2)}, u32[]{:S(2)}) async-start(bf16[32,8,256]{2,1,0:T(8,128)(2,1)} %bitcast.26), calls=%async_computation.3 | async-start | bytes 262144 | tf_op jit(solution)/shard_map/all_to_all | solution.py:18
  188.0 0.7 copy-start.2
  219.3 16.2 %all-to-all-start.4 = ((bf16[32,2,128]{2,1,0:T(2,128)(2,1)}), bf16[32,2,128]{2,1,0:T(2,128)(2,1)S(1)}, u32[]{:S(2)}, u32[]{:S(2)}) async-start(bf16[32,2,128]{2,1,0:T(2,128)(2,1)} %reshape.247), calls=%async_computation.4 | async-start | bytes 32768 | tf_op jit(solution)/shard_map/all_to_all | solution.py:18
Sparse Core Ops, SparseCore 0:
  85.0 31.6 all-gather.1

commit v2 on v1

--- a/solution.py
+++ b/solution.py
@@ -80,9 +80,17 @@
         preferred_element_type=jnp.float32,
     ).astype(jnp.bfloat16)
     arrived = exchanged(sent_rows.reshape(groups, capacity, WIDE), "z").reshape(rows, WIDE)
-    gathered = lax.all_gather(arrived, HALF, axis=0, tiled=False)
+    chips = parts // 2
+    same_core = exchanged(jnp.broadcast_to(arrived[None], (chips, rows, WIDE)), ("y", "x"))
+    other_core = lax.ppermute(same_core, "c", [(0, 1), (1, 0)])
+    by_core = gate_up.reshape(chips, 2, SLICE, 2 * units)
+    core = lax.axis_index("c")
+    same_weights = lax.dynamic_index_in_dim(by_core, core, 1, keepdims=False)
+    other_weights = lax.dynamic_index_in_dim(by_core, 1 - core, 1, keepdims=False)
     partial_sum = jnp.einsum(
-        "urk,ukn->rn", gathered[:, :, :SLICE], gate_up, preferred_element_type=jnp.float32
+        "urk,ukn->rn", same_core[:, :, :SLICE], same_weights, preferred_element_type=jnp.float32
+    ) + jnp.einsum(
+        "urk,ukn->rn", other_core[:, :, :SLICE], other_weights, preferred_element_type=jnp.float32
     )
     partner_sum = lax.ppermute(partial_sum.astype(jnp.bfloat16), "h", [(0, 1), (1, 0)])
     combined = partial_sum + partner_sum.astype(jnp.float32)

time: 244 us -> 203 us (0.83)
  waiting for transfers between devices: 85.3 us -> 56.5 us
  blocking collectives: 73.3 us -> 88.7 us
  starting transfers between devices: 47.3 us -> 32.1 us
  between operations: 14.9 us -> 1.59 us
    all_gather x1 -> x0, waiting for transfers between devices: 31.8 us -> none  [expert_part(): gathered = lax.all_gather(arrived, HALF, axis=0, tiled=False)]
    all_to_all x3, starting transfers between devices: 37.4 us -> 17.9 us  [exchanged(): return lax.all_to_all(value, axes, split_axis=0, concat_axis=0, tiled=True)]
    all_to_all x2 -> x3, blocking collectives: 73.3 us -> 88.7 us  [exchanged(): return lax.all_to_all(value, axes, split_axis=0, concat_axis=0, tiled=True)]
    ppermute x0 -> x1, starting transfers between devices: none -> 5.47 us  [expert_part(): other_core = lax.ppermute(same_core, 'c', [(0, 1), (1, 0)])]
  transfers between devices with their start and end apart: 7 -> 7, of which waited for: 5 -> 5; matrix products, arithmetic and copies ran while one was open for 4% -> 5% of each run, Pallas kernels for 0% -> 0%
where the time goes in v2:
time: 203 us; the launch traced here: 202 us
  blocking collectives  88.7 us (44%)
  waiting for transfers between devices  56.5 us (28%)
  starting transfers between devices  32.1 us (16%)
  local copies, waits for them, and re-layouts  7.98 us (4%)
  matrix products  7.85 us (4%)
  other arithmetic  7.58 us (4%)
    all_to_all x3, blocking collectives, exchanged(): return lax.all_to_all(value, axes, split_axis=0, concat_axis=0, tiled=True)  88.7 us
    all_to_all x3, waiting for transfers between devices, exchanged(): return lax.all_to_all(value, axes, split_axis=0, concat_axis=0, tiled=True)  51.3 us
    all_to_all x3, starting transfers between devices, exchanged(): return lax.all_to_all(value, axes, split_axis=0, concat_axis=0, tiled=True)  17.9 us
    ppermute x1, starting transfers between devices, expert_part(): other_core = lax.ppermute(same_core, 'c', [(0, 1), (1, 0)])  5.47 us
  transfers between devices with their start and end apart: 7, of which 5 were waited for; matrix products, arithmetic and copies ran while one was open for 5% of the time, Pallas kernels for 0%

profile of v2, /device:TPU:1, one launch (start us, length us, event | category | flops | bytes accessed | tf_op | source)
XLA Modules:
  0.0 202.4 jit_solution(174233247830630184)
XLA Ops:
  0.6 0.0 copy-start
  0.6 1.0 reduce.3
  1.6 0.1 reshape.215
  1.7 0.7 convert_bitcast_fusion.1
  2.4 0.7 fusion.42
  3.1 0.1 pad.11.clone
  3.2 0.5 broadcast.173
  3.7 0.6 reduce.4
  4.3 23.8 %all_to_all.44 = bf16[32,2,128]{2,1,0:T(2,128)(2,1)S(1)} all-to-all(bf16[32,2,128]{2,1,0:T(2,128)(2,1)S(1)} %reshape.243), channel_id=1, replica_groups=mesh['z'=32,'h'=2,'y'=2,'x'=4,'c'=2] {'h','y','x','c'}, dimensions={0} | all-to-all | bytes 32768 | tf_op jit(solution)/shard_map/all_to_all | solution.py:18
  28.2 0.1 slice_convert_fusion
  28.2 0.1 fusion.20
  28.4 0.2 fusion.35
  28.5 0.1 copy.36
  28.6 0.2 copy-done.3
  28.8 0.3 copy-done.5
  29.1 0.6 copy-done.7
  29.7 0.2 fusion.3
  29.9 49.4 %all_to_all.45 = bf16[32,8,256]{2,1,0:T(8,128)(2,1)S(1)} all-to-all(bf16[32,8,256]{2,1,0:T(8,128)(2,1)S(1)} %fusion.3), channel_id=1, replica_groups=mesh['z'=32,'h'=2,'y'=2,'x'=4,'c'=2] {'z'}, dimensions={0} | all-to-all | bytes 262144 | tf_op jit(solution)/shard_map/all_to_all | solution.py:18
  79.3 0.1 copy.39
  79.4 0.1 broadcast_in_dim.105
  79.5 15.5 %all_to_all.46 = bf16[8,256,256]{1,2,0:T(8,128)(2,1)S(1)} all-to-all(bf16[8,256,256]{1,2,0:T(8,128)(2,1)S(1)} %broadcast_in_dim.105), channel_id=1, replica_groups=mesh['z'=32,'h'=2,'y'=2,'x'=4,'c'=2] {'y','x'}, dimensions={0} | all-to-all | bytes 2097152 | tf_op jit(solution)/shard_map/all_to_all | solution.py:18
  95.0 5.5 %collective-permute-start.2 = (bf16[8,256,256]{1,2,0:T(8,128)(2,1)S(1)}, bf16[8,256,256]{1,2,0:T(8,128)(2,1)}, u32[]{:S(2)}, u32[]{:S(2)}) collective-permute-start(bf16[8,256,256]{1,2,0:T(8,128)(2,1)S(1)} %all_to_all.46), channel_id=1, source_target_pairs={{0,1},{1,0},{2,3},{3,2},{4,5},{5,4},{6,7},{7,6},{8,9},{9,8},{10,11... | collective-permute-start | bytes 3145736 | tf_op jit(solution)/shard_map/ppermute | solution.py:85
  100.5 0.4 convolution_bitcast_fusion.1
  100.9 1.9 collective-permute-done.2
  102.8 1.6 fusion.49
  104.5 3.2 %collective-permute-start.3 = (bf16[256,256]{1,0:T(8,128)(2,1)S(1)}, bf16[256,256]{1,0:T(8,128)(2,1)S(1)}, u32[]{:S(2)}, u32[]{:S(2)}) collective-permute-start(bf16[256,256]{1,0:T(8,128)(2,1)S(1)} %get-tuple-element.6), channel_id=1, source_target_pairs={{0,16},{16,0},{1,17},{17,1},{2,18},{18,2},{3,19},{19,3},{4,20},{20... | collective-permute-start | bytes 393224 | tf_op jit(solution)/shard_map/ppermute | solution.py:95
  107.7 1.6 copy.38
  109.3 3.3 %collective-permute-done.3 = bf16[256,256]{1,0:T(8,128)(2,1)S(1)} collective-permute-done((bf16[256,256]{1,0:T(8,128)(2,1)S(1)}, bf16[256,256]{1,0:T(8,128)(2,1)S(1)}, u32[]{:S(2)}, u32[]{:S(2)}) %collective-permute-start.3) | collective-permute-done | bytes 131104 | tf_op jit(solution)/shard_map/ppermute | solution.py:95
  112.6 2.0 convert_bitcast_fusion
  114.6 5.5 %all-to-all-start.3 = ((bf16[16,256,256]{1,2,0:T(8,128)(2,1)}), bf16[16,256,256]{1,2,0:T(8,128)(2,1)}, u32[]{:S(2)}, u32[]{:S(2)}) async-start(bf16[16,256,256]{1,2,0:T(8,128)(2,1)} %convert_bitcast_fusion), calls=%async_computation.3 | async-start | bytes 4194304 | tf_op jit(solution)/shard_map/all_to_all | solution.py:18
  120.1 0.0 copy-done.9
  120.1 0.0 copy-start.10
  120.2 0.6 gather_fusion
  120.8 0.1 broadcast_select_fusion.1
  120.9 0.0 copy-start.4
  121.0 3.5 %collective-permute-start = (bf16[2,64,576]{2,1,0:T(8,128)(2,1)S(1)}, bf16[2,64,576]{2,1,0:T(8,128)(2,1)S(1)}, u32[]{:S(2)}, u32[]{:S(2)}) collective-permute-start(bf16[2,64,576]{2,1,0:T(8,128)(2,1)S(1)} %get-tuple-element.2), channel_id=1, source_target_pairs={{0,1},{1,2},{2,3},{3,4},{4,5},{5,6},{6,7},{7,8},{8,9},{9,10},{10,1... | collective-permute-start | bytes 442376 | tf_op jit(solution)/shard_map/ppermute | solution.py:28
  124.5 1.9 collective-permute-start.1
  127.1 0.0 copy-done.10
  127.1 0.1 broadcast_in_dim.95
  127.2 0.1 broadcast_in_dim.96
  127.3 0.2 convert_reduce_fusion
  127.5 20.2 %all-to-all-done.3 = bf16[16,256,256]{1,2,0:T(8,128)(2,1)} async-done(((bf16[16,256,256]{1,2,0:T(8,128)(2,1)}), bf16[16,256,256]{1,2,0:T(8,128)(2,1)}, u32[]{:S(2)}, u32[]{:S(2)}) %all-to-all-start.3) | async-done | bytes 2097184 | tf_op jit(solution)/shard_map/all_to_all | solution.py:18
  147.7 1.9 reduce_sum.42
  149.6 0.8 copy.42
  150.4 4.6 %all-to-all-start.4 = ((bf16[32,8,256]{2,1,0:T(8,128)(2,1)}), bf16[32,8,256]{2,1,0:T(8,128)(2,1)}, u32[]{:S(2)}, u32[]{:S(2)}) async-start(bf16[32,8,256]{2,1,0:T(8,128)(2,1)} %bitcast.29), calls=%async_computation.4 | async-start | bytes 262144 | tf_op jit(solution)/shard_map/all_to_all | solution.py:18
  154.9 0.1 fusion.34
  155.0 0.1 select_reduce_fusion
  155.2 0.1 copy.37
  155.3 0.0 collective-permute-done
  155.3 0.7 copy-done.2
  155.9 0.0 collective-permute-done.1
  155.9 1.2 pad_maximum_fusion
  157.1 0.7 gather_fusion.1
  157.8 0.1 broadcast_select_fusion
  157.9 1.3 fusion.48
  159.2 0.1 fusion.15
  159.3 25.2 %all-to-all-done.4 = bf16[32,8,256]{2,1,0:T(8,128)(2,1)} async-done(((bf16[32,8,256]{2,1,0:T(8,128)(2,1)}), bf16[32,8,256]{2,1,0:T(8,128)(2,1)}, u32[]{:S(2)}, u32[]{:S(2)}) %all-to-all-start.4) | async-done | bytes 131104 | tf_op jit(solution)/shard_map/all_to_all | solution.py:18
  184.5 1.2 fusion.5
  185.7 0.6 reduce.5
  186.3 0.6 reshape.245
  186.9 7.9 %all-to-all-start.5 = ((bf16[32,2,128]{2,1,0:T(2,128)(2,1)}), bf16[32,2,128]{2,1,0:T(2,128)(2,1)S(1)}, u32[]{:S(2)}, u32[]{:S(2)}) async-start(bf16[32,2,128]{2,1,0:T(2,128)(2,1)} %reshape.245), calls=%async_computation.5 | async-start | bytes 32768 | tf_op jit(solution)/shard_map/all_to_all | solution.py:18
  194.8 1.0 fusion.2
  195.8 5.9 %all-to-all-done.5 = bf16[32,2,128]{2,1,0:T(2,128)(2,1)S(1)} async-done(((bf16[32,2,128]{2,1,0:T(2,128)(2,1)}), bf16[32,2,128]{2,1,0:T(2,128)(2,1)S(1)}, u32[]{:S(2)}, u32[]{:S(2)}) %all-to-all-start.5) | async-done | bytes 16416 | tf_op jit(solution)/shard_map/all_to_all | solution.py:18
  201.6 0.7 reshape.220
  (28 shorter events, 0.2 us)
Async XLA Ops:
  0.6 99.8 %copy-start = (bf16[1,1,3584,256]{3,2,1,0:T(8,128)(2,1)S(1)}, bf16[1,1,3584,256]{3,2,1,0:T(8,128)(2,1)}, u32[]{:S(2)}) copy-start(bf16[1,1,3584,256]{3,2,1,0:T(8,128)(2,1)} %param.13) | copy-start | bytes 5505028
  28.2 0.6 copy-start.3
  28.5 0.6 copy-start.5
  29.1 0.6 copy-start.7
  95.0 7.9 %collective-permute-start.2 = (bf16[8,256,256]{1,2,0:T(8,128)(2,1)S(1)}, bf16[8,256,256]{1,2,0:T(8,128)(2,1)}, u32[]{:S(2)}, u32[]{:S(2)}) collective-permute-start(bf16[8,256,256]{1,2,0:T(8,128)(2,1)S(1)} %all_to_all.46), channel_id=1, source_target_pairs={{0,1},{1,0},{2,3},{3,2},{4,5},{5,4},{6,7},{7,6},{8,9},{9,8},{10,11... | collective-permute-start | bytes 3145736 | tf_op jit(solution)/shard_map/ppermute | solution.py:85
  104.5 8.1 %collective-permute-start.3 = (bf16[256,256]{1,0:T(8,128)(2,1)S(1)}, bf16[256,256]{1,0:T(8,128)(2,1)S(1)}, u32[]{:S(2)}, u32[]{:S(2)}) collective-permute-start(bf16[256,256]{1,0:T(8,128)(2,1)S(1)} %get-tuple-element.6), channel_id=1, source_target_pairs={{0,16},{16,0},{1,17},{17,1},{2,18},{18,2},{3,19},{19,3},{4,20},{20... | collective-permute-start | bytes 393224 | tf_op jit(solution)/shard_map/ppermute | solution.py:95
  114.6 5.5 %copy-start.9 = (s32[1,4]{1,0:T(1,128)S(1)}, s32[1,4]{1,0:T(1,128)}, u32[]{:S(2)}) copy-start(s32[1,4]{1,0:T(1,128)} %param.17) | copy-start | bytes 52
  114.6 5.5 %copy-start.1 = (bf16[8,64,576]{2,1,0:T(8,128)(2,1)S(1)}, bf16[8,64,576]{2,1,0:T(8,128)(2,1)}, u32[]{:S(2)}) copy-start(bf16[8,64,576]{2,1,0:T(8,128)(2,1)} %param.16) | copy-start | bytes 1769476
  114.6 33.1 %all-to-all-start.3 = ((bf16[16,256,256]{1,2,0:T(8,128)(2,1)}), bf16[16,256,256]{1,2,0:T(8,128)(2,1)}, u32[]{:S(2)}, u32[]{:S(2)}) async-start(bf16[16,256,256]{1,2,0:T(8,128)(2,1)} %convert_bitcast_fusion), calls=%async_computation.3 | async-start | bytes 4194304 | tf_op jit(solution)/shard_map/all_to_all | solution.py:18
  120.1 7.0 %copy-start.10 = (s32[1,8]{1,0:T(1,128)S(1)}, s32[1,8]{1,0:T(1,128)}, u32[]{:S(2)}) copy-start(s32[1,8]{1,0:T(1,128)} %param.18) | copy-start | bytes 100
  120.9 34.1 %copy-start.4 = (f32[32,8]{1,0:T(8,128)S(1)}, f32[32,8]{1,0:T(8,128)}, u32[]{:S(2)}) copy-start(f32[32,8]{1,0:T(8,128)} %copy-done.3) | copy-start | bytes 3076
  121.0 34.3 %collective-permute-start = (bf16[2,64,576]{2,1,0:T(8,128)(2,1)S(1)}, bf16[2,64,576]{2,1,0:T(8,128)(2,1)S(1)}, u32[]{:S(2)}, u32[]{:S(2)}) collective-permute-start(bf16[2,64,576]{2,1,0:T(8,128)(2,1)S(1)} %get-tuple-element.2), channel_id=1, source_target_pairs={{0,1},{1,2},{2,3},{3,4},{4,5},{5,6},{6,7},{7,8},{8,9},{9,10},{10,1... | collective-permute-start | bytes 442376 | tf_op jit(solution)/shard_map/ppermute | solution.py:28
  124.5 31.4 %collective-permute-start.1 = (bf16[2,64,576]{2,1,0:T(8,128)(2,1)S(1)}, bf16[2,64,576]{2,1,0:T(8,128)(2,1)}, u32[]{:S(2)}, u32[]{:S(2)}) collective-permute-start(bf16[2,64,576]{2,1,0:T(8,128)(2,1)S(1)} %get-tuple-element.3), channel_id=1, source_target_pairs={{1,0},{2,1},{3,2},{4,3},{5,4},{6,5},{7,6},{8,7},{9,8},{10,9},{11,1... | collective-permute-start | bytes 442376 | tf_op jit(solution)/shard_map/ppermute | solution.py:29
  150.4 34.1 %all-to-all-start.4 = ((bf16[32,8,256]{2,1,0:T(8,128)(2,1)}), bf16[32,8,256]{2,1,0:T(8,128)(2,1)}, u32[]{:S(2)}, u32[]{:S(2)}) async-start(bf16[32,8,256]{2,1,0:T(8,128)(2,1)} %bitcast.29), calls=%async_computation.4 | async-start | bytes 262144 | tf_op jit(solution)/shard_map/all_to_all | solution.py:18
  155.3 0.7 copy-start.2
  157.1 27.4 %copy-start.6 = (f32[32,32]{1,0:T(8,128)S(1)}, f32[32,32]{1,0:T(8,128)}, u32[]{:S(2)}) copy-start(f32[32,32]{1,0:T(8,128)} %copy-done.5) | copy-start | bytes 12292
  157.1 27.4 %copy-start.8 = (pred[32,32]{1,0:T(8,128)(4,1)S(1)}, pred[32,32]{1,0:T(8,128)(4,1)}, u32[]{:S(2)}) copy-start(pred[32,32]{1,0:T(8,128)(4,1)} %copy-done.7) | copy-start | bytes 3076
  186.9 14.7 %all-to-all-start.5 = ((bf16[32,2,128]{2,1,0:T(2,128)(2,1)}), bf16[32,2,128]{2,1,0:T(2,128)(2,1)S(1)}, u32[]{:S(2)}, u32[]{:S(2)}) async-start(bf16[32,2,128]{2,1,0:T(2,128)(2,1)} %reshape.245), calls=%async_computation.5 | async-start | bytes 32768 | tf_op jit(solution)/shard_map/all_to_all | solution.py:18

commit v3 on v1

--- a/solution.py
+++ b/solution.py
@@ -1,12 +1,15 @@
 import jax
 import jax.numpy as jnp
 from jax import lax
+from jax.experimental import pallas as pl
+from jax.experimental.pallas import tpu as pltpu
 from jax.sharding import Mesh, PartitionSpec as P
 
 KVL = 512
 SLICE = 224
 WIDE = 256
 HALF = ("y", "x", "c")
+CHIPS = ("h", "y", "x")
 EP = ("h",) + HALF
 
 
@@ -16,6 +19,96 @@
 
 def exchanged(value, axes):
     return lax.all_to_all(value, axes, split_axis=0, concat_axis=0, tiled=True)
+
+
+def gate_up_kernel(core, own, other, weights, out):
+    mine = core[0]
+    chips, units = weights.shape[0], weights.shape[3] // 2
+    part = units // 2
+    for i in range(chips):
+        sums = jnp.dot(own[...], weights[i, mine], preferred_element_type=jnp.float32)
+        sums += jnp.dot(other[...], weights[i, 1 - mine], preferred_element_type=jnp.float32)
+        for h in range(2):
+            pair = [sums[:, n * part : (n + 1) * part] for n in (h, 2 + h)]
+            out[h * chips + i] = jnp.concatenate(pair, axis=1).astype(out.dtype)
+
+
+def gate_up_sums(core, own, other, weights):
+    chips, _, width, columns = weights.shape
+    rows = own.shape[0]
+    out_shape = (2 * chips, rows, columns // 2)
+    return pl.pallas_call(
+        gate_up_kernel,
+        out_shape=jax.ShapeDtypeStruct(out_shape, jnp.bfloat16),
+        in_specs=[pl.BlockSpec(memory_space=pltpu.SMEM)]
+        + [pl.BlockSpec(memory_space=pltpu.VMEM)] * 3,
+        out_specs=pl.BlockSpec(memory_space=pltpu.VMEM),
+        compiler_params=pltpu.CompilerParams(vmem_limit_bytes=32 << 20),
+        cost_estimate=pl.CostEstimate(
+            flops=4 * chips * rows * width * columns,
+            bytes_accessed=2 * weights.size + 4 * out_shape[0] * rows * columns // 2,
+            transcendentals=0,
+        ),
+    )(core, own, other, weights)
+
+
+def activation_kernel(parts, out):
+    units = parts.shape[2] // 2
+    sums = parts[0].astype(jnp.float32)
+    for n in range(1, parts.shape[0]):
+        sums += parts[n].astype(jnp.float32)
+    gate, up = sums[:, :units], sums[:, units:]
+    value = (jax.nn.silu(gate) * up).T.astype(out.dtype)
+    for n in range(out.shape[0]):
+        out[n] = value
+
+
+def activated(parts):
+    count, rows, columns = parts.shape
+    out_shape = (count, columns // 2, rows)
+    return pl.pallas_call(
+        activation_kernel,
+        out_shape=jax.ShapeDtypeStruct(out_shape, jnp.bfloat16),
+        in_specs=[pl.BlockSpec(memory_space=pltpu.VMEM)],
+        out_specs=pl.BlockSpec(memory_space=pltpu.VMEM),
+        compiler_params=pltpu.CompilerParams(vmem_limit_bytes=32 << 20),
+        cost_estimate=pl.CostEstimate(
+            flops=2 * parts.size, bytes_accessed=3 * parts.size, transcendentals=0
+        ),
+    )(parts)
+
+
+def down_kernel(core, values, weights, kept, given):
+    mine = core[0]
+    chips, _, units, width = weights.shape
+    pieces = [values[h * chips + i] for i in range(chips) for h in range(2)]
+    held = jnp.concatenate(pieces, axis=0)
+    for n, out in ((mine, kept), (1 - mine, given)):
+        matrix = jnp.concatenate([weights[i, n] for i in range(chips)], axis=0)
+        out[...] = lax.dot_general(
+            held, matrix, (((0,), (0,)), ((), ())), preferred_element_type=jnp.float32
+        ).astype(out.dtype)
+
+
+def down_sums(core, values, weights):
+    chips, _, units, width = weights.shape
+    rows = values.shape[2]
+    return pl.pallas_call(
+        down_kernel,
+        out_shape=(
+            jax.ShapeDtypeStruct((rows, width), jnp.float32),
+            jax.ShapeDtypeStruct((rows, width), jnp.bfloat16),
+        ),
+        in_specs=[pl.BlockSpec(memory_space=pltpu.SMEM)]
+        + [pl.BlockSpec(memory_space=pltpu.VMEM)] * 2,
+        out_specs=(pl.BlockSpec(memory_space=pltpu.VMEM),) * 2,
+        compiler_params=pltpu.CompilerParams(vmem_limit_bytes=32 << 20),
+        cost_estimate=pl.CostEstimate(
+            flops=4 * chips * rows * width * units,
+            bytes_accessed=2 * weights.size + 2 * values.size + 6 * rows * width,
+            transcendentals=0,
+        ),
+    )(core, values, weights)
 
 
 def attention_part(queries, latent_pool, page_moves, page_list, lengths):
@@ -47,10 +140,8 @@
     parts = lax.axis_size(HALF)
     choices = expert_ids.shape[2]
     capacity = members * choices // groups
-    gate_up = gate_up_blocks.reshape(parts, SLICE, gate_up_blocks.shape[3])
-    units = gate_up.shape[2] // 2
-    down = down_blocks.reshape(units, parts, SLICE)
-    down = jnp.pad(down.transpose(1, 0, 2), ((0, 0), (0, 0), (0, WIDE - SLICE)))
+    chips = parts // 2
+    units = gate_up_blocks.shape[3] // 2
     routing = jnp.concatenate(
         [expert_ids.reshape(1, choices).astype(jnp.bfloat16), affinity.reshape(1, choices)], axis=1
     )
@@ -76,29 +167,28 @@
     rows = groups * capacity
     sent_rows = jnp.dot(
         selector.astype(jnp.bfloat16).reshape(rows, members),
-        held,
+        held[:, :SLICE],
         preferred_element_type=jnp.float32,
     ).astype(jnp.bfloat16)
-    arrived = exchanged(sent_rows.reshape(groups, capacity, WIDE), "z").reshape(rows, WIDE)
-    gathered = lax.all_gather(arrived, HALF, axis=0, tiled=False)
-    partial_sum = jnp.einsum(
-        "urk,ukn->rn", gathered[:, :, :SLICE], gate_up, preferred_element_type=jnp.float32
-    )
-    partner_sum = lax.ppermute(partial_sum.astype(jnp.bfloat16), "h", [(0, 1), (1, 0)])
-    combined = partial_sum + partner_sum.astype(jnp.float32)
-    activation = (jax.nn.silu(combined[:, :units]) * combined[:, units:]).astype(jnp.bfloat16)
-    partial_out = jnp.einsum(
-        "ru,cuk->crk", activation, down, preferred_element_type=jnp.float32
-    ).astype(jnp.bfloat16)
-    summed = jnp.sum(exchanged(partial_out, HALF).astype(jnp.float32), axis=0)
-    summed = summed.astype(jnp.bfloat16).reshape(groups, capacity, WIDE)
-    returned = exchanged(summed, "z").reshape(rows, WIDE)
+    arrived = exchanged(sent_rows.reshape(groups, capacity, SLICE), "z").reshape(rows, SLICE)
+    gate_up = gate_up_blocks.reshape(chips, 2 * SLICE, 2 * units)
+    gate_up = exchanged(gate_up, ("y", "x")).reshape(chips, 2, SLICE, 2 * units)
+    down = down_blocks.reshape(units, chips, 2, SLICE).transpose(1, 2, 0, 3)
+    down = exchanged(down, ("y", "x"))
+    core = lax.axis_index("c").reshape(1).astype(jnp.int32)
+    other = lax.ppermute(arrived, "c", [(0, 1), (1, 0)])
+    partial_sum = gate_up_sums(core, arrived, other, gate_up)
+    activation = activated(exchanged(partial_sum, CHIPS))
+    activation = exchanged(activation, CHIPS)
+    kept, given = down_sums(core, activation, down)
+    summed = kept + lax.ppermute(given, "c", [(0, 1), (1, 0)]).astype(jnp.float32)
+    summed = summed.astype(jnp.bfloat16).reshape(groups, capacity, SLICE)
+    returned = exchanged(summed, "z").reshape(rows, SLICE)
     weighted = jnp.where(selector, weight_of.T[:, None, :], 0.0).reshape(rows, members)
     mixed = jnp.einsum(
         "rn,rk->nk", weighted, returned.astype(jnp.float32), precision=lax.Precision.HIGHEST
     )
-    own = exchanged(mixed.astype(jnp.bfloat16), EP)
-    return own[:, :SLICE].reshape(1, -1)
+    return exchanged(mixed.astype(jnp.bfloat16), EP).reshape(1, -1)
 
 
 def shards(

time: 244 us -> 216 us (0.89)
  blocking collectives: 73.3 us -> 48.7 us
  between operations: 14.9 us -> 1.58 us
  starting transfers between devices: 47.3 us -> 58.8 us
  matrix products: 8.08 us -> 2.08 us
  Pallas kernels: 0 us -> 3.3 us
  waiting for transfers between devices: 85.3 us -> 88.1 us
    all_to_all x3 -> x7, waiting for transfers between devices: 51.2 us -> 86.4 us  [exchanged(): return lax.all_to_all(value, axes, split_axis=0, concat_axis=0, tiled=True)]
    all_gather x1 -> x0, waiting for transfers between devices: 31.8 us -> none  [expert_part(): gathered = lax.all_gather(arrived, HALF, axis=0, tiled=False)]
    all_to_all x2 -> x1, blocking collectives: 73.3 us -> 48.7 us  [exchanged(): return lax.all_to_all(value, axes, split_axis=0, concat_axis=0, tiled=True)]
    ppermute x1 -> x2, starting transfers between devices: 4.4 us -> 9.19 us  [the longest x1 4.7 us: expert_part(): other = lax.ppermute(arrived, 'c', [(0, 1), (1, 0)])]
    all_to_all x3 -> x7, starting transfers between devices: 37.4 us -> 41.8 us  [exchanged(): return lax.all_to_all(value, axes, split_axis=0, concat_axis=0, tiled=True)]
    dot_general x3 -> x1, matrix products: 4.47 us -> 0.29 us  [expert_part(): jnp.dot(selector.astype(jnp.bfloat16).reshape(rows, members), held[:, :SL...]
    pallas_call x0 -> x3, Pallas kernels: none -> 3.3 us  [the longest x1 1.76 us: gate_up_sums(): pl.pallas_call(gate_up_kernel, out_shape=jax.ShapeDtypeStruct(out_shape,...]
  transfers between devices with their start and end apart: 7 -> 11, of which waited for: 5 -> 9; matrix products, arithmetic and copies ran while one was open for 4% -> 4% of each run, Pallas kernels for 0% -> 1%
where the time goes in v3:
time: 216 us; the launch traced here: 215 us
  waiting for transfers between devices  88.1 us (41%)
  starting transfers between devices  58.8 us (27%)
  blocking collectives  48.7 us (23%)
  local copies, waits for them, and re-layouts  6.99 us (3%)
  other arithmetic  5.88 us (3%)
  Pallas kernels  3.3 us (2%)
    all_to_all x7, waiting for transfers between devices, exchanged(): return lax.all_to_all(value, axes, split_axis=0, concat_axis=0, tiled=True)  86.4 us
    all_to_all x1, blocking collectives, exchanged(): return lax.all_to_all(value, axes, split_axis=0, concat_axis=0, tiled=True)  48.7 us
    all_to_all x7, starting transfers between devices, exchanged(): return lax.all_to_all(value, axes, split_axis=0, concat_axis=0, tiled=True)  41.8 us
    ppermute x1, starting transfers between devices, attention_part(): low = lax.ppermute(departing[moving:], EP, forward)  5.92 us
    ppermute x1, starting transfers between devices, expert_part(): other = lax.ppermute(arrived, 'c', [(0, 1), (1, 0)])  4.7 us
    ppermute x1, starting transfers between devices, expert_part(): lax.ppermute(given, 'c', [(0, 1), (1, 0)]).astype(jnp.float32)  4.49 us
  transfers between devices with their start and end apart: 11, of which 9 were waited for; matrix products, arithmetic and copies ran while one was open for 4% of the time, Pallas kernels for 1%

profile of v3, /device:TPU:1, one launch (start us, length us, event | category | flops | bytes accessed | tf_op | source)
XLA Modules:
  0.0 215.4 jit_solution(8771747475502889888)
XLA Ops:
  0.6 0.0 copy-start
  0.6 0.9 reduce.2
  1.5 0.1 reshape.194
  1.6 0.7 convert_bitcast_fusion
  2.3 0.7 fusion.29
  3.0 0.1 pad.6.clone
  3.1 0.5 broadcast.143
  3.6 0.7 reduce.4
  4.3 0.6 reshape.224
  4.9 17.6 %all-to-all-start = ((bf16[32,2,128]{2,1,0:T(2,128)(2,1)}), bf16[32,2,128]{2,1,0:T(2,128)(2,1)S(1)}, u32[]{:S(2)}, u32[]{:S(2)}) async-start(bf16[32,2,128]{2,1,0:T(2,128)(2,1)} %reshape.224), calls=%async_computation | async-start | bytes 32768 | tf_op jit(solution)/shard_map/all_to_all | solution.py:21
  22.5 0.1 eq.45
  22.6 6.9 %all-to-all-done = bf16[32,2,128]{2,1,0:T(2,128)(2,1)S(1)} async-done(((bf16[32,2,128]{2,1,0:T(2,128)(2,1)}), bf16[32,2,128]{2,1,0:T(2,128)(2,1)S(1)}, u32[]{:S(2)}, u32[]{:S(2)}) %all-to-all-start) | async-done | bytes 16416 | tf_op jit(solution)/shard_map/all_to_all | solution.py:21
  29.5 0.1 slice_convert_fusion
  29.6 0.1 fusion.12
  29.7 0.2 fusion.24
  29.9 0.1 copy.31
  30.0 0.3 convolution_convert_fusion.1
  30.3 0.1 copy.33
  30.4 48.7 %all_to_all.51 = bf16[32,8,224]{2,1,0:T(8,128)(2,1)S(1)} all-to-all(bf16[32,8,224]{2,1,0:T(8,128)(2,1)S(1)} %bitcast.70), channel_id=1, replica_groups=mesh['z'=32,'h'=2,'y'=2,'x'=4,'c'=2] {'z'}, dimensions={0} | all-to-all | bytes 229376 | tf_op jit(solution)/shard_map/all_to_all | solution.py:21
  79.1 3.6 %all-to-all-start.2 = ((bf16[8,448,256]{2,1,0:T(8,128)(2,1)}), bf16[8,448,256]{2,1,0:T(8,128)(2,1)S(1)}, u32[]{:S(2)}, u32[]{:S(2)}) async-start(bf16[8,448,256]{2,1,0:T(8,128)(2,1)} %bitcast.69), calls=%async_computation.2 | async-start | bytes 3670016 | tf_op jit(solution)/shard_map/all_to_all | solution.py:21
  82.7 4.7 %collective-permute-start.2 = (bf16[256,224]{1,0:T(8,128)(2,1)S(1)}, bf16[256,224]{1,0:T(8,128)(2,1)S(1)}, u32[]{:S(2)}, u32[]{:S(2)}) collective-permute-start(bf16[256,224]{1,0:T(8,128)(2,1)S(1)} %bitcast.65), channel_id=1, source_target_pairs={{0,1},{1,0},{2,3},{3,2},{4,5},{5,4},{6,7},{7,6},{8,9},{9,8},{10,11... | collective-permute-start | bytes 344072 | tf_op jit(solution)/shard_map/ppermute | solution.py:179
  87.4 1.0 collective-permute-done.2.other
  88.4 18.5 %all-to-all-done.2 = bf16[8,448,256]{2,1,0:T(8,128)(2,1)S(1)} async-done(((bf16[8,448,256]{2,1,0:T(8,128)(2,1)}), bf16[8,448,256]{2,1,0:T(8,128)(2,1)S(1)}, u32[]{:S(2)}, u32[]{:S(2)}) %all-to-all-start.2) | async-done | bytes 1835040 | tf_op jit(solution)/shard_map/all_to_all | solution.py:21
  106.9 1.8 shard_map.113
  108.6 3.8 %all-to-all-start.3 = ((bf16[16,256,128]{2,1,0:T(8,128)(2,1)}), bf16[16,256,128]{2,1,0:T(8,128)(2,1)S(1)}, u32[]{:S(2)}, u32[]{:S(2)}) async-start(bf16[16,256,128]{2,1,0:T(8,128)(2,1)} %shard_map.113), calls=%async_computation.3 | async-start | bytes 2097152 | tf_op jit(solution)/shard_map/all_to_all | solution.py:21
  112.4 1.3 copy.34
  113.8 0.0 copy-start.4
  113.8 0.6 gather_fusion
  114.4 14.1 %all-to-all-done.3.parts = bf16[16,256,128]{2,1,0:T(8,128)(2,1)S(1)} async-done(((bf16[16,256,128]{2,1,0:T(8,128)(2,1)}), bf16[16,256,128]{2,1,0:T(8,128)(2,1)S(1)}, u32[]{:S(2)}, u32[]{:S(2)}) %all-to-all-start.3) | async-done | bytes 1048608 | tf_op jit(solution)/shard_map/all_to_all | solution.py:21
  128.5 3.6 %all-to-all-start.5 = ((bf16[8,2,128,224]{2,3,1,0:T(8,128)(2,1)}), bf16[8,2,128,224]{2,3,1,0:T(8,128)(2,1)S(1)}, u32[]{:S(2)}, u32[]{:S(2)}) async-start(bf16[8,2,128,224]{2,3,1,0:T(8,128)(2,1)} %bitcast.25), calls=%async_computation.5 | async-start | bytes 1835008 | tf_op jit(solution)/shard_map/all_to_all | solution.py:21
  132.1 0.1 broadcast_select_fusion.1
  132.2 0.7 fusion.31
  132.9 5.9 %collective-permute-start = (bf16[2,64,576]{2,1,0:T(8,128)(2,1)}, bf16[2,64,576]{2,1,0:T(8,128)(2,1)}, u32[]{:S(2)}, u32[]{:S(2)}) collective-permute-start(bf16[2,64,576]{2,1,0:T(8,128)(2,1)} %get-tuple-element.6), channel_id=1, source_target_pairs={{0,1},{1,2},{2,3},{3,4},{4,5},{5,6},{6,7},{7,8},{8,9},{9,10},{10,1... | collective-permute-start | bytes 442376 | tf_op jit(solution)/shard_map/ppermute | solution.py:121
  138.8 1.9 collective-permute-start.1
  141.4 1.1 shard_map.114
  142.5 3.9 %all-to-all-done.5 = bf16[8,2,128,224]{2,3,1,0:T(8,128)(2,1)S(1)} async-done(((bf16[8,2,128,224]{2,3,1,0:T(8,128)(2,1)}), bf16[8,2,128,224]{2,3,1,0:T(8,128)(2,1)S(1)}, u32[]{:S(2)}, u32[]{:S(2)}) %all-to-all-start.5) | async-done | bytes 917536 | tf_op jit(solution)/shard_map/all_to_all | solution.py:21
  146.4 3.6 %all-to-all-start.4 = ((bf16[16,64,256]{2,1,0:T(8,128)(2,1)}), bf16[16,64,256]{2,1,0:T(8,128)(2,1)S(1)}, u32[]{:S(2)}, u32[]{:S(2)}) async-start(bf16[16,64,256]{2,1,0:T(8,128)(2,1)} %shard_map.114), calls=%async_computation.4 | async-start | bytes 1048576 | tf_op jit(solution)/shard_map/all_to_all | solution.py:21
  150.0 0.1 broadcast_in_dim.88
  150.1 0.1 broadcast_in_dim.89
  150.2 0.2 convert_reduce_fusion
  150.3 0.1 fusion.22
  150.4 0.5 copy.35.weights
  150.9 8.9 %all-to-all-done.4.values = bf16[16,64,256]{2,1,0:T(8,128)(2,1)S(1)} async-done(((bf16[16,64,256]{2,1,0:T(8,128)(2,1)}), bf16[16,64,256]{2,1,0:T(8,128)(2,1)S(1)}, u32[]{:S(2)}, u32[]{:S(2)}) %all-to-all-start.4) | async-done | bytes 524320 | tf_op jit(solution)/shard_map/all_to_all | solution.py:21
  159.9 0.5 shard_map.115
  160.3 4.5 %collective-permute-start.3 = (bf16[256,224]{1,0:T(8,128)(2,1)S(1)}, bf16[256,224]{1,0:T(8,128)(2,1)S(1)}, u32[]{:S(2)}, u32[]{:S(2)}) collective-permute-start(bf16[256,224]{1,0:T(8,128)(2,1)S(1)} %get-tuple-element.5), channel_id=1, source_target_pairs={{0,1},{1,0},{2,3},{3,2},{4,5},{5,4},{6,7},{7,6},{8,9},{9,8},{10,11... | collective-permute-start | bytes 344072 | tf_op jit(solution)/shard_map/ppermute | solution.py:184
  164.8 0.1 select_reduce_fusion
  165.0 0.1 copy.32
  165.1 0.7 collective-permute-done.3
  165.8 0.7 fusion.8
  166.5 3.9 %all-to-all-start.6 = ((bf16[32,8,224]{2,1,0:T(8,128)(2,1)}), bf16[32,8,224]{2,1,0:T(8,128)(2,1)S(1)}, u32[]{:S(2)}, u32[]{:S(2)}) async-start(bf16[32,8,224]{2,1,0:T(8,128)(2,1)} %fusion.8), calls=%async_computation.6 | async-start | bytes 262144 | tf_op jit(solution)/shard_map/all_to_all | solution.py:21
  170.4 0.0 collective-permute-done.1
  170.4 1.2 pad_maximum_fusion
  171.6 0.7 gather_fusion.1
  172.3 0.1 broadcast_select_fusion
  172.4 0.4 fusion.32
  172.8 0.1 fusion.6
  172.9 27.7 %all-to-all-done.6 = bf16[32,8,224]{2,1,0:T(8,128)(2,1)S(1)} async-done(((bf16[32,8,224]{2,1,0:T(8,128)(2,1)}), bf16[32,8,224]{2,1,0:T(8,128)(2,1)S(1)}, u32[]{:S(2)}, u32[]{:S(2)}) %all-to-all-start.6) | async-done | bytes 114720 | tf_op jit(solution)/shard_map/all_to_all | solution.py:21
  200.5 0.3 fusion.3
  200.8 0.6 copy.38
  201.4 5.8 %all-to-all-start.7 = ((bf16[32,1,224]{2,1,0:T(2,128)(2,1)}), bf16[32,1,224]{2,1,0:T(2,128)(2,1)S(1)}, u32[]{:S(2)}, u32[]{:S(2)}) async-start(bf16[32,1,224]{2,1,0:T(2,128)(2,1)} %copy.38), calls=%async_computation.7 | async-start | bytes 65536 | tf_op jit(solution)/shard_map/all_to_all | solution.py:21
  207.3 1.0 fusion.1
  208.3 6.4 %all-to-all-done.7 = bf16[32,1,224]{2,1,0:T(2,128)(2,1)S(1)} async-done(((bf16[32,1,224]{2,1,0:T(2,128)(2,1)}), bf16[32,1,224]{2,1,0:T(2,128)(2,1)S(1)}, u32[]{:S(2)}, u32[]{:S(2)}) %all-to-all-start.7) | async-done | bytes 14368 | tf_op jit(solution)/shard_map/all_to_all | solution.py:21
  214.6 0.1 reduce.3
  214.7 0.7 reshape.203
  (21 shorter events, 0.1 us)
Async XLA Ops:
  0.6 171.8 %copy-start = (bf16[1,128,576]{1,2,0:T(8,128)(2,1)S(1)}, bf16[1,128,576]{1,2,0:T(8,128)(2,1)}, u32[]{:S(2)}) copy-start(bf16[1,128,576]{1,2,0:T(8,128)(2,1)} %param.15) | copy-start | bytes 442372
  4.9 24.6 %all-to-all-start = ((bf16[32,2,128]{2,1,0:T(2,128)(2,1)}), bf16[32,2,128]{2,1,0:T(2,128)(2,1)S(1)}, u32[]{:S(2)}, u32[]{:S(2)}) async-start(bf16[32,2,128]{2,1,0:T(2,128)(2,1)} %reshape.224), calls=%async_computation | async-start | bytes 32768 | tf_op jit(solution)/shard_map/all_to_all | solution.py:21
  79.1 27.8 %all-to-all-start.2 = ((bf16[8,448,256]{2,1,0:T(8,128)(2,1)}), bf16[8,448,256]{2,1,0:T(8,128)(2,1)S(1)}, u32[]{:S(2)}, u32[]{:S(2)}) async-start(bf16[8,448,256]{2,1,0:T(8,128)(2,1)} %bitcast.69), calls=%async_computation.2 | async-start | bytes 3670016 | tf_op jit(solution)/shard_map/all_to_all | solution.py:21
  82.7 5.7 %collective-permute-start.2 = (bf16[256,224]{1,0:T(8,128)(2,1)S(1)}, bf16[256,224]{1,0:T(8,128)(2,1)S(1)}, u32[]{:S(2)}, u32[]{:S(2)}) collective-permute-start(bf16[256,224]{1,0:T(8,128)(2,1)S(1)} %bitcast.65), channel_id=1, source_target_pairs={{0,1},{1,0},{2,3},{3,2},{4,5},{5,4},{6,7},{7,6},{8,9},{9,8},{10,11... | collective-permute-start | bytes 344072 | tf_op jit(solution)/shard_map/ppermute | solution.py:179
  108.6 3.8 %copy-start.2 = (bf16[1,1,128,3584]{3,2,1,0:T(8,128)(2,1)S(1)}, bf16[1,1,128,3584]{3,2,1,0:T(8,128)(2,1)}, u32[]{:S(2)}) copy-start(bf16[1,1,128,3584]{3,2,1,0:T(8,128)(2,1)} %param.14) | copy-start | bytes 2752516
  108.6 5.1 %copy-start.3 = (s32[1,4]{1,0:T(1,128)S(1)}, s32[1,4]{1,0:T(1,128)}, u32[]{:S(2)}) copy-start(s32[1,4]{1,0:T(1,128)} %param.17) | copy-start | bytes 52
  108.6 5.1 %copy-start.1 = (bf16[8,64,576]{2,1,0:T(8,128)(2,1)S(1)}, bf16[8,64,576]{2,1,0:T(8,128)(2,1)}, u32[]{:S(2)}) copy-start(bf16[8,64,576]{2,1,0:T(8,128)(2,1)} %param.16) | copy-start | bytes 1769476
  108.6 19.9 %all-to-all-start.3 = ((bf16[16,256,128]{2,1,0:T(8,128)(2,1)}), bf16[16,256,128]{2,1,0:T(8,128)(2,1)S(1)}, u32[]{:S(2)}, u32[]{:S(2)}) async-start(bf16[16,256,128]{2,1,0:T(8,128)(2,1)} %shard_map.113), calls=%async_computation.3 | async-start | bytes 2097152 | tf_op jit(solution)/shard_map/all_to_all | solution.py:21
  113.8 27.6 %copy-start.4 = (s32[1,8]{1,0:T(1,128)S(1)}, s32[1,8]{1,0:T(1,128)}, u32[]{:S(2)}) copy-start(s32[1,8]{1,0:T(1,128)} %param.18) | copy-start | bytes 100
  128.5 17.9 %all-to-all-start.5 = ((bf16[8,2,128,224]{2,3,1,0:T(8,128)(2,1)}), bf16[8,2,128,224]{2,3,1,0:T(8,128)(2,1)S(1)}, u32[]{:S(2)}, u32[]{:S(2)}) async-start(bf16[8,2,128,224]{2,3,1,0:T(8,128)(2,1)} %bitcast.25), calls=%async_computation.5 | async-start | bytes 1835008 | tf_op jit(solution)/shard_map/all_to_all | solution.py:21
  132.9 37.5 %collective-permute-start = (bf16[2,64,576]{2,1,0:T(8,128)(2,1)}, bf16[2,64,576]{2,1,0:T(8,128)(2,1)}, u32[]{:S(2)}, u32[]{:S(2)}) collective-permute-start(bf16[2,64,576]{2,1,0:T(8,128)(2,1)} %get-tuple-element.6), channel_id=1, source_target_pairs={{0,1},{1,2},{2,3},{3,4},{4,5},{5,6},{6,7},{7,8},{8,9},{9,10},{10,1... | collective-permute-start | bytes 442376 | tf_op jit(solution)/shard_map/ppermute | solution.py:121
  138.8 31.6 %collective-permute-start.1 = (bf16[2,64,576]{2,1,0:T(8,128)(2,1)S(1)}, bf16[2,64,576]{2,1,0:T(8,128)(2,1)}, u32[]{:S(2)}, u32[]{:S(2)}) collective-permute-start(bf16[2,64,576]{2,1,0:T(8,128)(2,1)S(1)} %get-tuple-element.7), channel_id=1, source_target_pairs={{1,0},{2,1},{3,2},{4,3},{5,4},{6,5},{7,6},{8,7},{9,8},{10,9},{11,1... | collective-permute-start | bytes 442376 | tf_op jit(solution)/shard_map/ppermute | solution.py:122
  146.4 13.5 %all-to-all-start.4 = ((bf16[16,64,256]{2,1,0:T(8,128)(2,1)}), bf16[16,64,256]{2,1,0:T(8,128)(2,1)S(1)}, u32[]{:S(2)}, u32[]{:S(2)}) async-start(bf16[16,64,256]{2,1,0:T(8,128)(2,1)} %shard_map.114), calls=%async_computation.4 | async-start | bytes 1048576 | tf_op jit(solution)/shard_map/all_to_all | solution.py:21
  160.3 5.5 %collective-permute-start.3 = (bf16[256,224]{1,0:T(8,128)(2,1)S(1)}, bf16[256,224]{1,0:T(8,128)(2,1)S(1)}, u32[]{:S(2)}, u32[]{:S(2)}) collective-permute-start(bf16[256,224]{1,0:T(8,128)(2,1)S(1)} %get-tuple-element.5), channel_id=1, source_target_pairs={{0,1},{1,0},{2,3},{3,2},{4,5},{5,4},{6,7},{7,6},{8,9},{9,8},{10,11... | collective-permute-start | bytes 344072 | tf_op jit(solution)/shard_map/ppermute | solution.py:184
  166.5 34.1 %all-to-all-start.6 = ((bf16[32,8,224]{2,1,0:T(8,128)(2,1)}), bf16[32,8,224]{2,1,0:T(8,128)(2,1)S(1)}, u32[]{:S(2)}, u32[]{:S(2)}) async-start(bf16[32,8,224]{2,1,0:T(8,128)(2,1)} %fusion.8), calls=%async_computation.6 | async-start | bytes 262144 | tf_op jit(solution)/shard_map/all_to_all | solution.py:21
  201.4 13.2 %all-to-all-start.7 = ((bf16[32,1,224]{2,1,0:T(2,128)(2,1)}), bf16[32,1,224]{2,1,0:T(2,128)(2,1)S(1)}, u32[]{:S(2)}, u32[]{:S(2)}) async-start(bf16[32,1,224]{2,1,0:T(2,128)(2,1)} %copy.38), calls=%async_computation.7 | async-start | bytes 65536 | tf_op jit(solution)/shard_map/all_to_all | solution.py:21

commit v4 on v3

--- a/solution.py
+++ b/solution.py
@@ -9,7 +9,6 @@
 SLICE = 224
 WIDE = 256
 HALF = ("y", "x", "c")
-CHIPS = ("h", "y", "x")
 EP = ("h",) + HALF
 
 
@@ -21,68 +20,34 @@
     return lax.all_to_all(value, axes, split_axis=0, concat_axis=0, tiled=True)
 
 
-def gate_up_kernel(core, own, other, weights, out):
-    mine = core[0]
-    chips, units = weights.shape[0], weights.shape[3] // 2
-    part = units // 2
-    for i in range(chips):
-        sums = jnp.dot(own[...], weights[i, mine], preferred_element_type=jnp.float32)
-        sums += jnp.dot(other[...], weights[i, 1 - mine], preferred_element_type=jnp.float32)
-        for h in range(2):
-            pair = [sums[:, n * part : (n + 1) * part] for n in (h, 2 + h)]
-            out[h * chips + i] = jnp.concatenate(pair, axis=1).astype(out.dtype)
-
-
-def gate_up_sums(core, own, other, weights):
-    chips, _, width, columns = weights.shape
-    rows = own.shape[0]
-    out_shape = (2 * chips, rows, columns // 2)
-    return pl.pallas_call(
-        gate_up_kernel,
-        out_shape=jax.ShapeDtypeStruct(out_shape, jnp.bfloat16),
-        in_specs=[pl.BlockSpec(memory_space=pltpu.SMEM)]
-        + [pl.BlockSpec(memory_space=pltpu.VMEM)] * 3,
-        out_specs=pl.BlockSpec(memory_space=pltpu.VMEM),
-        compiler_params=pltpu.CompilerParams(vmem_limit_bytes=32 << 20),
-        cost_estimate=pl.CostEstimate(
-            flops=4 * chips * rows * width * columns,
-            bytes_accessed=2 * weights.size + 4 * out_shape[0] * rows * columns // 2,
-            transcendentals=0,
-        ),
-    )(core, own, other, weights)
-
-
-def activation_kernel(parts, out):
-    units = parts.shape[2] // 2
-    sums = parts[0].astype(jnp.float32)
-    for n in range(1, parts.shape[0]):
-        sums += parts[n].astype(jnp.float32)
+def activation_kernel(own, partner, out):
+    units = out.shape[1]
+    sums = own[...] + partner[...].astype(jnp.float32)
     gate, up = sums[:, :units], sums[:, units:]
     value = (jax.nn.silu(gate) * up).T.astype(out.dtype)
     for n in range(out.shape[0]):
         out[n] = value
 
 
-def activated(parts):
-    count, rows, columns = parts.shape
+def activated(own, partner, count):
+    rows, columns = own.shape
     out_shape = (count, columns // 2, rows)
     return pl.pallas_call(
         activation_kernel,
         out_shape=jax.ShapeDtypeStruct(out_shape, jnp.bfloat16),
-        in_specs=[pl.BlockSpec(memory_space=pltpu.VMEM)],
+        in_specs=[pl.BlockSpec(memory_space=pltpu.VMEM)] * 2,
         out_specs=pl.BlockSpec(memory_space=pltpu.VMEM),
         compiler_params=pltpu.CompilerParams(vmem_limit_bytes=32 << 20),
         cost_estimate=pl.CostEstimate(
-            flops=2 * parts.size, bytes_accessed=3 * parts.size, transcendentals=0
+            flops=8 * own.size, bytes_accessed=6 * own.size + count * own.size, transcendentals=0
         ),
-    )(parts)
+    )(own, partner)
 
 
 def down_kernel(core, values, weights, kept, given):
     mine = core[0]
     chips, _, units, width = weights.shape
-    pieces = [values[h * chips + i] for i in range(chips) for h in range(2)]
-    held = jnp.concatenate(pieces, axis=0)
+    held = jnp.concatenate([values[i] for i in range(chips)], axis=0)
     for n, out in ((mine, kept), (1 - mine, given)):
         matrix = jnp.concatenate([weights[i, n] for i in range(chips)], axis=0)
         out[...] = lax.dot_general(
@@ -171,15 +136,23 @@
         preferred_element_type=jnp.float32,
     ).astype(jnp.bfloat16)
     arrived = exchanged(sent_rows.reshape(groups, capacity, SLICE), "z").reshape(rows, SLICE)
-    gate_up = gate_up_blocks.reshape(chips, 2 * SLICE, 2 * units)
-    gate_up = exchanged(gate_up, ("y", "x")).reshape(chips, 2, SLICE, 2 * units)
+    same_core = exchanged(jnp.broadcast_to(arrived[None], (chips, rows, SLICE)), ("y", "x"))
     down = down_blocks.reshape(units, chips, 2, SLICE).transpose(1, 2, 0, 3)
+    down, same_core = lax.optimization_barrier((down, same_core))
     down = exchanged(down, ("y", "x"))
-    core = lax.axis_index("c").reshape(1).astype(jnp.int32)
-    other = lax.ppermute(arrived, "c", [(0, 1), (1, 0)])
-    partial_sum = gate_up_sums(core, arrived, other, gate_up)
-    activation = activated(exchanged(partial_sum, CHIPS))
-    activation = exchanged(activation, CHIPS)
+    other_core = lax.ppermute(same_core, "c", [(0, 1), (1, 0)])
+    by_core = gate_up_blocks.reshape(chips, 2, SLICE, 2 * units)
+    core = lax.axis_index("c")
+    same_weights = lax.dynamic_index_in_dim(by_core, core, 1, keepdims=False)
+    other_weights = lax.dynamic_index_in_dim(by_core, 1 - core, 1, keepdims=False)
+    partial_sum = jnp.einsum(
+        "urk,ukn->rn", same_core, same_weights, preferred_element_type=jnp.float32
+    ) + jnp.einsum("urk,ukn->rn", other_core, other_weights, preferred_element_type=jnp.float32)
+    partner_sum = lax.ppermute(partial_sum.astype(jnp.bfloat16), "h", [(0, 1), (1, 0)])
+    activation = activated(partial_sum, partner_sum, chips)
+    activation, down = lax.optimization_barrier((activation, down))
+    activation = exchanged(activation, ("y", "x"))
+    core = core.reshape(1).astype(jnp.int32)
     kept, given = down_sums(core, activation, down)
     summed = kept + lax.ppermute(given, "c", [(0, 1), (1, 0)]).astype(jnp.float32)
     summed = summed.astype(jnp.bfloat16).reshape(groups, capacity, SLICE)

time: 216 us -> 203 us (0.940)
  waiting for transfers between devices: 88.1 us -> 63.9 us
  other arithmetic: 5.88 us -> 12 us
  local copies, waits for them, and re-layouts: 6.99 us -> 12.1 us
  matrix products: 2.08 us -> 5.96 us
  starting transfers between devices: 58.8 us -> 56.5 us
    all_to_all x7 -> x6, waiting for transfers between devices: 86.4 us -> 55.7 us  [exchanged(): return lax.all_to_all(value, axes, split_axis=0, concat_axis=0, tiled=True)]
    ppermute x1 -> x2, waiting for transfers between devices: 0.96 us -> 8.15 us  [the longest x1 8.14 us: expert_part(): lax.ppermute(partial_sum.astype(jnp.bfloat16), 'h', [(0, 1), (1, 0)])]
    ppermute x1, starting transfers between devices: 5.92 us -> 2.44 us  [attention_part(): low = lax.ppermute(departing[moving:], EP, forward)]
    ppermute x1 -> x2, starting transfers between devices: 4.7 us -> 7.41 us  [the longest x1 4.26 us: expert_part(): lax.ppermute(partial_sum.astype(jnp.bfloat16), 'h', [(0, 1), (1, 0)])]
    all_to_all x7 -> x6, starting transfers between devices: 41.8 us -> 42 us  [exchanged(): return lax.all_to_all(value, axes, split_axis=0, concat_axis=0, tiled=True)]
  transfers between devices with their start and end apart: 11 -> 11, of which waited for: 9 -> 6; matrix products, arithmetic and copies ran while one was open for 4% -> 10% of each run, Pallas kernels for 1% -> 1%
where the time goes in v4:
time: 203 us; the launch traced here: 202 us
  waiting for transfers between devices  63.9 us (31%)
  starting transfers between devices  56.5 us (28%)
  blocking collectives  48.7 us (24%)
  local copies, waits for them, and re-layouts  12.1 us (6%)
  other arithmetic  12 us (6%)
  matrix products  5.96 us (3%)
    all_to_all x6, waiting for transfers between devices, exchanged(): return lax.all_to_all(value, axes, split_axis=0, concat_axis=0, tiled=True)  55.7 us
    all_to_all x1, blocking collectives, exchanged(): return lax.all_to_all(value, axes, split_axis=0, concat_axis=0, tiled=True)  48.7 us
    all_to_all x6, starting transfers between devices, exchanged(): return lax.all_to_all(value, axes, split_axis=0, concat_axis=0, tiled=True)  42 us
    ppermute x1, waiting for transfers between devices, expert_part(): lax.ppermute(partial_sum.astype(jnp.bfloat16), 'h', [(0, 1), (1, 0)])  8.14 us
    ppermute x1, starting transfers between devices, expert_part(): lax.ppermute(partial_sum.astype(jnp.bfloat16), 'h', [(0, 1), (1, 0)])  4.26 us
  transfers between devices with their start and end apart: 11, of which 6 were waited for; matrix products, arithmetic and copies ran while one was open for 10% of the time, Pallas kernels for 1%

profile of v4, /device:TPU:1, one launch (start us, length us, event | category | flops | bytes accessed | tf_op | source)
XLA Modules:
  0.0 202.1 jit_solution(8778632634363632361)
XLA Ops:
  0.6 1.0 reduce.2
  1.6 0.1 reshape.189
  1.7 0.7 convert_bitcast_fusion
  2.4 0.7 fusion.36
  3.1 0.1 pad.6.clone
  3.2 0.5 broadcast.143
  3.7 0.7 reduce.4
  4.4 0.6 reshape.219
  5.0 17.6 %all-to-all-start = ((bf16[32,2,128]{2,1,0:T(2,128)(2,1)}), bf16[32,2,128]{2,1,0:T(2,128)(2,1)S(1)}, u32[]{:S(2)}, u32[]{:S(2)}) async-start(bf16[32,2,128]{2,1,0:T(2,128)(2,1)} %reshape.219), calls=%async_computation | async-start | bytes 32768 | tf_op jit(solution)/shard_map/all_to_all | solution.py:20
  22.6 0.1 eq.45
  22.7 6.9 %all-to-all-done = bf16[32,2,128]{2,1,0:T(2,128)(2,1)S(1)} async-done(((bf16[32,2,128]{2,1,0:T(2,128)(2,1)}), bf16[32,2,128]{2,1,0:T(2,128)(2,1)S(1)}, u32[]{:S(2)}, u32[]{:S(2)}) %all-to-all-start) | async-done | bytes 16416 | tf_op jit(solution)/shard_map/all_to_all | solution.py:20
  29.6 0.1 slice_convert_fusion
  29.7 0.1 fusion.17
  29.8 0.2 fusion.29
  30.0 0.1 copy.38
  30.1 0.3 convolution_convert_fusion.1
  30.4 0.1 copy.41
  30.5 48.7 %all_to_all.46 = bf16[32,8,224]{2,1,0:T(8,128)(2,1)S(1)} all-to-all(bf16[32,8,224]{2,1,0:T(8,128)(2,1)S(1)} %bitcast.87), channel_id=1, replica_groups=mesh['z'=32,'h'=2,'y'=2,'x'=4,'c'=2] {'z'}, dimensions={0} | all-to-all | bytes 229376 | tf_op jit(solution)/shard_map/all_to_all | solution.py:20
  79.2 0.1 copy.42
  79.3 1.0 broadcast_in_dim.105
  80.4 3.7 %all-to-all-start.2 = ((bf16[8,256,224]{1,2,0:T(8,128)(2,1)}), bf16[8,256,224]{1,2,0:T(8,128)(2,1)S(1)}, u32[]{:S(2)}, u32[]{:S(2)}) async-start(bf16[8,256,224]{1,2,0:T(8,128)(2,1)} %broadcast_in_dim.105), calls=%async_computation.2 | async-start | bytes 1835008 | tf_op jit(solution)/shard_map/all_to_all | solution.py:20
  84.1 2.2 %copy.40 = bf16[1,1,128,3584]{2,3,1,0:T(8,128)(2,1)} copy(bf16[1,1,128,3584]{3,2,1,0:T(8,128)(2,1)} %param.14) | data formatting | bytes 1835008 | tf_op args[4]
  86.3 11.7 %all-to-all-done.2 = bf16[8,256,224]{1,2,0:T(8,128)(2,1)S(1)} async-done(((bf16[8,256,224]{1,2,0:T(8,128)(2,1)}), bf16[8,256,224]{1,2,0:T(8,128)(2,1)S(1)}, u32[]{:S(2)}, u32[]{:S(2)}) %all-to-all-start.2) | async-done | bytes 917536 | tf_op jit(solution)/shard_map/all_to_all | solution.py:20
  98.0 3.2 %collective-permute-start.2 = (bf16[8,256,224]{1,2,0:T(8,128)(2,1)S(1)}, bf16[8,256,224]{1,2,0:T(8,128)(2,1)}, u32[]{:S(2)}, u32[]{:S(2)}) collective-permute-start(bf16[8,256,224]{1,2,0:T(8,128)(2,1)S(1)} %all-to-all-done.2), channel_id=1, source_target_pairs={{0,1},{1,0},{2,3},{3,2},{4,5},{5,4},{6,7},{7,6},{8,9},{9,8},{10,11... | collective-permute-start | bytes 2752520 | tf_op jit(solution)/shard_map/ppermute | solution.py:143
  101.2 1.3 gather_fusion
  102.5 1.1 broadcast_select_fusion.1
  103.6 0.8 fusion.38
  104.3 2.4 %collective-permute-start = (bf16[2,64,576]{2,1,0:T(8,128)(2,1)}, bf16[2,64,576]{2,1,0:T(8,128)(2,1)}, u32[]{:S(2)}, u32[]{:S(2)}) collective-permute-start(bf16[2,64,576]{2,1,0:T(8,128)(2,1)} %get-tuple-element.14), channel_id=1, source_target_pairs={{0,1},{1,2},{2,3},{3,4},{4,5},{5,6},{6,7},{7,8},{8,9},{9,10},{10,1... | collective-permute-start | bytes 442376 | tf_op jit(solution)/shard_map/ppermute | solution.py:86
  106.8 1.9 collective-permute-start.1
  109.4 4.2 %all-to-all-start.3 = ((bf16[8,2,128,224]{2,3,1,0:T(8,128)(2,1)}), bf16[8,2,128,224]{2,3,1,0:T(8,128)(2,1)}, u32[]{:S(2)}, u32[]{:S(2)}) async-start(bf16[8,2,128,224]{2,3,1,0:T(8,128)(2,1)} %bitcast.19), calls=%async_computation.3 | async-start | bytes 1835008 | tf_op jit(solution)/shard_map/all_to_all | solution.py:20
  113.7 0.4 convolution_bitcast_fusion.1
  114.1 1.6 fusion.40
  115.8 4.3 %collective-permute-start.3 = (bf16[256,256]{1,0:T(8,128)(2,1)S(1)}, bf16[256,256]{1,0:T(8,128)(2,1)S(1)}, u32[]{:S(2)}, u32[]{:S(2)}) collective-permute-start(bf16[256,256]{1,0:T(8,128)(2,1)S(1)} %get-tuple-element.18), channel_id=1, source_target_pairs={{0,16},{16,0},{1,17},{17,1},{2,18},{18,2},{3,19},{19,3},{4,20},{20... | collective-permute-start | bytes 393224 | tf_op jit(solution)/shard_map/ppermute | solution.py:151
  120.0 8.1 %collective-permute-done.3.partner = bf16[256,256]{1,0:T(8,128)(2,1)S(1)} collective-permute-done((bf16[256,256]{1,0:T(8,128)(2,1)S(1)}, bf16[256,256]{1,0:T(8,128)(2,1)S(1)}, u32[]{:S(2)}, u32[]{:S(2)}) %collective-permute-start.3) | collective-permute-done | bytes 131104 | tf_op jit(solution)/shard_map/ppermute | solution.py:151
  128.2 0.9 shard_map.113
  129.1 5.8 %all-to-all-start.4 = ((bf16[8,128,256]{2,1,0:T(8,128)(2,1)}), bf16[8,128,256]{2,1,0:T(8,128)(2,1)S(1)}, u32[]{:S(2)}, u32[]{:S(2)}) async-start(bf16[8,128,256]{2,1,0:T(8,128)(2,1)} %shard_map.113), calls=%async_computation.4 | async-start | bytes 1048576 | tf_op jit(solution)/shard_map/all_to_all | solution.py:20
  134.9 0.5 iota_compare_fusion.4
  135.4 0.1 broadcast_in_dim.95
  135.5 0.6 broadcast_in_dim.96
  136.1 0.6 pad_clamp_fusion
  136.7 0.2 convert_reduce_fusion
  136.9 0.7 fusion.27
  137.6 1.5 copy.45.weights
  139.1 6.0 %all-to-all-done.4.values = bf16[8,128,256]{2,1,0:T(8,128)(2,1)S(1)} async-done(((bf16[8,128,256]{2,1,0:T(8,128)(2,1)}), bf16[8,128,256]{2,1,0:T(8,128)(2,1)S(1)}, u32[]{:S(2)}, u32[]{:S(2)}) %all-to-all-start.4) | async-done | bytes 524320 | tf_op jit(solution)/shard_map/all_to_all | solution.py:20
  145.1 0.5 shard_map.114
  145.6 0.7 copy-done.1
  146.3 2.8 %collective-permute-start.4 = (bf16[256,224]{1,0:T(8,128)(2,1)S(1)}, bf16[256,224]{1,0:T(8,128)(2,1)S(1)}, u32[]{:S(2)}, u32[]{:S(2)}) collective-permute-start(bf16[256,224]{1,0:T(8,128)(2,1)S(1)} %get-tuple-element.13), channel_id=1, source_target_pairs={{0,1},{1,0},{2,3},{3,2},{4,5},{5,4},{6,7},{7,6},{8,9},{9,8},{10,11... | collective-permute-start | bytes 344072 | tf_op jit(solution)/shard_map/ppermute | solution.py:157
  149.0 0.9 select_reduce_fusion
  150.0 1.6 fusion.13
  151.6 4.7 %all-to-all-start.5 = ((bf16[32,8,224]{2,1,0:T(8,128)(2,1)}), bf16[32,8,224]{2,1,0:T(8,128)(2,1)}, u32[]{:S(2)}, u32[]{:S(2)}) async-start(bf16[32,8,224]{2,1,0:T(8,128)(2,1)} %fusion.13), calls=%async_computation.5 | async-start | bytes 262144 | tf_op jit(solution)/shard_map/all_to_all | solution.py:20
  156.3 1.4 fusion.20
  157.8 1.4 pad_maximum_fusion
  159.2 0.8 gather_fusion.1
  160.0 0.1 broadcast_select_fusion
  160.2 1.3 fusion.39
  161.4 0.1 fusion.11
  161.5 24.8 %all-to-all-done.5 = bf16[32,8,224]{2,1,0:T(8,128)(2,1)} async-done(((bf16[32,8,224]{2,1,0:T(8,128)(2,1)}), bf16[32,8,224]{2,1,0:T(8,128)(2,1)}, u32[]{:S(2)}, u32[]{:S(2)}) %all-to-all-start.5) | async-done | bytes 114720 | tf_op jit(solution)/shard_map/all_to_all | solution.py:20
  186.3 1.2 fusion.4
  187.5 0.6 copy.48
  188.1 5.9 %all-to-all-start.6 = ((bf16[32,1,224]{2,1,0:T(2,128)(2,1)}), bf16[32,1,224]{2,1,0:T(2,128)(2,1)S(1)}, u32[]{:S(2)}, u32[]{:S(2)}) async-start(bf16[32,1,224]{2,1,0:T(2,128)(2,1)} %copy.48), calls=%async_computation.6 | async-start | bytes 65536 | tf_op jit(solution)/shard_map/all_to_all | solution.py:20
  194.0 1.0 fusion.2
  195.0 6.3 %all-to-all-done.6 = bf16[32,1,224]{2,1,0:T(2,128)(2,1)S(1)} async-done(((bf16[32,1,224]{2,1,0:T(2,128)(2,1)}), bf16[32,1,224]{2,1,0:T(2,128)(2,1)S(1)}, u32[]{:S(2)}, u32[]{:S(2)}) %all-to-all-start.6) | async-done | bytes 14368 | tf_op jit(solution)/shard_map/all_to_all | solution.py:20
  201.3 0.1 reduce.3
  201.4 0.7 reshape.196
  (38 shorter events, 0.2 us)
Async XLA Ops:
  0.6 113.0 %copy-start = (bf16[1,1,3584,256]{3,2,1,0:T(8,128)(2,1)S(1)}, bf16[1,1,3584,256]{3,2,1,0:T(8,128)(2,1)}, u32[]{:S(2)}) copy-start(bf16[1,1,3584,256]{3,2,1,0:T(8,128)(2,1)} %param.13) | copy-start | bytes 5505028
  5.0 24.6 %all-to-all-start = ((bf16[32,2,128]{2,1,0:T(2,128)(2,1)}), bf16[32,2,128]{2,1,0:T(2,128)(2,1)S(1)}, u32[]{:S(2)}, u32[]{:S(2)}) async-start(bf16[32,2,128]{2,1,0:T(2,128)(2,1)} %reshape.219), calls=%async_computation | async-start | bytes 32768 | tf_op jit(solution)/shard_map/all_to_all | solution.py:20
  30.0 50.3 %copy-start.4 = (f32[32,32]{1,0:T(8,128)}, f32[32,32]{1,0:T(8,128)S(1)}, u32[]{:S(2)}) copy-start(f32[32,32]{1,0:T(8,128)S(1)} %fusion.29) | copy-start | bytes 12292
  30.1 50.3 %copy-start.5 = (pred[32,32]{1,0:T(8,128)(4,1)}, pred[32,32]{1,0:T(8,128)(4,1)S(1)}, u32[]{:S(2)}) copy-start(pred[32,32]{1,0:T(8,128)(4,1)S(1)} %copy.38) | copy-start | bytes 3076
  80.3 5.9 %copy-start.9 = (s32[1,4]{1,0:T(1,128)S(1)}, s32[1,4]{1,0:T(1,128)}, u32[]{:S(2)}) copy-start(s32[1,4]{1,0:T(1,128)} %param.17) | copy-start | bytes 52
  80.3 20.8 %copy-start.2 = (bf16[8,64,576]{2,1,0:T(8,128)(2,1)S(1)}, bf16[8,64,576]{2,1,0:T(8,128)(2,1)}, u32[]{:S(2)}) copy-start(bf16[8,64,576]{2,1,0:T(8,128)(2,1)} %param.16) | copy-start | bytes 1769476
  80.4 17.6 %all-to-all-start.2 = ((bf16[8,256,224]{1,2,0:T(8,128)(2,1)}), bf16[8,256,224]{1,2,0:T(8,128)(2,1)S(1)}, u32[]{:S(2)}, u32[]{:S(2)}) async-start(bf16[8,256,224]{1,2,0:T(8,128)(2,1)} %broadcast_in_dim.105), calls=%async_computation.2 | async-start | bytes 1835008 | tf_op jit(solution)/shard_map/all_to_all | solution.py:20
  98.0 16.1 %collective-permute-start.2 = (bf16[8,256,224]{1,2,0:T(8,128)(2,1)S(1)}, bf16[8,256,224]{1,2,0:T(8,128)(2,1)}, u32[]{:S(2)}, u32[]{:S(2)}) collective-permute-start(bf16[8,256,224]{1,2,0:T(8,128)(2,1)S(1)} %all-to-all-done.2), channel_id=1, source_target_pairs={{0,1},{1,0},{2,3},{3,2},{4,5},{5,4},{6,7},{7,6},{8,9},{9,8},{10,11... | collective-permute-start | bytes 2752520 | tf_op jit(solution)/shard_map/ppermute | solution.py:143
  101.2 12.5 %copy-start.10 = (s32[1,8]{1,0:T(1,128)S(1)}, s32[1,8]{1,0:T(1,128)}, u32[]{:S(2)}) copy-start(s32[1,8]{1,0:T(1,128)} %param.18) | copy-start | bytes 100
  104.3 53.4 %collective-permute-start = (bf16[2,64,576]{2,1,0:T(8,128)(2,1)}, bf16[2,64,576]{2,1,0:T(8,128)(2,1)}, u32[]{:S(2)}, u32[]{:S(2)}) collective-permute-start(bf16[2,64,576]{2,1,0:T(8,128)(2,1)} %get-tuple-element.14), channel_id=1, source_target_pairs={{0,1},{1,2},{2,3},{3,4},{4,5},{5,6},{6,7},{7,8},{8,9},{9,10},{10,1... | collective-permute-start | bytes 442376 | tf_op jit(solution)/shard_map/ppermute | solution.py:86
  106.8 51.0 %collective-permute-start.1 = (bf16[2,64,576]{2,1,0:T(8,128)(2,1)}, bf16[2,64,576]{2,1,0:T(8,128)(2,1)}, u32[]{:S(2)}, u32[]{:S(2)}) collective-permute-start(bf16[2,64,576]{2,1,0:T(8,128)(2,1)} %get-tuple-element.15), channel_id=1, source_target_pairs={{1,0},{2,1},{3,2},{4,3},{5,4},{6,5},{7,6},{8,7},{9,8},{10,9},{11,1... | collective-permute-start | bytes 442376 | tf_op jit(solution)/shard_map/ppermute | solution.py:87
  109.4 19.7 %all-to-all-start.3 = ((bf16[8,2,128,224]{2,3,1,0:T(8,128)(2,1)}), bf16[8,2,128,224]{2,3,1,0:T(8,128)(2,1)}, u32[]{:S(2)}, u32[]{:S(2)}) async-start(bf16[8,2,128,224]{2,3,1,0:T(8,128)(2,1)} %bitcast.19), calls=%async_computation.3 | async-start | bytes 1835008 | tf_op jit(solution)/shard_map/all_to_all | solution.py:20
  115.8 12.4 %collective-permute-start.3 = (bf16[256,256]{1,0:T(8,128)(2,1)S(1)}, bf16[256,256]{1,0:T(8,128)(2,1)S(1)}, u32[]{:S(2)}, u32[]{:S(2)}) collective-permute-start(bf16[256,256]{1,0:T(8,128)(2,1)S(1)} %get-tuple-element.18), channel_id=1, source_target_pairs={{0,16},{16,0},{1,17},{17,1},{2,18},{18,2},{3,19},{19,3},{4,20},{20... | collective-permute-start | bytes 393224 | tf_op jit(solution)/shard_map/ppermute | solution.py:151
  120.0 16.1 %copy-start.7 = (pred[8]{0:T(512)(128)(4,1)}, pred[8]{0:T(512)(128)(4,1)S(1)}, u32[]{:S(2)}) copy-start(pred[8]{0:T(512)(128)(4,1)S(1)} %compare_and_fusion.1) | copy-start | bytes 28
  129.1 16.0 %all-to-all-start.4 = ((bf16[8,128,256]{2,1,0:T(8,128)(2,1)}), bf16[8,128,256]{2,1,0:T(8,128)(2,1)S(1)}, u32[]{:S(2)}, u32[]{:S(2)}) async-start(bf16[8,128,256]{2,1,0:T(8,128)(2,1)} %shard_map.113), calls=%async_computation.4 | async-start | bytes 1048576 | tf_op jit(solution)/shard_map/all_to_all | solution.py:20
  145.6 0.7 copy-start.1
  146.3 3.7 %collective-permute-start.4 = (bf16[256,224]{1,0:T(8,128)(2,1)S(1)}, bf16[256,224]{1,0:T(8,128)(2,1)S(1)}, u32[]{:S(2)}, u32[]{:S(2)}) collective-permute-start(bf16[256,224]{1,0:T(8,128)(2,1)S(1)} %get-tuple-element.13), channel_id=1, source_target_pairs={{0,1},{1,0},{2,3},{3,2},{4,5},{5,4},{6,7},{7,6},{8,9},{9,8},{10,11... | collective-permute-start | bytes 344072 | tf_op jit(solution)/shard_map/ppermute | solution.py:157
  151.6 8.4 %copy-start.8 = (pred[8]{0:T(512)(128)(4,1)S(1)}, pred[8]{0:T(512)(128)(4,1)}, u32[]{:S(2)}) copy-start(pred[8]{0:T(512)(128)(4,1)} %copy-done.7) | copy-start | bytes 28
  151.6 34.7 %all-to-all-start.5 = ((bf16[32,8,224]{2,1,0:T(8,128)(2,1)}), bf16[32,8,224]{2,1,0:T(8,128)(2,1)}, u32[]{:S(2)}, u32[]{:S(2)}) async-start(bf16[32,8,224]{2,1,0:T(8,128)(2,1)} %fusion.13), calls=%async_computation.5 | async-start | bytes 262144 | tf_op jit(solution)/shard_map/all_to_all | solution.py:20
  157.8 2.4 %copy-start.6 = (pred[512]{0:T(512)(128)(4,1)S(1)}, pred[512]{0:T(512)(128)(4,1)}, u32[]{:S(2)}) copy-start(pred[512]{0:T(512)(128)(4,1)} %iota_compare_fusion.4) | copy-start | bytes 1540
  160.0 26.3 %copy-start.3 = (f32[32,8,32]{2,1,0:T(8,128)S(1)}, f32[32,8,32]{2,1,0:T(8,128)}, u32[]{:S(2)}) copy-start(f32[32,8,32]{2,1,0:T(8,128)} %fusion.20) | copy-start | bytes 98308
  160.0 34.0 %copy-start.11 = (pred[512]{0:T(512)(128)(4,1)S(1)}, pred[512]{0:T(512)(128)(4,1)}, u32[]{:S(2)}) copy-start(pred[512]{0:T(512)(128)(4,1)} %broadcast_in_dim.96) | copy-start | bytes 1540
  188.1 13.2 %all-to-all-start.6 = ((bf16[32,1,224]{2,1,0:T(2,128)(2,1)}), bf16[32,1,224]{2,1,0:T(2,128)(2,1)S(1)}, u32[]{:S(2)}, u32[]{:S(2)}) async-start(bf16[32,1,224]{2,1,0:T(2,128)(2,1)} %copy.48), calls=%async_computation.6 | async-start | bytes 65536 | tf_op jit(solution)/shard_map/all_to_all | solution.py:20

commit v5 on v4

v5 whole, which is shorter than its diff:
```python
import jax
import jax.numpy as jnp
from jax import lax
from jax.experimental import pallas as pl
from jax.experimental.pallas import tpu as pltpu
from jax.sharding import Mesh, PartitionSpec as P

KVL = 512
SLICE = 224
WIDE = 256
HALF = ("y", "x", "c")
EP = ("h",) + HALF


softmax_scale = 192.0 ** (-0.5)
routed_scale = 2.5


def exchanged(value, axes):
    return lax.all_to_all(value, axes, split_axis=0, concat_axis=0, tiled=True)


def activation_kernel(own, partner, out):
    units = out.shape[1]
    sums = own[...] + partner[...].astype(jnp.float32)
    gate, up = sums[:, :units], sums[:, units:]
    value = (jax.nn.silu(gate) * up).T.astype(out.dtype)
    for n in range(out.shape[0]):
        out[n] = value


def activated(own, partner, count):
    rows, columns = own.shape
    out_shape = (count, columns // 2, rows)
    return pl.pallas_call(
        activation_kernel,
        out_shape=jax.ShapeDtypeStruct(out_shape, jnp.bfloat16),
        in_specs=[pl.BlockSpec(memory_space=pltpu.VMEM)] * 2,
        out_specs=pl.BlockSpec(memory_space=pltpu.VMEM),
        compiler_params=pltpu.CompilerParams(vmem_limit_bytes=32 << 20),
        cost_estimate=pl.CostEstimate(
            flops=8 * own.size, bytes_accessed=6 * own.size + count * own.size, transcendentals=0
        ),
    )(own, partner)


def down_kernel(core, values, weights, kept, given):
    mine = core[0]
    chips, _, units, width = weights.shape
    held = jnp.concatenate([values[i] for i in range(chips)], axis=0)
    for n, out in ((mine, kept), (1 - mine, given)):
        matrix = jnp.concatenate([weights[i, n] for i in range(chips)], axis=0)
        out[...] = lax.dot_general(
            held, matrix, (((0,), (0,)), ((), ())), preferred_element_type=jnp.float32
        ).astype(out.dtype)


def down_sums(core, values, weights):
    chips, _, units, width = weights.shape
    rows = values.shape[2]
    return pl.pallas_call(
        down_kernel,
        out_shape=(
            jax.ShapeDtypeStruct((rows, width), jnp.float32),
            jax.ShapeDtypeStruct((rows, width), jnp.bfloat16),
        ),
        in_specs=[pl.BlockSpec(memory_space=pltpu.SMEM)]
        + [pl.BlockSpec(memory_space=pltpu.VMEM)] * 2,
        out_specs=(pl.BlockSpec(memory_space=pltpu.VMEM),) * 2,
        compiler_params=pltpu.CompilerParams(vmem_limit_bytes=32 << 20),
        cost_estimate=pl.CostEstimate(
            flops=4 * chips * rows * width * units,
            bytes_accessed=2 * weights.size + 2 * values.size + 6 * rows * width,
            transcendentals=0,
        ),
    )(core, values, weights)


def whole(count):
    return [pl.BlockSpec(memory_space=pltpu.VMEM)] * count


def page_kernel(moves, first, rest, lower, higher):
    lower[...] = first[...]
    higher[...] = rest[...]


def departing_pages(latent_pool, page_moves):
    block = (1,) + latent_pool.shape[1:]
    moving = page_moves.shape[1] // 2
    shape = jax.ShapeDtypeStruct((moving,) + latent_pool.shape[1:], latent_pool.dtype)
    return pl.pallas_call(
        page_kernel,
        out_shape=(shape, shape),
        grid_spec=pltpu.PrefetchScalarGridSpec(
            num_scalar_prefetch=1,
            grid=(moving,),
            in_specs=[
                pl.BlockSpec(block, lambda i, moves: (moves[0, i], 0, 0)),
                pl.BlockSpec(block, lambda i, moves: (moves[0, moving + i], 0, 0)),
            ],
            out_specs=[pl.BlockSpec(block, lambda i, moves: (i, 0, 0))] * 2,
        ),
        cost_estimate=pl.CostEstimate(
            flops=0, bytes_accessed=8 * moving * block[1] * block[2], transcendentals=0
        ),
    )(page_moves, latent_pool, latent_pool)


def attention_kernel(page_list, lengths, queries, pool, low, high, out, rows):
    count, page = page_list.shape[1], pool.shape[1]
    moving = low.shape[0]
    for j in range(count):
        number = page_list[0, j]
        if j < 2 * moving:
            number = number - pool.shape[0]
            upper = number >= moving
            from_low = low[jnp.where(upper, 0, number)]
            from_high = high[jnp.where(upper, number - moving, 0)]
            block = jnp.where(upper, from_high, from_low)
        else:
            block = pool[number]
        rows[j * page : (j + 1) * page, :] = block
    scores = lax.dot_general(
        queries[0], rows[...], (((1,), (1,)), ((), ())), preferred_element_type=jnp.float32
    )
    place = lax.broadcasted_iota(jnp.int32, scores.shape, 1)
    scores = jnp.where(place < lengths[0], scores * softmax_scale, -1e30)
    values = jnp.exp(scores - jnp.max(scores, axis=1, keepdims=True))
    weights = (values / jnp.sum(values, axis=1, keepdims=True)).astype(jnp.bfloat16)
    mixed = jnp.dot(weights, rows[:, : out.shape[2]], preferred_element_type=jnp.float32)
    out[0] = mixed.astype(out.dtype)


def attention(queries, latent_pool, low, high, page_list, lengths):
    _, heads, width = queries.shape
    count = page_list.shape[1] * latent_pool.shape[1]
    return pl.pallas_call(
        attention_kernel,
        out_shape=jax.ShapeDtypeStruct((1, heads, KVL), jnp.bfloat16),
        in_specs=[pl.BlockSpec(memory_space=pltpu.SMEM)] * 2 + whole(4),
        out_specs=pl.BlockSpec(memory_space=pltpu.VMEM),
        scratch_shapes=[pltpu.VMEM((count, width), jnp.bfloat16)],
        compiler_params=pltpu.CompilerParams(vmem_limit_bytes=16 << 20),
        cost_estimate=pl.CostEstimate(
            flops=2 * heads * count * (width + KVL),
            bytes_accessed=2 * (latent_pool.size + 2 * queries.size),
            transcendentals=heads * count,
        ),
    )(page_list, lengths, queries, latent_pool, low, high)


def prepare_kernel(tokens, chosen, affinity, out):
    members, _, lanes = out.shape
    row = tokens[...].astype(jnp.float32)
    choices = chosen.shape[2]
    routing = [chosen[0].astype(jnp.float32), affinity[0].astype(jnp.float32)]
    routing.append(jnp.zeros((1, 2 * lanes - SLICE - 2 * choices), jnp.float32))
    for p in range(members):
        first = row[:, p * SLICE : p * SLICE + lanes]
        second = [row[:, p * SLICE + lanes : (p + 1) * SLICE]] + routing
        pair = [first, jnp.concatenate(second, axis=1)]
        out[p] = jnp.concatenate(pair, axis=0).astype(out.dtype)


def prepared(tokens, expert_ids, affinity, members):
    return pl.pallas_call(
        prepare_kernel,
        out_shape=jax.ShapeDtypeStruct((members, 2, WIDE // 2), jnp.bfloat16),
        in_specs=whole(3),
        out_specs=pl.BlockSpec(memory_space=pltpu.VMEM),
        cost_estimate=pl.CostEstimate(
            flops=0, bytes_accessed=4 * tokens.size, transcendentals=0
        ),
    )(tokens, expert_ids, affinity)


def sum_kernel(kept, given, out):
    out[...] = (kept[...] + given[...].astype(jnp.float32)).astype(out.dtype).reshape(out.shape)


def added(kept, given, groups):
    rows, width = kept.shape
    return pl.pallas_call(
        sum_kernel,
        out_shape=jax.ShapeDtypeStruct((groups, rows // groups, width), jnp.bfloat16),
        in_specs=whole(2),
        out_specs=pl.BlockSpec(memory_space=pltpu.VMEM),
        cost_estimate=pl.CostEstimate(
            flops=kept.size, bytes_accessed=8 * kept.size, transcendentals=0
        ),
    )(kept, given)


def shards(
    tokens,
    expert_ids,
    affinity,
    gate_up_blocks,
    down_blocks,
    queries,
    latent_pool,
    page_moves,
    page_list,
    lengths,
):
    members = lax.axis_size(EP)
    groups = lax.axis_size("z")
    chips = lax.axis_size(HALF) // 2
    choices = expert_ids.shape[2]
    capacity = members * choices // groups
    rows = groups * capacity
    units = gate_up_blocks.shape[3] // 2
    core = lax.axis_index("c")
    held = exchanged(prepared(tokens, expert_ids, affinity, members), EP)
    held, page_moves = lax.optimization_barrier((held, page_moves))
    held = held.reshape(members, WIDE)
    chosen = held[:, SLICE : SLICE + choices].astype(jnp.float32)
    affinity_all = held[:, SLICE + choices : SLICE + 2 * choices].astype(jnp.float32)
    route_weights = routed_scale * affinity_all / jnp.sum(affinity_all, axis=1, keepdims=True)
    matches = chosen[:, :, None] == jnp.arange(groups, dtype=jnp.float32)[None, None, :]
    member = jnp.any(matches, axis=1)
    weight_of = jnp.sum(jnp.where(matches, route_weights[:, :, None], 0.0), axis=1)
    earlier = jnp.arange(members)[:, None] > jnp.arange(members)[None, :]
    position = jnp.dot(
        earlier.astype(jnp.bfloat16),
        member.astype(jnp.bfloat16),
        preferred_element_type=jnp.float32,
    )
    slot_number = jnp.arange(capacity, dtype=jnp.float32)
    selector = member.T[:, None, :] & (position.T[:, None, :] == slot_number[None, :, None])
    sent_rows = jnp.dot(
        selector.astype(jnp.bfloat16).reshape(rows, members),
        held[:, :SLICE],
        preferred_element_type=jnp.float32,
    ).astype(jnp.bfloat16)
    arrived = exchanged(sent_rows.reshape(groups, capacity, SLICE), "z").reshape(rows, SLICE)
    to_lower, to_higher = departing_pages(latent_pool, page_moves)
    forward = [(i, (i + 1) % members) for i in range(members)]
    backward = [(target, source) for source, target in forward]
    low = lax.ppermute(to_higher, EP, forward)
    high = lax.ppermute(to_lower, EP, backward)
    arrived, low, high = lax.optimization_barrier((arrived, low, high))
    same_core = exchanged(jnp.broadcast_to(arrived[None], (chips, rows, SLICE)), ("y", "x"))
    down = down_blocks.reshape(units, chips, 2, SLICE).transpose(1, 2, 0, 3)
    down, same_core = lax.optimization_barrier((down, same_core))
    down = exchanged(down, ("y", "x"))
    other_core = lax.ppermute(same_core, "c", [(0, 1), (1, 0)])
    by_core = gate_up_blocks.reshape(chips, 2, SLICE, 2 * units)
    same_weights = lax.dynamic_index_in_dim(by_core, core, 1, keepdims=False)
    other_weights = lax.dynamic_index_in_dim(by_core, 1 - core, 1, keepdims=False)
    partial_sum = jnp.einsum(
        "urk,ukn->rn", same_core, same_weights, preferred_element_type=jnp.float32
    ) + jnp.einsum("urk,ukn->rn", other_core, other_weights, preferred_element_type=jnp.float32)
    partner_sum = lax.ppermute(partial_sum.astype(jnp.bfloat16), "h", [(0, 1), (1, 0)])
    activation = activated(partial_sum, partner_sum, chips)
    activation, down = lax.optimization_barrier((activation, down))
    activation = exchanged(activation, ("y", "x"))
    kept, given = down_sums(core.reshape(1).astype(jnp.int32), activation, down)
    summed = added(kept, lax.ppermute(given, "c", [(0, 1), (1, 0)]), groups)
    summed, low, high = lax.optimization_barrier((summed, low, high))
    attention_latent = attention(queries, latent_pool, low, high, page_list, lengths)
    returned = exchanged(summed, "z").reshape(rows, SLICE)
    returned, attention_latent = lax.optimization_barrier((returned, attention_latent))
    weighted = jnp.where(selector, weight_of.T[:, None, :], 0.0).reshape(rows, members)
    mixed = jnp.einsum(
        "rn,rk->nk", weighted, returned.astype(jnp.float32), precision=lax.Precision.HIGHEST
    )
    expert_mix = exchanged(mixed.astype(jnp.bfloat16), EP).reshape(1, -1)
    return (attention_latent, expert_mix)


def solution(mesh):
    fine = Mesh(mesh.devices.reshape(32, 2, 2, 4, 2), ("z",) + EP)
    both = ("z",) + EP
    placed = (
        P(both, None),
        P("z", EP, None),
        P("z", EP, None),
        P("z", EP, None, None),
        P("z", EP, None, None),
        P(both, None, None),
        P(both, None, None),
        P(both, None),
        P(both, None),
        P(both),
    )
    return jax.shard_map(
        shards,
        mesh=fine,
        in_specs=placed,
        out_specs=(P(both, None, None), P(both, None)),
        check_vma=False,
    )
```

time: 203 us -> 197 us (0.970)
  blocking collectives: 48.7 us -> 15.1 us
  waiting for transfers between devices: 63.9 us -> 82.1 us
  starting transfers between devices: 56.5 us -> 68.9 us
  other arithmetic: 12 us -> 2.82 us
  Pallas kernels: 1.38 us -> 10.1 us
  matrix products: 5.96 us -> 2.86 us
    all_to_all x1, blocking collectives: 48.7 us -> 15.1 us  [exchanged(): return lax.all_to_all(value, axes, split_axis=0, concat_axis=0, tiled=True)]
    all_to_all x6, starting transfers between devices: 42 us -> 55.2 us  [exchanged(): return lax.all_to_all(value, axes, split_axis=0, concat_axis=0, tiled=True)]
    all_to_all x6, waiting for transfers between devices: 55.7 us -> 65.5 us  [exchanged(): return lax.all_to_all(value, axes, split_axis=0, concat_axis=0, tiled=True)]
    ppermute x5, waiting for transfers between devices: 8.17 us -> 16.6 us  [the longest x1 11.1 us: shards(): lax.ppermute(partial_sum.astype(jnp.bfloat16), 'h', [(0, 1), (1, 0)])]
    pallas_call x0 -> x4, Pallas kernels: none -> 7.68 us  [the longest x1 2.39 us: departing_pages(): pl.pallas_call(page_kernel, out_shape=(shape, shape), grid_spec=pltpu.Pre...]
    unnamed x28 -> x29, local copies, waits for them, and re-layouts: 3.59 us -> 8.43 us
    dot_general x7 -> x5, matrix products: 5.96 us -> 2.86 us  [the longest x1 1.63 us: shards(): jnp.einsum('urk,ukn->rn', other_core, other_weights, preferred_element_ty...]
    select_n x5 -> x0, other arithmetic: 2.63 us -> none  [the longest x1 1.41 us: expert_part(): jnp.where(selector, weight_of.T[:, None, :], 0.0).reshape(rows, members)]
  transfers between devices with their start and end apart: 11 -> 11, of which waited for: 6 -> 9; matrix products, arithmetic and copies ran while one was open for 10% -> 5% of each run, Pallas kernels for 1% -> 3%
where the time goes in v5:
time: 197 us; the launch traced here: 196 us
  waiting for transfers between devices  82.1 us (42%)
  starting transfers between devices  68.9 us (35%)
  blocking collectives  15.1 us (8%)
  local copies, waits for them, and re-layouts  12.8 us (6%)
  Pallas kernels  10.1 us (5%)
  matrix products  2.86 us (1%)
  other arithmetic  2.82 us (1%)
    all_to_all x6, waiting for transfers between devices, exchanged(): return lax.all_to_all(value, axes, split_axis=0, concat_axis=0, tiled=True)  65.5 us
    all_to_all x6, starting transfers between devices, exchanged(): return lax.all_to_all(value, axes, split_axis=0, concat_axis=0, tiled=True)  55.2 us
    all_to_all x1, blocking collectives, exchanged(): return lax.all_to_all(value, axes, split_axis=0, concat_axis=0, tiled=True)  15.1 us
    ppermute x1, waiting for transfers between devices, shards(): lax.ppermute(partial_sum.astype(jnp.bfloat16), 'h', [(0, 1), (1, 0)])  11.1 us
    unnamed x29, local copies, waits for them, and re-layouts  8.43 us
  transfers between devices with their start and end apart: 11, of which 9 were waited for; matrix products, arithmetic and copies ran while one was open for 5% of the time, Pallas kernels for 3%

profile of v5, /device:TPU:1, one launch (start us, length us, event | category | flops | bytes accessed | tf_op | source)
XLA Modules:
  0.0 196.2 jit_solution(986219806109301078)
XLA Ops:
  0.6 0.0 copy-start
  0.6 1.7 shard_map.113
  2.4 17.6 %all-to-all-start = ((bf16[32,2,128]{2,1,0:T(2,128)(2,1)}), bf16[32,2,128]{2,1,0:T(2,128)(2,1)S(1)}, u32[]{:S(2)}, u32[]{:S(2)}) async-start(bf16[32,2,128]{2,1,0:T(2,128)(2,1)} %shard_map.113), calls=%async_computation | async-start | bytes 32768 | tf_op jit(solution)/shard_map/all_to_all | solution.py:20
  20.0 0.1 eq.40
  20.1 6.9 %all-to-all-done = bf16[32,2,128]{2,1,0:T(2,128)(2,1)S(1)} async-done(((bf16[32,2,128]{2,1,0:T(2,128)(2,1)}), bf16[32,2,128]{2,1,0:T(2,128)(2,1)S(1)}, u32[]{:S(2)}, u32[]{:S(2)}) %all-to-all-start) | async-done | bytes 16416 | tf_op jit(solution)/shard_map/all_to_all | solution.py:20
  27.0 0.1 slice_convert_fusion
  27.1 0.6 copy-done.9
  27.7 0.1 fusion.6
  27.8 0.2 fusion.20
  28.0 0.1 copy.43
  28.1 0.3 convolution_convert_fusion
  28.4 0.8 copy.44
  29.1 0.0 copy-done.8
  29.1 19.3 %all-to-all-start.1 = ((bf16[32,8,224]{2,1,0:T(8,128)(2,1)}), bf16[32,8,224]{2,1,0:T(8,128)(2,1)S(1)}, u32[]{:S(2)}, u32[]{:S(2)}) async-start(bf16[32,8,224]{2,1,0:T(8,128)(2,1)} %bitcast.6), calls=%async_computation.1 | async-start | bytes 262144 | tf_op jit(solution)/shard_map/all_to_all | solution.py:20
  48.4 2.4 %shard_map.114 = (bf16[2,64,576]{2,1,0:T(8,128)(2,1)}, bf16[2,64,576]{2,1,0:T(8,128)(2,1)}) custom-call(s32[1,4]{1,0:T(1,128)} %moves, bf16[8,64,576]{2,1,0:T(8,128)(2,1)} %pool.1, bf16[8,64,576]{2,1,0:T(8,128)(2,1)} %pool.1), custom_call_target="tpu_custom_call" | custom-call | bytes 589824 | tf_op jit(solution)/shard_map/pallas_call | solution.py:92
  50.8 3.0 %collective-permute-start = (bf16[2,64,576]{2,1,0:T(8,128)(2,1)}, bf16[2,64,576]{2,1,0:T(8,128)(2,1)S(1)}, u32[]{:S(2)}, u32[]{:S(2)}) collective-permute-start(bf16[2,64,576]{2,1,0:T(8,128)(2,1)} %get-tuple-element.22), channel_id=1, source_target_pairs={{0,1},{1,2},{2,3},{3,4},{4,5},{5,6},{6,7},{7,8},{8,9},{9,10},{10,1... | collective-permute-start | bytes 442376 | tf_op jit(solution)/shard_map/ppermute | solution.py:241
  53.9 1.9 collective-permute-start.1
  55.8 0.6 collective-permute-done.low
  56.4 0.7 copy-done.3
  57.1 3.9 %collective-permute-done.1.high = bf16[2,64,576]{2,1,0:T(8,128)(2,1)S(1)} collective-permute-done((bf16[2,64,576]{2,1,0:T(8,128)(2,1)}, bf16[2,64,576]{2,1,0:T(8,128)(2,1)S(1)}, u32[]{:S(2)}, u32[]{:S(2)}) %collective-permute-start.1) | collective-permute-done | bytes 147488 | tf_op jit(solution)/shard_map/ppermute | solution.py:242
  61.0 0.7 copy-done.5
  61.7 16.4 %all-to-all-done.1 = bf16[32,8,224]{2,1,0:T(8,128)(2,1)S(1)} async-done(((bf16[32,8,224]{2,1,0:T(8,128)(2,1)}), bf16[32,8,224]{2,1,0:T(8,128)(2,1)S(1)}, u32[]{:S(2)}, u32[]{:S(2)}) %all-to-all-start.1) | async-done | bytes 114720 | tf_op jit(solution)/shard_map/all_to_all | solution.py:20
  78.1 0.0 copy-done.11
  78.1 0.1 copy.45
  78.2 1.0 broadcast_in_dim.24
  79.2 3.6 %all-to-all-start.2 = ((bf16[8,256,224]{1,2,0:T(8,128)(2,1)}), bf16[8,256,224]{1,2,0:T(8,128)(2,1)S(1)}, u32[]{:S(2)}, u32[]{:S(2)}) async-start(bf16[8,256,224]{1,2,0:T(8,128)(2,1)} %broadcast_in_dim.24), calls=%async_computation.2 | async-start | bytes 1835008 | tf_op jit(solution)/shard_map/all_to_all | solution.py:20
  82.8 2.2 %copy.42 = bf16[1,1,128,3584]{2,3,1,0:T(8,128)(2,1)} copy(bf16[1,1,128,3584]{3,2,1,0:T(8,128)(2,1)} %param.14) | data formatting | bytes 1835008 | tf_op args[4]
  85.0 11.7 %all-to-all-done.2 = bf16[8,256,224]{1,2,0:T(8,128)(2,1)S(1)} async-done(((bf16[8,256,224]{1,2,0:T(8,128)(2,1)}), bf16[8,256,224]{1,2,0:T(8,128)(2,1)S(1)}, u32[]{:S(2)}, u32[]{:S(2)}) %all-to-all-start.2) | async-done | bytes 917536 | tf_op jit(solution)/shard_map/all_to_all | solution.py:20
  96.7 3.2 %collective-permute-start.2 = (bf16[8,256,224]{1,2,0:T(8,128)(2,1)S(1)}, bf16[8,256,224]{1,2,0:T(8,128)(2,1)}, u32[]{:S(2)}, u32[]{:S(2)}) collective-permute-start(bf16[8,256,224]{1,2,0:T(8,128)(2,1)S(1)} %all-to-all-done.2), channel_id=1, source_target_pairs={{0,1},{1,0},{2,3},{3,2},{4,5},{5,4},{6,7},{7,6},{8,9},{9,8},{10,11... | collective-permute-start | bytes 2752520 | tf_op jit(solution)/shard_map/ppermute | solution.py:248
  99.9 4.2 %all-to-all-start.3 = ((bf16[8,2,128,224]{2,3,1,0:T(8,128)(2,1)}), bf16[8,2,128,224]{2,3,1,0:T(8,128)(2,1)}, u32[]{:S(2)}, u32[]{:S(2)}) async-start(bf16[8,2,128,224]{2,3,1,0:T(8,128)(2,1)} %bitcast.2), calls=%async_computation.3 | async-start | bytes 1835008 | tf_op jit(solution)/shard_map/all_to_all | solution.py:20
  104.1 0.0 copy-done
  104.1 0.4 convolution_bitcast_fusion.1
  104.6 0.0 collective-permute-done.2
  104.6 1.6 fusion.25
  106.2 2.9 %collective-permute-start.3 = (bf16[256,256]{1,0:T(8,128)(2,1)S(1)}, bf16[256,256]{1,0:T(8,128)(2,1)S(1)}, u32[]{:S(2)}, u32[]{:S(2)}) collective-permute-start(bf16[256,256]{1,0:T(8,128)(2,1)S(1)} %get-tuple-element.38), channel_id=1, source_target_pairs={{0,16},{16,0},{1,17},{17,1},{2,18},{18,2},{3,19},{19,3},{4,20},{20... | collective-permute-start | bytes 393224 | tf_op jit(solution)/shard_map/ppermute | solution.py:255
  109.1 11.1 %collective-permute-done.3.partner = bf16[256,256]{1,0:T(8,128)(2,1)S(1)} collective-permute-done((bf16[256,256]{1,0:T(8,128)(2,1)S(1)}, bf16[256,256]{1,0:T(8,128)(2,1)S(1)}, u32[]{:S(2)}, u32[]{:S(2)}) %collective-permute-start.3) | collective-permute-done | bytes 131104 | tf_op jit(solution)/shard_map/ppermute | solution.py:255
  120.2 0.9 shard_map.115
  121.1 0.0 all-to-all-done.3
  121.1 4.1 %all-to-all-start.4 = ((bf16[8,128,256]{2,1,0:T(8,128)(2,1)}), bf16[8,128,256]{2,1,0:T(8,128)(2,1)}, u32[]{:S(2)}, u32[]{:S(2)}) async-start(bf16[8,128,256]{2,1,0:T(8,128)(2,1)} %shard_map.115), calls=%async_computation.4 | async-start | bytes 1048576 | tf_op jit(solution)/shard_map/all_to_all | solution.py:20
  125.2 1.5 copy.48.weights
  126.7 0.0 copy-start.1
  126.7 0.0 copy-start.7
  126.7 8.8 %all-to-all-done.4.values = bf16[8,128,256]{2,1,0:T(8,128)(2,1)} async-done(((bf16[8,128,256]{2,1,0:T(8,128)(2,1)}), bf16[8,128,256]{2,1,0:T(8,128)(2,1)}, u32[]{:S(2)}, u32[]{:S(2)}) %all-to-all-start.4) | async-done | bytes 524320 | tf_op jit(solution)/shard_map/all_to_all | solution.py:20
  135.5 1.5 shard_map.116
  137.0 0.7 copy-done.2
  137.7 2.8 %collective-permute-start.4 = (bf16[256,224]{1,0:T(8,128)(2,1)S(1)}, bf16[256,224]{1,0:T(8,128)(2,1)S(1)}, u32[]{:S(2)}, u32[]{:S(2)}) collective-permute-start(bf16[256,224]{1,0:T(8,128)(2,1)S(1)} %get-tuple-element.30), channel_id=1, source_target_pairs={{0,1},{1,0},{2,3},{3,2},{4,5},{5,4},{6,7},{7,6},{8,9},{9,8},{10,11... | collective-permute-start | bytes 344072 | tf_op jit(solution)/shard_map/ppermute | solution.py:260
  140.5 1.0 collective-permute-done.4.given
  141.5 0.7 copy-done.10
  142.2 1.7 shard_map.117
  143.8 6.3 %all-to-all-start.5 = ((bf16[32,8,224]{2,1,0:T(8,128)(2,1)}), bf16[32,8,224]{2,1,0:T(8,128)(2,1)S(1)}, u32[]{:S(2)}, u32[]{:S(2)}) async-start(bf16[32,8,224]{2,1,0:T(8,128)(2,1)} %shard_map.117), calls=%async_computation.5 | async-start | bytes 262144 | tf_op jit(solution)/shard_map/all_to_all | solution.py:20
  150.1 1.1 copy.49.queries
  151.8 0.9 convert_reduce_fusion
  152.7 0.8 fusion.18
  153.5 0.9 select_reduce_fusion
  154.4 0.1 copy.50
  154.4 0.0 copy-done.1
  154.5 0.9 copy-done.4
  155.4 0.9 copy-done.6
  156.3 1.9 shard_map.118
  158.2 21.7 %all-to-all-done.5 = bf16[32,8,224]{2,1,0:T(8,128)(2,1)S(1)} async-done(((bf16[32,8,224]{2,1,0:T(8,128)(2,1)}), bf16[32,8,224]{2,1,0:T(8,128)(2,1)S(1)}, u32[]{:S(2)}, u32[]{:S(2)}) %all-to-all-start.5) | async-done | bytes 114720 | tf_op jit(solution)/shard_map/all_to_all | solution.py:20
  179.9 0.3 fusion.1
  180.3 15.1 %all_to_all.39 = bf16[32,1,224]{2,1,0:T(2,128)(2,1)S(1)} all-to-all(bf16[32,1,224]{2,1,0:T(2,128)(2,1)S(1)} %copy.51), channel_id=1, replica_groups=mesh['z'=32,'h'=2,'y'=2,'x'=4,'c'=2] {'h','y','x','c'}, dimensions={0} | all-to-all | bytes 28672 | tf_op jit(solution)/shard_map/all_to_all | solution.py:20
  195.4 0.1 reduce
  195.5 0.7 reshape.54
  (15 shorter events, 0.1 us)
Async XLA Ops:
  0.6 103.5 %copy-start = (bf16[1,1,3584,256]{3,2,1,0:T(8,128)(2,1)S(1)}, bf16[1,1,3584,256]{3,2,1,0:T(8,128)(2,1)}, u32[]{:S(2)}) copy-start(bf16[1,1,3584,256]{3,2,1,0:T(8,128)(2,1)} %param.13) | copy-start | bytes 5505028
  2.4 24.6 %all-to-all-start = ((bf16[32,2,128]{2,1,0:T(2,128)(2,1)}), bf16[32,2,128]{2,1,0:T(2,128)(2,1)S(1)}, u32[]{:S(2)}, u32[]{:S(2)}) async-start(bf16[32,2,128]{2,1,0:T(2,128)(2,1)} %shard_map.113), calls=%async_computation | async-start | bytes 32768 | tf_op jit(solution)/shard_map/all_to_all | solution.py:20
  27.0 2.1 %copy-start.8 = (bf16[4,8,2,128]{3,1,2,0:T(8,128)(2,1)}, bf16[4,8,2,128]{3,1,2,0:T(8,128)(2,1)S(1)}, u32[]{:S(2)}) copy-start(bf16[4,8,2,128]{3,1,2,0:T(8,128)(2,1)S(1)} %copy.56) | copy-start | bytes 49156
  27.1 0.6 copy-start.9
  28.0 50.1 %copy-start.11 = (f32[32,32]{1,0:T(8,128)}, f32[32,32]{1,0:T(8,128)S(1)}, u32[]{:S(2)}) copy-start(f32[32,32]{1,0:T(8,128)S(1)} %fusion.20) | copy-start | bytes 12292
  29.1 48.9 %all-to-all-start.1 = ((bf16[32,8,224]{2,1,0:T(8,128)(2,1)}), bf16[32,8,224]{2,1,0:T(8,128)(2,1)S(1)}, u32[]{:S(2)}, u32[]{:S(2)}) async-start(bf16[32,8,224]{2,1,0:T(8,128)(2,1)} %bitcast.6), calls=%async_computation.1 | async-start | bytes 262144 | tf_op jit(solution)/shard_map/all_to_all | solution.py:20
  50.8 5.6 %collective-permute-start = (bf16[2,64,576]{2,1,0:T(8,128)(2,1)}, bf16[2,64,576]{2,1,0:T(8,128)(2,1)S(1)}, u32[]{:S(2)}, u32[]{:S(2)}) collective-permute-start(bf16[2,64,576]{2,1,0:T(8,128)(2,1)} %get-tuple-element.22), channel_id=1, source_target_pairs={{0,1},{1,2},{2,3},{3,4},{4,5},{5,6},{6,7},{7,8},{8,9},{9,10},{10,1... | collective-permute-start | bytes 442376 | tf_op jit(solution)/shard_map/ppermute | solution.py:241
  53.9 7.1 %collective-permute-start.1 = (bf16[2,64,576]{2,1,0:T(8,128)(2,1)}, bf16[2,64,576]{2,1,0:T(8,128)(2,1)S(1)}, u32[]{:S(2)}, u32[]{:S(2)}) collective-permute-start(bf16[2,64,576]{2,1,0:T(8,128)(2,1)} %get-tuple-element.23), channel_id=1, source_target_pairs={{1,0},{2,1},{3,2},{4,3},{5,4},{6,5},{7,6},{8,7},{9,8},{10,9},{11,1... | collective-permute-start | bytes 442376 | tf_op jit(solution)/shard_map/ppermute | solution.py:242
  56.4 0.7 copy-start.3
  61.0 0.7 copy-start.5
  79.2 17.5 %all-to-all-start.2 = ((bf16[8,256,224]{1,2,0:T(8,128)(2,1)}), bf16[8,256,224]{1,2,0:T(8,128)(2,1)S(1)}, u32[]{:S(2)}, u32[]{:S(2)}) async-start(bf16[8,256,224]{1,2,0:T(8,128)(2,1)} %broadcast_in_dim.24), calls=%async_computation.2 | async-start | bytes 1835008 | tf_op jit(solution)/shard_map/all_to_all | solution.py:20
  96.7 7.9 %collective-permute-start.2 = (bf16[8,256,224]{1,2,0:T(8,128)(2,1)S(1)}, bf16[8,256,224]{1,2,0:T(8,128)(2,1)}, u32[]{:S(2)}, u32[]{:S(2)}) collective-permute-start(bf16[8,256,224]{1,2,0:T(8,128)(2,1)S(1)} %all-to-all-done.2), channel_id=1, source_target_pairs={{0,1},{1,0},{2,3},{3,2},{4,5},{5,4},{6,7},{7,6},{8,9},{9,8},{10,11... | collective-permute-start | bytes 2752520 | tf_op jit(solution)/shard_map/ppermute | solution.py:248
  99.9 21.2 %all-to-all-start.3 = ((bf16[8,2,128,224]{2,3,1,0:T(8,128)(2,1)}), bf16[8,2,128,224]{2,3,1,0:T(8,128)(2,1)}, u32[]{:S(2)}, u32[]{:S(2)}) async-start(bf16[8,2,128,224]{2,3,1,0:T(8,128)(2,1)} %bitcast.2), calls=%async_computation.3 | async-start | bytes 1835008 | tf_op jit(solution)/shard_map/all_to_all | solution.py:20
  106.2 14.0 %collective-permute-start.3 = (bf16[256,256]{1,0:T(8,128)(2,1)S(1)}, bf16[256,256]{1,0:T(8,128)(2,1)S(1)}, u32[]{:S(2)}, u32[]{:S(2)}) collective-permute-start(bf16[256,256]{1,0:T(8,128)(2,1)S(1)} %get-tuple-element.38), channel_id=1, source_target_pairs={{0,16},{16,0},{1,17},{17,1},{2,18},{18,2},{3,19},{19,3},{4,20},{20... | collective-permute-start | bytes 393224 | tf_op jit(solution)/shard_map/ppermute | solution.py:255
  121.1 14.4 %all-to-all-start.4 = ((bf16[8,128,256]{2,1,0:T(8,128)(2,1)}), bf16[8,128,256]{2,1,0:T(8,128)(2,1)}, u32[]{:S(2)}, u32[]{:S(2)}) async-start(bf16[8,128,256]{2,1,0:T(8,128)(2,1)} %shard_map.115), calls=%async_computation.4 | async-start | bytes 1048576 | tf_op jit(solution)/shard_map/all_to_all | solution.py:20
  126.7 27.7 %copy-start.1 = (bf16[8,64,576]{2,1,0:T(8,128)(2,1)S(1)}, bf16[8,64,576]{2,1,0:T(8,128)(2,1)}, u32[]{:S(2)}) copy-start(bf16[8,64,576]{2,1,0:T(8,128)(2,1)} %pool.1) | copy-start | bytes 1769476
  126.7 27.7 %copy-start.7 = (s32[1,8]{1,0:T(1,128)S(1)}, s32[1,8]{1,0:T(1,128)}, u32[]{:S(2)}) copy-start(s32[1,8]{1,0:T(1,128)} %page_list.1) | copy-start | bytes 100
  137.0 0.7 copy-start.2
  137.7 42.2 %copy-start.12 = (f32[32,32]{1,0:T(8,128)S(1)}, f32[32,32]{1,0:T(8,128)}, u32[]{:S(2)}) copy-start(f32[32,32]{1,0:T(8,128)} %copy-done.11) | copy-start | bytes 12292
  137.7 3.8 %collective-permute-start.4 = (bf16[256,224]{1,0:T(8,128)(2,1)S(1)}, bf16[256,224]{1,0:T(8,128)(2,1)S(1)}, u32[]{:S(2)}, u32[]{:S(2)}) collective-permute-start(bf16[256,224]{1,0:T(8,128)(2,1)S(1)} %get-tuple-element.30), channel_id=1, source_target_pairs={{0,1},{1,0},{2,3},{3,2},{4,5},{5,4},{6,7},{7,6},{8,9},{9,8},{10,11... | collective-permute-start | bytes 344072 | tf_op jit(solution)/shard_map/ppermute | solution.py:260
  141.5 0.7 copy-start.10
  143.8 36.1 %all-to-all-start.5 = ((bf16[32,8,224]{2,1,0:T(8,128)(2,1)}), bf16[32,8,224]{2,1,0:T(8,128)(2,1)S(1)}, u32[]{:S(2)}, u32[]{:S(2)}) async-start(bf16[32,8,224]{2,1,0:T(8,128)(2,1)} %shard_map.117), calls=%async_computation.5 | async-start | bytes 262144 | tf_op jit(solution)/shard_map/all_to_all | solution.py:20
  154.5 0.9 copy-start.4
  155.4 0.9 copy-start.6

commit v6 on v5

--- a/solution.py
+++ b/solution.py
@@ -10,6 +10,7 @@
 WIDE = 256
 HALF = ("y", "x", "c")
 EP = ("h",) + HALF
+MINOR = (((1,), (1,)), ((), ()))
 
 
 softmax_scale = 192.0 ** (-0.5)
@@ -20,60 +21,62 @@
     return lax.all_to_all(value, axes, split_axis=0, concat_axis=0, tiled=True)
 
 
-def activation_kernel(own, partner, out):
-    units = out.shape[1]
+def given_kernel(core, own, partner, weights, values, given):
+    theirs = 1 - core[0]
+    units = values.shape[1]
     sums = own[...] + partner[...].astype(jnp.float32)
-    gate, up = sums[:, :units], sums[:, units:]
-    value = (jax.nn.silu(gate) * up).T.astype(out.dtype)
-    for n in range(out.shape[0]):
-        out[n] = value
-
-
-def activated(own, partner, count):
+    value = jax.nn.silu(sums[:, :units]) * sums[:, units:]
+    values[...] = value.astype(values.dtype)
+    for i in range(weights.shape[0]):
+        given[i] = lax.dot_general(
+            weights[i, theirs], values[...], MINOR, preferred_element_type=jnp.float32
+        ).astype(given.dtype)
+
+
+def given_sums(core, own, partner, weights):
     rows, columns = own.shape
-    out_shape = (count, columns // 2, rows)
-    return pl.pallas_call(
-        activation_kernel,
-        out_shape=jax.ShapeDtypeStruct(out_shape, jnp.bfloat16),
-        in_specs=[pl.BlockSpec(memory_space=pltpu.VMEM)] * 2,
-        out_specs=pl.BlockSpec(memory_space=pltpu.VMEM),
-        compiler_params=pltpu.CompilerParams(vmem_limit_bytes=32 << 20),
-        cost_estimate=pl.CostEstimate(
-            flops=8 * own.size, bytes_accessed=6 * own.size + count * own.size, transcendentals=0
-        ),
-    )(own, partner)
-
-
-def down_kernel(core, values, weights, kept, given):
+    chips, _, width, units = weights.shape
+    return pl.pallas_call(
+        given_kernel,
+        out_shape=(
+            jax.ShapeDtypeStruct((rows, units), jnp.bfloat16),
+            jax.ShapeDtypeStruct((chips, width, rows), jnp.bfloat16),
+        ),
+        in_specs=[pl.BlockSpec(memory_space=pltpu.SMEM)] + whole(3),
+        out_specs=tuple(whole(2)),
+        compiler_params=pltpu.CompilerParams(vmem_limit_bytes=24 << 20),
+        cost_estimate=pl.CostEstimate(
+            flops=2 * chips * rows * width * units,
+            bytes_accessed=2 * weights.size + 6 * own.size + 2 * chips * rows * width,
+            transcendentals=rows * units,
+        ),
+    )(core, own, partner, weights)
+
+
+def kept_kernel(core, values, weights, received, out):
     mine = core[0]
-    chips, _, units, width = weights.shape
-    held = jnp.concatenate([values[i] for i in range(chips)], axis=0)
-    for n, out in ((mine, kept), (1 - mine, given)):
-        matrix = jnp.concatenate([weights[i, n] for i in range(chips)], axis=0)
-        out[...] = lax.dot_general(
-            held, matrix, (((0,), (0,)), ((), ())), preferred_element_type=jnp.float32
-        ).astype(out.dtype)
-
-
-def down_sums(core, values, weights):
-    chips, _, units, width = weights.shape
-    rows = values.shape[2]
-    return pl.pallas_call(
-        down_kernel,
-        out_shape=(
-            jax.ShapeDtypeStruct((rows, width), jnp.float32),
-            jax.ShapeDtypeStruct((rows, width), jnp.bfloat16),
-        ),
-        in_specs=[pl.BlockSpec(memory_space=pltpu.SMEM)]
-        + [pl.BlockSpec(memory_space=pltpu.VMEM)] * 2,
-        out_specs=(pl.BlockSpec(memory_space=pltpu.VMEM),) * 2,
-        compiler_params=pltpu.CompilerParams(vmem_limit_bytes=32 << 20),
-        cost_estimate=pl.CostEstimate(
-            flops=4 * chips * rows * width * units,
-            bytes_accessed=2 * weights.size + 2 * values.size + 6 * rows * width,
+    for i in range(weights.shape[0]):
+        sums = lax.dot_general(
+            weights[i, mine], values[...], MINOR, preferred_element_type=jnp.float32
+        )
+        out[i] = (sums + received[i].astype(jnp.float32)).astype(out.dtype)
+
+
+def kept_sums(core, values, weights, received):
+    chips, _, width, units = weights.shape
+    rows = values.shape[0]
+    return pl.pallas_call(
+        kept_kernel,
+        out_shape=jax.ShapeDtypeStruct((chips, width, rows), jnp.bfloat16),
+        in_specs=[pl.BlockSpec(memory_space=pltpu.SMEM)] + whole(3),
+        out_specs=pl.BlockSpec(memory_space=pltpu.VMEM),
+        compiler_params=pltpu.CompilerParams(vmem_limit_bytes=24 << 20),
+        cost_estimate=pl.CostEstimate(
+            flops=2 * chips * rows * width * units,
+            bytes_accessed=2 * weights.size + 4 * chips * rows * width,
             transcendentals=0,
         ),
-    )(core, values, weights)
+    )(core, values, weights, received)
 
 
 def whole(count):
@@ -175,21 +178,25 @@
     )(tokens, expert_ids, affinity)
 
 
-def sum_kernel(kept, given, out):
-    out[...] = (kept[...] + given[...].astype(jnp.float32)).astype(out.dtype).reshape(out.shape)
-
-
-def added(kept, given, groups):
-    rows, width = kept.shape
+def sum_kernel(parts, out):
+    sums = parts[0].astype(jnp.float32)
+    for n in range(1, parts.shape[0]):
+        sums += parts[n].astype(jnp.float32)
+    out[...] = sums.T.reshape(out.shape).astype(out.dtype)
+
+
+def added(parts, groups):
+    _, width, rows = parts.shape
     return pl.pallas_call(
         sum_kernel,
         out_shape=jax.ShapeDtypeStruct((groups, rows // groups, width), jnp.bfloat16),
-        in_specs=whole(2),
-        out_specs=pl.BlockSpec(memory_space=pltpu.VMEM),
-        cost_estimate=pl.CostEstimate(
-            flops=kept.size, bytes_accessed=8 * kept.size, transcendentals=0
-        ),
-    )(kept, given)
+        in_specs=whole(1),
+        out_specs=pl.BlockSpec(memory_space=pltpu.VMEM),
+        compiler_params=pltpu.CompilerParams(vmem_limit_bytes=24 << 20),
+        cost_estimate=pl.CostEstimate(
+            flops=parts.size, bytes_accessed=2 * parts.size, transcendentals=0
+        ),
+    )(parts)
 
 
 def shards(
@@ -242,9 +249,6 @@
     high = lax.ppermute(to_lower, EP, backward)
     arrived, low, high = lax.optimization_barrier((arrived, low, high))
     same_core = exchanged(jnp.broadcast_to(arrived[None], (chips, rows, SLICE)), ("y", "x"))
-    down = down_blocks.reshape(units, chips, 2, SLICE).transpose(1, 2, 0, 3)
-    down, same_core = lax.optimization_barrier((down, same_core))
-    down = exchanged(down, ("y", "x"))
     other_core = lax.ppermute(same_core, "c", [(0, 1), (1, 0)])
     by_core = gate_up_blocks.reshape(chips, 2, SLICE, 2 * units)
     same_weights = lax.dynamic_index_in_dim(by_core, core, 1, keepdims=False)
@@ -253,11 +257,11 @@
         "urk,ukn->rn", same_core, same_weights, preferred_element_type=jnp.float32
     ) + jnp.einsum("urk,ukn->rn", other_core, other_weights, preferred_element_type=jnp.float32)
     partner_sum = lax.ppermute(partial_sum.astype(jnp.bfloat16), "h", [(0, 1), (1, 0)])
-    activation = activated(partial_sum, partner_sum, chips)
-    activation, down = lax.optimization_barrier((activation, down))
-    activation = exchanged(activation, ("y", "x"))
-    kept, given = down_sums(core.reshape(1).astype(jnp.int32), activation, down)
-    summed = added(kept, lax.ppermute(given, "c", [(0, 1), (1, 0)]), groups)
+    down = down_blocks.reshape(units, chips, 2, SLICE).transpose(1, 2, 3, 0)
+    core = core.reshape(1).astype(jnp.int32)
+    values, given = given_sums(core, partial_sum, partner_sum, down)
+    received = lax.ppermute(given, "c", [(0, 1), (1, 0)])
+    summed = added(exchanged(kept_sums(core, values, down, received), ("y", "x")), groups)
     summed, low, high = lax.optimization_barrier((summed, low, high))
     attention_latent = attention(queries, latent_pool, low, high, page_list, lengths)
     returned = exchanged(summed, "z").reshape(rows, SLICE)

time: 197 us -> 185 us (0.939)
  blocking collectives: 15.1 us -> 43.3 us
  waiting for transfers between devices: 82.1 us -> 62.6 us
  local copies, waits for them, and re-layouts: 12.8 us -> 3.67 us
  starting transfers between devices: 68.9 us -> 61.4 us
  Pallas kernels: 10.1 us -> 7.71 us
  other arithmetic: 2.82 us -> 0.72 us
    all_to_all x1 -> x3, blocking collectives: 15.1 us -> 43.3 us  [exchanged(): return lax.all_to_all(value, axes, split_axis=0, concat_axis=0, tiled=True)]
    all_to_all x6 -> x3, waiting for transfers between devices: 65.5 us -> 50.1 us  [exchanged(): return lax.all_to_all(value, axes, split_axis=0, concat_axis=0, tiled=True)]
    all_to_all x6 -> x3, starting transfers between devices: 55.2 us -> 44.3 us  [exchanged(): return lax.all_to_all(value, axes, split_axis=0, concat_axis=0, tiled=True)]
    ppermute x1, waiting for transfers between devices: 11.1 us -> 3.48 us  [shards(): lax.ppermute(partial_sum.astype(jnp.bfloat16), 'h', [(0, 1), (1, 0)])]
    unnamed x29 -> x11, local copies, waits for them, and re-layouts: 8.43 us -> 1.75 us
    ppermute x1, starting transfers between devices: 3.15 us -> 5.82 us  [shards(): other_core = lax.ppermute(same_core, 'c', [(0, 1), (1, 0)])]
  transfers between devices with their start and end apart: 11 -> 8, of which waited for: 9 -> 8; matrix products, arithmetic and copies ran while one was open for 5% -> 1% of each run, Pallas kernels for 3% -> 2%
where the time goes in v6:
time: 185 us; the launch traced here: 184 us
  waiting for transfers between devices  62.6 us (34%)
  starting transfers between devices  61.4 us (33%)
  blocking collectives  43.3 us (23%)
  Pallas kernels  7.71 us (4%)
  local copies, waits for them, and re-layouts  3.67 us (2%)
  matrix products  3.51 us (2%)
    all_to_all x3, waiting for transfers between devices, exchanged(): return lax.all_to_all(value, axes, split_axis=0, concat_axis=0, tiled=True)  50.1 us
    all_to_all x3, starting transfers between devices, exchanged(): return lax.all_to_all(value, axes, split_axis=0, concat_axis=0, tiled=True)  44.3 us
    all_to_all x3, blocking collectives, exchanged(): return lax.all_to_all(value, axes, split_axis=0, concat_axis=0, tiled=True)  43.3 us
    ppermute x1, starting transfers between devices, shards(): other_core = lax.ppermute(same_core, 'c', [(0, 1), (1, 0)])  5.82 us
    ppermute x1, waiting for transfers between devices, shards(): high = lax.ppermute(to_lower, EP, backward)  4.58 us
  transfers between devices with their start and end apart: 8, of which 8 were waited for; matrix products, arithmetic and copies ran while one was open for 1% of the time, Pallas kernels for 2%

profile of v6, /device:TPU:1, one launch (start us, length us, event | category | flops | bytes accessed | tf_op | source)
XLA Modules:
  0.0 184.4 jit_solution(1217377363221381624)
XLA Ops:
  0.6 0.0 copy-start
  0.6 1.7 shard_map.113
  2.4 17.6 %all-to-all-start = ((bf16[32,2,128]{2,1,0:T(2,128)(2,1)}), bf16[32,2,128]{2,1,0:T(2,128)(2,1)S(1)}, u32[]{:S(2)}, u32[]{:S(2)}) async-start(bf16[32,2,128]{2,1,0:T(2,128)(2,1)} %shard_map.113), calls=%async_computation | async-start | bytes 32768 | tf_op jit(solution)/shard_map/all_to_all | solution.py:21
  20.0 0.1 eq.40
  20.1 6.9 %all-to-all-done = bf16[32,2,128]{2,1,0:T(2,128)(2,1)S(1)} async-done(((bf16[32,2,128]{2,1,0:T(2,128)(2,1)}), bf16[32,2,128]{2,1,0:T(2,128)(2,1)S(1)}, u32[]{:S(2)}, u32[]{:S(2)}) %all-to-all-start) | async-done | bytes 16416 | tf_op jit(solution)/shard_map/all_to_all | solution.py:21
  27.0 0.1 slice_convert_fusion
  27.1 0.1 fusion.6
  27.2 0.2 fusion.20
  27.4 0.1 copy.40
  27.5 0.3 convolution_convert_fusion
  27.8 0.8 copy.41
  28.5 19.3 %all-to-all-start.1 = ((bf16[32,8,224]{2,1,0:T(8,128)(2,1)}), bf16[32,8,224]{2,1,0:T(8,128)(2,1)S(1)}, u32[]{:S(2)}, u32[]{:S(2)}) async-start(bf16[32,8,224]{2,1,0:T(8,128)(2,1)} %bitcast.4), calls=%async_computation.1 | async-start | bytes 262144 | tf_op jit(solution)/shard_map/all_to_all | solution.py:21
  47.8 2.4 %shard_map.114 = (bf16[2,64,576]{2,1,0:T(8,128)(2,1)}, bf16[2,64,576]{2,1,0:T(8,128)(2,1)}) custom-call(s32[1,4]{1,0:T(1,128)} %moves, bf16[8,64,576]{2,1,0:T(8,128)(2,1)} %pool.1, bf16[8,64,576]{2,1,0:T(8,128)(2,1)} %pool.1), custom_call_target="tpu_custom_call" | custom-call | bytes 589824 | tf_op jit(solution)/shard_map/pallas_call | solution.py:95
  50.2 3.0 %collective-permute-start = (bf16[2,64,576]{2,1,0:T(8,128)(2,1)}, bf16[2,64,576]{2,1,0:T(8,128)(2,1)S(1)}, u32[]{:S(2)}, u32[]{:S(2)}) collective-permute-start(bf16[2,64,576]{2,1,0:T(8,128)(2,1)} %get-tuple-element.18), channel_id=1, source_target_pairs={{0,1},{1,2},{2,3},{3,4},{4,5},{5,6},{6,7},{7,8},{8,9},{9,10},{10,1... | collective-permute-start | bytes 442376 | tf_op jit(solution)/shard_map/ppermute | solution.py:248
  53.3 1.9 %collective-permute-start.1 = (bf16[2,64,576]{2,1,0:T(8,128)(2,1)}, bf16[2,64,576]{2,1,0:T(8,128)(2,1)S(1)}, u32[]{:S(2)}, u32[]{:S(2)}) collective-permute-start(bf16[2,64,576]{2,1,0:T(8,128)(2,1)} %get-tuple-element.19), channel_id=1, source_target_pairs={{1,0},{2,1},{3,2},{4,3},{5,4},{6,5},{7,6},{8,7},{9,8},{10,9},{11,1... | collective-permute-start | bytes 442376 | tf_op jit(solution)/shard_map/ppermute | solution.py:249
  55.2 0.6 collective-permute-done.low
  55.8 4.6 %collective-permute-done.1.high = bf16[2,64,576]{2,1,0:T(8,128)(2,1)S(1)} collective-permute-done((bf16[2,64,576]{2,1,0:T(8,128)(2,1)}, bf16[2,64,576]{2,1,0:T(8,128)(2,1)S(1)}, u32[]{:S(2)}, u32[]{:S(2)}) %collective-permute-start.1) | collective-permute-done | bytes 147488 | tf_op jit(solution)/shard_map/ppermute | solution.py:249
  60.4 17.0 %all-to-all-done.1 = bf16[32,8,224]{2,1,0:T(8,128)(2,1)S(1)} async-done(((bf16[32,8,224]{2,1,0:T(8,128)(2,1)}), bf16[32,8,224]{2,1,0:T(8,128)(2,1)S(1)}, u32[]{:S(2)}, u32[]{:S(2)}) %all-to-all-start.1) | async-done | bytes 114720 | tf_op jit(solution)/shard_map/all_to_all | solution.py:21
  77.4 0.1 copy.42
  77.5 0.1 broadcast_in_dim.24
  77.6 13.7 %all_to_all.34 = bf16[8,256,224]{1,2,0:T(8,128)(2,1)S(1)} all-to-all(bf16[8,256,224]{1,2,0:T(8,128)(2,1)S(1)} %broadcast_in_dim.24), channel_id=1, replica_groups=mesh['z'=32,'h'=2,'y'=2,'x'=4,'c'=2] {'y','x'}, dimensions={0} | all-to-all | bytes 1835008 | tf_op jit(solution)/shard_map/all_to_all | solution.py:21
  91.3 5.8 %collective-permute-start.2 = (bf16[8,256,224]{1,2,0:T(8,128)(2,1)S(1)}, bf16[8,256,224]{1,2,0:T(8,128)(2,1)}, u32[]{:S(2)}, u32[]{:S(2)}) collective-permute-start(bf16[8,256,224]{1,2,0:T(8,128)(2,1)S(1)} %all_to_all.34), channel_id=1, source_target_pairs={{0,1},{1,0},{2,3},{3,2},{4,5},{5,4},{6,7},{7,6},{8,9},{9,8},{10,11... | collective-permute-start | bytes 2752520 | tf_op jit(solution)/shard_map/ppermute | solution.py:252
  97.2 0.0 copy-done
  97.2 0.4 convolution_bitcast_fusion.1
  97.6 1.7 collective-permute-done.2
  99.4 2.3 %fusion.25 = (bf16[256,256]{1,0:T(8,128)(2,1)}, f32[256,256]{1,0:T(8,128)S(1)}) fusion(f32[256,256]{1,0:T(8,128)S(1)} %convolution_bitcast_fusion.1, bf16[8,256,224]{1,2,0:T(8,128)(2,1)} %collective-permute-done.2, bf16[8,2,224,256]{3,2,1,0:T(8,128)(2,1)S(1)} %bitcast.54, s32[]{:T(128)S(6)} %select_n.17), kind=kOutput, calls=%fused_computation.36 | convolution fusion | flops 235012096 | bytes 2490372 | tf_op jit(solution)/shard_map/urk,ukn->rn/dot_general | solution.py:258
  101.7 3.3 %collective-permute-start.3 = (bf16[256,256]{1,0:T(8,128)(2,1)}, bf16[256,256]{1,0:T(8,128)(2,1)S(1)}, u32[]{:S(2)}, u32[]{:S(2)}) collective-permute-start(bf16[256,256]{1,0:T(8,128)(2,1)} %get-tuple-element.30), channel_id=1, source_target_pairs={{0,16},{16,0},{1,17},{17,1},{2,18},{18,2},{3,19},{19,3},{4,20},{20... | collective-permute-start | bytes 393224 | tf_op jit(solution)/shard_map/ppermute | solution.py:259
  104.9 1.6 copy.45
  106.5 3.5 %collective-permute-done.3.partner = bf16[256,256]{1,0:T(8,128)(2,1)S(1)} collective-permute-done((bf16[256,256]{1,0:T(8,128)(2,1)}, bf16[256,256]{1,0:T(8,128)(2,1)S(1)}, u32[]{:S(2)}, u32[]{:S(2)}) %collective-permute-start.3) | collective-permute-done | bytes 131104 | tf_op jit(solution)/shard_map/ppermute | solution.py:259
  110.0 0.4 shard_map.115
  110.4 3.1 %collective-permute-start.4 = (bf16[8,224,256]{2,1,0:T(8,128)(2,1)S(1)}, bf16[8,224,256]{2,1,0:T(8,128)(2,1)S(1)}, u32[]{:S(2)}, u32[]{:S(2)}) collective-permute-start(bf16[8,224,256]{2,1,0:T(8,128)(2,1)S(1)} %get-tuple-element.22), channel_id=1, source_target_pairs={{0,1},{1,0},{2,3},{3,2},{4,5},{5,4},{6,7},{7,6},{8,9},{9,8},{10,11... | collective-permute-start | bytes 2752520 | tf_op jit(solution)/shard_map/ppermute | solution.py:263
  113.5 2.1 %collective-permute-done.4.received = bf16[8,224,256]{2,1,0:T(8,128)(2,1)S(1)} collective-permute-done((bf16[8,224,256]{2,1,0:T(8,128)(2,1)S(1)}, bf16[8,224,256]{2,1,0:T(8,128)(2,1)S(1)}, u32[]{:S(2)}, u32[]{:S(2)}) %collective-permute-start.4) | collective-permute-done | bytes 917536 | tf_op jit(solution)/shard_map/ppermute | solution.py:263
  115.6 0.4 shard_map.116
  116.0 0.0 copy-start.3
  116.0 0.0 copy-start.1
  116.0 0.0 copy-start.2
  116.0 16.7 %all_to_all.35.parts = bf16[8,224,256]{2,1,0:T(8,128)(2,1)S(1)} all-to-all(bf16[8,224,256]{2,1,0:T(8,128)(2,1)S(1)} %shard_map.116), channel_id=1, replica_groups=mesh['z'=32,'h'=2,'y'=2,'x'=4,'c'=2] {'y','x'}, dimensions={0} | all-to-all | bytes 1835008 | tf_op jit(solution)/shard_map/all_to_all | solution.py:21
  132.7 0.8 shard_map.117
  133.5 7.4 %all-to-all-start.4 = ((bf16[32,8,224]{2,1,0:T(8,128)(2,1)}), bf16[32,8,224]{2,1,0:T(8,128)(2,1)S(1)}, u32[]{:S(2)}, u32[]{:S(2)}) async-start(bf16[32,8,224]{2,1,0:T(8,128)(2,1)} %shard_map.117), calls=%async_computation.4 | async-start | bytes 262144 | tf_op jit(solution)/shard_map/all_to_all | solution.py:21
  141.6 0.0 copy-done.3
  141.6 0.2 copy.46.queries
  141.7 0.2 convert_reduce_fusion
  141.9 0.1 fusion.18
  142.0 0.2 select_reduce_fusion
  142.2 0.1 copy.47
  142.2 0.0 copy-done.1
  142.2 0.0 copy-done.2
  142.2 1.9 %shard_map.118 = bf16[1,128,512]{2,1,0:T(8,128)(2,1)} custom-call(s32[1,8]{1,0:T(1,128)S(1)} %copy-done.2, s32[1]{0:T(128)S(6)} %copy.54.lengths, bf16[1,128,576]{2,1,0:T(8,128)(2,1)S(1)} %copy.46.queries, bf16[8,64,576]{2,1,0:T(8,128)(2,1)S(1)} %copy-done.1, bf16[2,64,576]{2,1,0:T(8,128)(2,1)S(1)} %collective-permute-done.low, ...), custom_call_target="tpu_custom_call" | custom-call | flops 142606336 | bytes 884736 | tf_op jit(solution)/shard_map/pallas_call | solution.py:141
  144.2 26.1 %all-to-all-done.4 = bf16[32,8,224]{2,1,0:T(8,128)(2,1)S(1)} async-done(((bf16[32,8,224]{2,1,0:T(8,128)(2,1)}), bf16[32,8,224]{2,1,0:T(8,128)(2,1)S(1)}, u32[]{:S(2)}, u32[]{:S(2)}) %all-to-all-start.4) | async-done | bytes 114720 | tf_op jit(solution)/shard_map/all_to_all | solution.py:21
  170.3 0.3 fusion.1
  170.7 12.9 %all_to_all.36 = bf16[32,1,224]{2,1,0:T(2,128)(2,1)S(1)} all-to-all(bf16[32,1,224]{2,1,0:T(2,128)(2,1)S(1)} %copy.48), channel_id=1, replica_groups=mesh['z'=32,'h'=2,'y'=2,'x'=4,'c'=2] {'h','y','x','c'}, dimensions={0} | all-to-all | bytes 28672 | tf_op jit(solution)/shard_map/all_to_all | solution.py:21
  183.6 0.1 reduce
  183.7 0.7 reshape.54
  (3 shorter events, 0.0 us)
Async XLA Ops:
  0.6 96.6 %copy-start = (bf16[1,1,3584,256]{3,2,1,0:T(8,128)(2,1)S(1)}, bf16[1,1,3584,256]{3,2,1,0:T(8,128)(2,1)}, u32[]{:S(2)}) copy-start(bf16[1,1,3584,256]{3,2,1,0:T(8,128)(2,1)} %param.13) | copy-start | bytes 5505028
  2.4 24.6 %all-to-all-start = ((bf16[32,2,128]{2,1,0:T(2,128)(2,1)}), bf16[32,2,128]{2,1,0:T(2,128)(2,1)S(1)}, u32[]{:S(2)}, u32[]{:S(2)}) async-start(bf16[32,2,128]{2,1,0:T(2,128)(2,1)} %shard_map.113), calls=%async_computation | async-start | bytes 32768 | tf_op jit(solution)/shard_map/all_to_all | solution.py:21
  28.5 48.9 %all-to-all-start.1 = ((bf16[32,8,224]{2,1,0:T(8,128)(2,1)}), bf16[32,8,224]{2,1,0:T(8,128)(2,1)S(1)}, u32[]{:S(2)}, u32[]{:S(2)}) async-start(bf16[32,8,224]{2,1,0:T(8,128)(2,1)} %bitcast.4), calls=%async_computation.1 | async-start | bytes 262144 | tf_op jit(solution)/shard_map/all_to_all | solution.py:21
  50.2 5.6 %collective-permute-start = (bf16[2,64,576]{2,1,0:T(8,128)(2,1)}, bf16[2,64,576]{2,1,0:T(8,128)(2,1)S(1)}, u32[]{:S(2)}, u32[]{:S(2)}) collective-permute-start(bf16[2,64,576]{2,1,0:T(8,128)(2,1)} %get-tuple-element.18), channel_id=1, source_target_pairs={{0,1},{1,2},{2,3},{3,4},{4,5},{5,6},{6,7},{7,8},{8,9},{9,10},{10,1... | collective-permute-start | bytes 442376 | tf_op jit(solution)/shard_map/ppermute | solution.py:248
  53.3 7.1 %collective-permute-start.1 = (bf16[2,64,576]{2,1,0:T(8,128)(2,1)}, bf16[2,64,576]{2,1,0:T(8,128)(2,1)S(1)}, u32[]{:S(2)}, u32[]{:S(2)}) collective-permute-start(bf16[2,64,576]{2,1,0:T(8,128)(2,1)} %get-tuple-element.19), channel_id=1, source_target_pairs={{1,0},{2,1},{3,2},{4,3},{5,4},{6,5},{7,6},{8,7},{9,8},{10,9},{11,1... | collective-permute-start | bytes 442376 | tf_op jit(solution)/shard_map/ppermute | solution.py:249
  91.3 8.0 %collective-permute-start.2 = (bf16[8,256,224]{1,2,0:T(8,128)(2,1)S(1)}, bf16[8,256,224]{1,2,0:T(8,128)(2,1)}, u32[]{:S(2)}, u32[]{:S(2)}) collective-permute-start(bf16[8,256,224]{1,2,0:T(8,128)(2,1)S(1)} %all_to_all.34), channel_id=1, source_target_pairs={{0,1},{1,0},{2,3},{3,2},{4,5},{5,4},{6,7},{7,6},{8,9},{9,8},{10,11... | collective-permute-start | bytes 2752520 | tf_op jit(solution)/shard_map/ppermute | solution.py:252
  101.7 8.3 %collective-permute-start.3 = (bf16[256,256]{1,0:T(8,128)(2,1)}, bf16[256,256]{1,0:T(8,128)(2,1)S(1)}, u32[]{:S(2)}, u32[]{:S(2)}) collective-permute-start(bf16[256,256]{1,0:T(8,128)(2,1)} %get-tuple-element.30), channel_id=1, source_target_pairs={{0,16},{16,0},{1,17},{17,1},{2,18},{18,2},{3,19},{19,3},{4,20},{20... | collective-permute-start | bytes 393224 | tf_op jit(solution)/shard_map/ppermute | solution.py:259
  110.4 5.2 %collective-permute-start.4 = (bf16[8,224,256]{2,1,0:T(8,128)(2,1)S(1)}, bf16[8,224,256]{2,1,0:T(8,128)(2,1)S(1)}, u32[]{:S(2)}, u32[]{:S(2)}) collective-permute-start(bf16[8,224,256]{2,1,0:T(8,128)(2,1)S(1)} %get-tuple-element.22), channel_id=1, source_target_pairs={{0,1},{1,0},{2,3},{3,2},{4,5},{5,4},{6,7},{7,6},{8,9},{9,8},{10,11... | collective-permute-start | bytes 2752520 | tf_op jit(solution)/shard_map/ppermute | solution.py:263
  116.0 25.6 %copy-start.3 = (bf16[1,128,576]{1,2,0:T(8,128)(2,1)S(1)}, bf16[1,128,576]{1,2,0:T(8,128)(2,1)}, u32[]{:S(2)}) copy-start(bf16[1,128,576]{1,2,0:T(8,128)(2,1)} %param.15) | copy-start | bytes 442372
  116.0 26.2 %copy-start.1 = (bf16[8,64,576]{2,1,0:T(8,128)(2,1)S(1)}, bf16[8,64,576]{2,1,0:T(8,128)(2,1)}, u32[]{:S(2)}) copy-start(bf16[8,64,576]{2,1,0:T(8,128)(2,1)} %pool.1) | copy-start | bytes 1769476
  116.0 26.2 %copy-start.2 = (s32[1,8]{1,0:T(1,128)S(1)}, s32[1,8]{1,0:T(1,128)}, u32[]{:S(2)}) copy-start(s32[1,8]{1,0:T(1,128)} %page_list.1) | copy-start | bytes 100
  133.5 36.8 %all-to-all-start.4 = ((bf16[32,8,224]{2,1,0:T(8,128)(2,1)}), bf16[32,8,224]{2,1,0:T(8,128)(2,1)S(1)}, u32[]{:S(2)}, u32[]{:S(2)}) async-start(bf16[32,8,224]{2,1,0:T(8,128)(2,1)} %shard_map.117), calls=%async_computation.4 | async-start | bytes 262144 | tf_op jit(solution)/shard_map/all_to_all | solution.py:21

commit v7 on v6

--- a/solution.py
+++ b/solution.py
@@ -6,11 +6,9 @@
 from jax.sharding import Mesh, PartitionSpec as P
 
 KVL = 512
-SLICE = 224
-WIDE = 256
-HALF = ("y", "x", "c")
-EP = ("h",) + HALF
+EP = ("h", "y", "x", "c")
 MINOR = (((1,), (1,)), ((), ()))
+MAJOR = (((0,), (0,)), ((), ()))
 
 
 softmax_scale = 192.0 ** (-0.5)
@@ -21,62 +19,68 @@
     return lax.all_to_all(value, axes, split_axis=0, concat_axis=0, tiled=True)
 
 
-def given_kernel(core, own, partner, weights, values, given):
-    theirs = 1 - core[0]
-    units = values.shape[1]
-    sums = own[...] + partner[...].astype(jnp.float32)
-    value = jax.nn.silu(sums[:, :units]) * sums[:, units:]
-    values[...] = value.astype(values.dtype)
-    for i in range(weights.shape[0]):
-        given[i] = lax.dot_general(
-            weights[i, theirs], values[...], MINOR, preferred_element_type=jnp.float32
-        ).astype(given.dtype)
-
-
-def given_sums(core, own, partner, weights):
-    rows, columns = own.shape
-    chips, _, width, units = weights.shape
-    return pl.pallas_call(
-        given_kernel,
+def gate_up_kernel(values, own, other, sums, rounded):
+    chips = values.shape[0]
+    for n, weights in enumerate((own, other)):
+        columns = weights.shape[2]
+        total = jnp.zeros((values.shape[2], columns), jnp.float32)
+        for i in range(chips):
+            total += lax.dot_general(
+                values[i], weights[i], MAJOR, preferred_element_type=jnp.float32
+            )
+        sums[:, n * columns : (n + 1) * columns] = total
+        rounded[:, n * columns : (n + 1) * columns] = total.astype(rounded.dtype)
+
+
+def gate_up_sums(values, own, other):
+    chips, width, rows = values.shape
+    columns = 2 * own.shape[2]
+    return pl.pallas_call(
+        gate_up_kernel,
         out_shape=(
-            jax.ShapeDtypeStruct((rows, units), jnp.bfloat16),
-            jax.ShapeDtypeStruct((chips, width, rows), jnp.bfloat16),
-        ),
-        in_specs=[pl.BlockSpec(memory_space=pltpu.SMEM)] + whole(3),
+            jax.ShapeDtypeStruct((rows, columns), jnp.float32),
+            jax.ShapeDtypeStruct((rows, columns), jnp.bfloat16),
+        ),
+        in_specs=whole(3),
         out_specs=tuple(whole(2)),
         compiler_params=pltpu.CompilerParams(vmem_limit_bytes=24 << 20),
         cost_estimate=pl.CostEstimate(
-            flops=2 * chips * rows * width * units,
-            bytes_accessed=2 * weights.size + 6 * own.size + 2 * chips * rows * width,
-            transcendentals=rows * units,
-        ),
-    )(core, own, partner, weights)
-
-
-def kept_kernel(core, values, weights, received, out):
-    mine = core[0]
-    for i in range(weights.shape[0]):
-        sums = lax.dot_general(
-            weights[i, mine], values[...], MINOR, preferred_element_type=jnp.float32
-        )
-        out[i] = (sums + received[i].astype(jnp.float32)).astype(out.dtype)
-
-
-def kept_sums(core, values, weights, received):
-    chips, _, width, units = weights.shape
-    rows = values.shape[0]
-    return pl.pallas_call(
-        kept_kernel,
+            flops=2 * chips * rows * width * columns,
+            bytes_accessed=4 * own.size + 2 * values.size + 6 * rows * columns,
+            transcendentals=0,
+        ),
+    )(values, own, other)
+
+
+def down_kernel(sums, partner, own, other, out):
+    units = own.shape[2]
+    total = sums[...] + partner[...].astype(jnp.float32)
+    values = []
+    for n in range(2):
+        gate = total[:, 2 * n * units : (2 * n + 1) * units]
+        up = total[:, (2 * n + 1) * units : (2 * n + 2) * units]
+        values.append((jax.nn.silu(gate) * up).astype(jnp.bfloat16))
+    for i in range(out.shape[0]):
+        mixed = lax.dot_general(own[i], values[0], MINOR, preferred_element_type=jnp.float32)
+        mixed += lax.dot_general(other[i], values[1], MINOR, preferred_element_type=jnp.float32)
+        out[i] = mixed.astype(out.dtype)
+
+
+def down_sums(sums, partner, own, other):
+    chips, width, units = own.shape
+    rows = sums.shape[0]
+    return pl.pallas_call(
+        down_kernel,
         out_shape=jax.ShapeDtypeStruct((chips, width, rows), jnp.bfloat16),
-        in_specs=[pl.BlockSpec(memory_space=pltpu.SMEM)] + whole(3),
+        in_specs=whole(4),
         out_specs=pl.BlockSpec(memory_space=pltpu.VMEM),
         compiler_params=pltpu.CompilerParams(vmem_limit_bytes=24 << 20),
         cost_estimate=pl.CostEstimate(
-            flops=2 * chips * rows * width * units,
-            bytes_accessed=2 * weights.size + 4 * chips * rows * width,
-            transcendentals=0,
-        ),
-    )(core, values, weights, received)
+            flops=4 * chips * rows * width * units,
+            bytes_accessed=4 * own.size + 6 * sums.size + 2 * chips * rows * width,
+            transcendentals=2 * rows * units,
+        ),
+    )(sums, partner, own, other)
 
 
 def whole(count):
@@ -154,22 +158,26 @@
 
 
 def prepare_kernel(tokens, chosen, affinity, out):
-    members, _, lanes = out.shape
+    chips, lines, lanes = out.shape[0] // 2, out.shape[1], out.shape[2]
     row = tokens[...].astype(jnp.float32)
+    width = row.shape[1] // chips
     choices = chosen.shape[2]
     routing = [chosen[0].astype(jnp.float32), affinity[0].astype(jnp.float32)]
-    routing.append(jnp.zeros((1, 2 * lanes - SLICE - 2 * choices), jnp.float32))
-    for p in range(members):
-        first = row[:, p * SLICE : p * SLICE + lanes]
-        second = [row[:, p * SLICE + lanes : (p + 1) * SLICE]] + routing
-        pair = [first, jnp.concatenate(second, axis=1)]
-        out[p] = jnp.concatenate(pair, axis=0).astype(out.dtype)
+    routing.append(jnp.zeros((1, lines * lanes - width - 2 * choices), jnp.float32))
+    for p in range(chips):
+        start = p * width
+        block = [row[:, start + n * lanes : start + (n + 1) * lanes] for n in range(lines - 1)]
+        last = [row[:, start + (lines - 1) * lanes : start + width]] + routing
+        block.append(jnp.concatenate(last, axis=1))
+        block = jnp.concatenate(block, axis=0).astype(out.dtype)
+        out[2 * p] = block
+        out[2 * p + 1] = block
 
 
 def prepared(tokens, expert_ids, affinity, members):
     return pl.pallas_call(
         prepare_kernel,
-        out_shape=jax.ShapeDtypeStruct((members, 2, WIDE // 2), jnp.bfloat16),
+        out_shape=jax.ShapeDtypeStruct((members, 4, 128), jnp.bfloat16),
         in_specs=whole(3),
         out_specs=pl.BlockSpec(memory_space=pltpu.VMEM),
         cost_estimate=pl.CostEstimate(
@@ -213,17 +221,22 @@
 ):
     members = lax.axis_size(EP)
     groups = lax.axis_size("z")
-    chips = lax.axis_size(HALF) // 2
+    chips = members // 4
     choices = expert_ids.shape[2]
-    capacity = members * choices // groups
-    rows = groups * capacity
+    slots = members * choices // groups // 2
+    rows = groups * slots
     units = gate_up_blocks.shape[3] // 2
-    core = lax.axis_index("c")
+    width = 2 * tokens.shape[1] // members
+    between_cores = [(0, 1), (1, 0)]
     held = exchanged(prepared(tokens, expert_ids, affinity, members), EP)
-    held, page_moves = lax.optimization_barrier((held, page_moves))
-    held = held.reshape(members, WIDE)
-    chosen = held[:, SLICE : SLICE + choices].astype(jnp.float32)
-    affinity_all = held[:, SLICE + choices : SLICE + 2 * choices].astype(jnp.float32)
+    gate_up = gate_up_blocks.reshape(chips, width, 2 * units)
+    other_gate_up = lax.ppermute(gate_up, "c", between_cores)
+    held, page_moves, other_gate_up, down_blocks = lax.optimization_barrier(
+        (held, page_moves, other_gate_up, down_blocks)
+    )
+    held = held.reshape(members, -1)
+    chosen = held[:, width : width + choices].astype(jnp.float32)
+    affinity_all = held[:, width + choices : width + 2 * choices].astype(jnp.float32)
     route_weights = routed_scale * affinity_all / jnp.sum(affinity_all, axis=1, keepdims=True)
     matches = chosen[:, :, None] == jnp.arange(groups, dtype=jnp.float32)[None, None, :]
     member = jnp.any(matches, axis=1)
@@ -234,43 +247,38 @@
         member.astype(jnp.bfloat16),
         preferred_element_type=jnp.float32,
     )
-    slot_number = jnp.arange(capacity, dtype=jnp.float32)
+    slot_number = (jnp.arange(slots) + lax.axis_index("c") * slots).astype(jnp.float32)
     selector = member.T[:, None, :] & (position.T[:, None, :] == slot_number[None, :, None])
     sent_rows = jnp.dot(
         selector.astype(jnp.bfloat16).reshape(rows, members),
-        held[:, :SLICE],
+        held[:, :width],
         preferred_element_type=jnp.float32,
     ).astype(jnp.bfloat16)
-    arrived = exchanged(sent_rows.reshape(groups, capacity, SLICE), "z").reshape(rows, SLICE)
+    arrived = exchanged(sent_rows.reshape(groups, slots, width), "z").reshape(rows, width)
     to_lower, to_higher = departing_pages(latent_pool, page_moves)
     forward = [(i, (i + 1) % members) for i in range(members)]
     backward = [(target, source) for source, target in forward]
     low = lax.ppermute(to_higher, EP, forward)
     high = lax.ppermute(to_lower, EP, backward)
-    arrived, low, high = lax.optimization_barrier((arrived, low, high))
-    same_core = exchanged(jnp.broadcast_to(arrived[None], (chips, rows, SLICE)), ("y", "x"))
-    other_core = lax.ppermute(same_core, "c", [(0, 1), (1, 0)])
-    by_core = gate_up_blocks.reshape(chips, 2, SLICE, 2 * units)
-    same_weights = lax.dynamic_index_in_dim(by_core, core, 1, keepdims=False)
-    other_weights = lax.dynamic_index_in_dim(by_core, 1 - core, 1, keepdims=False)
-    partial_sum = jnp.einsum(
-        "urk,ukn->rn", same_core, same_weights, preferred_element_type=jnp.float32
-    ) + jnp.einsum("urk,ukn->rn", other_core, other_weights, preferred_element_type=jnp.float32)
-    partner_sum = lax.ppermute(partial_sum.astype(jnp.bfloat16), "h", [(0, 1), (1, 0)])
-    down = down_blocks.reshape(units, chips, 2, SLICE).transpose(1, 2, 3, 0)
-    core = core.reshape(1).astype(jnp.int32)
-    values, given = given_sums(core, partial_sum, partner_sum, down)
-    received = lax.ppermute(given, "c", [(0, 1), (1, 0)])
-    summed = added(exchanged(kept_sums(core, values, down, received), ("y", "x")), groups)
+    down = down_blocks.reshape(units, chips, width).transpose(1, 2, 0)
+    arrived, low, high, down = lax.optimization_barrier((arrived, low, high, down))
+    gathered = exchanged(jnp.broadcast_to(arrived.T[None], (chips, width, rows)), ("y", "x"))
+    sums, rounded = gate_up_sums(gathered, gate_up, other_gate_up)
+    rounded, down = lax.optimization_barrier((rounded, down))
+    partner = lax.ppermute(rounded, "h", [(0, 1), (1, 0)])
+    other_down = lax.ppermute(down, "c", between_cores)
+    block_sums = down_sums(sums, partner, down, other_down)
+    summed = added(exchanged(block_sums, ("y", "x")), groups)
     summed, low, high = lax.optimization_barrier((summed, low, high))
     attention_latent = attention(queries, latent_pool, low, high, page_list, lengths)
-    returned = exchanged(summed, "z").reshape(rows, SLICE)
+    returned = exchanged(summed, "z").reshape(rows, width)
     returned, attention_latent = lax.optimization_barrier((returned, attention_latent))
     weighted = jnp.where(selector, weight_of.T[:, None, :], 0.0).reshape(rows, members)
     mixed = jnp.einsum(
         "rn,rk->nk", weighted, returned.astype(jnp.float32), precision=lax.Precision.HIGHEST
     )
-    expert_mix = exchanged(mixed.astype(jnp.bfloat16), EP).reshape(1, -1)
+    halves = exchanged(mixed.astype(jnp.bfloat16), EP).reshape(members // 2, 2, width)
+    expert_mix = jnp.sum(halves.astype(jnp.float32), axis=1).astype(jnp.bfloat16).reshape(1, -1)
     return (attention_latent, expert_mix)
 
 

time: 185 us -> 181 us (0.978)
  waiting for transfers between devices: 62.6 us -> 59.7 us
  matrix products: 3.51 us -> 0.65 us
    all_to_all x3, starting transfers between devices: 44.3 us -> 29.8 us  [exchanged(): return lax.all_to_all(value, axes, split_axis=0, concat_axis=0, tiled=True)]
    ppermute x3, starting transfers between devices: 12.2 us -> 25.3 us  [the longest x1 16.2 us: shards(): other_gate_up = lax.ppermute(gate_up, 'c', between_cores)]
    ppermute x1, waiting for transfers between devices: 4.58 us -> 0.01 us  [shards(): high = lax.ppermute(to_lower, EP, backward)]
    all_to_all x3, waiting for transfers between devices: 50.1 us -> 54.5 us  [exchanged(): return lax.all_to_all(value, axes, split_axis=0, concat_axis=0, tiled=True)]
    dot_general x3 -> x1, matrix products: 3.01 us -> 0.24 us  [shards(): jnp.dot(selector.astype(jnp.bfloat16).reshape(rows, members), held[:, :wi...]
    ppermute x3, waiting for transfers between devices: 7.3 us -> 5.24 us  [the longest x1 5.23 us: shards(): partner = lax.ppermute(rounded, 'h', [(0, 1), (1, 0)])]
  transfers between devices with their start and end apart: 8 -> 8, of which waited for: 8 -> 4; matrix products, arithmetic and copies ran while one was open for 1% -> 1% of each run, Pallas kernels for 2% -> 3%
where the time goes in v7:
time: 181 us
  starting transfers between devices  59.8 us (33%)
  waiting for transfers between devices  59.7 us (33%)
  blocking collectives  43.8 us (24%)
  Pallas kernels  8.15 us (5%)
  local copies, waits for them, and re-layouts  5.26 us (3%)
    all_to_all x3, waiting for transfers between devices, exchanged(): return lax.all_to_all(value, axes, split_axis=0, concat_axis=0, tiled=True)  54.5 us
    all_to_all x3, blocking collectives, exchanged(): return lax.all_to_all(value, axes, split_axis=0, concat_axis=0, tiled=True)  43.8 us
    all_to_all x3, starting transfers between devices, exchanged(): return lax.all_to_all(value, axes, split_axis=0, concat_axis=0, tiled=True)  29.8 us
    ppermute x1, starting transfers between devices, shards(): other_gate_up = lax.ppermute(gate_up, 'c', between_cores)  16.2 us
    ppermute x1, starting transfers between devices, shards(): other_down = lax.ppermute(down, 'c', between_cores)  5.8 us
    ppermute x1, waiting for transfers between devices, shards(): partner = lax.ppermute(rounded, 'h', [(0, 1), (1, 0)])  5.23 us
  transfers between devices with their start and end apart: 8, of which 4 were waited for; matrix products, arithmetic and copies ran while one was open for 1% of the time, Pallas kernels for 3%

profile of v7, /device:TPU:1, one launch (start us, length us, event | category | flops | bytes accessed | tf_op | source)
XLA Modules:
  0.0 180.6 jit_solution(12662234421916640338)
XLA Ops:
  0.6 0.0 copy-start.5
  0.6 16.2 %collective-permute-start = (bf16[8,448,256]{2,1,0:T(8,128)(2,1)}, bf16[8,448,256]{2,1,0:T(8,128)(2,1)S(1)}, u32[]{:S(2)}, u32[]{:S(2)}) collective-permute-start(bf16[8,448,256]{2,1,0:T(8,128)(2,1)} %bitcast.20), channel_id=1, source_target_pairs={{0,1},{1,0},{2,3},{3,2},{4,5},{5,4},{6,7},{7,6},{8,9},{9,8},{10,11... | collective-permute-start | bytes 5505032 | tf_op jit(solution)/shard_map/ppermute | solution.py:233
  16.8 1.6 shard_map.113
  18.4 3.6 %all-to-all-start = ((bf16[32,4,128]{2,1,0:T(4,128)(2,1)}), bf16[32,4,128]{2,1,0:T(4,128)(2,1)S(1)}, u32[]{:S(2)}, u32[]{:S(2)}) async-start(bf16[32,4,128]{2,1,0:T(4,128)(2,1)} %shard_map.113), calls=%async_computation | async-start | bytes 65536 | tf_op jit(solution)/shard_map/all_to_all | solution.py:19
  22.1 0.1 eq.40
  22.2 7.1 %all-to-all-done = bf16[32,4,128]{2,1,0:T(4,128)(2,1)S(1)} async-done(((bf16[32,4,128]{2,1,0:T(4,128)(2,1)}), bf16[32,4,128]{2,1,0:T(4,128)(2,1)S(1)}, u32[]{:S(2)}, u32[]{:S(2)}) %all-to-all-start) | async-done | bytes 32800 | tf_op jit(solution)/shard_map/all_to_all | solution.py:19
  29.3 0.0 collective-permute-done.other
  29.3 0.1 slice_convert_fusion
  29.4 0.1 fusion.1
  29.6 0.2 fusion.6
  29.7 0.1 copy.32
  29.9 0.1 compare_and_fusion
  30.0 0.2 convolution_convert_fusion
  30.2 0.1 copy.33
  30.3 0.7 reshape.54
  31.0 19.4 %all-to-all-start.1 = ((bf16[32,4,448]{2,1,0:T(4,128)(2,1)}), bf16[32,4,448]{2,1,0:T(4,128)(2,1)S(1)}, u32[]{:S(2)}, u32[]{:S(2)}) async-start(bf16[32,4,448]{2,1,0:T(4,128)(2,1)} %reshape.54), calls=%async_computation.1 | async-start | bytes 262144 | tf_op jit(solution)/shard_map/all_to_all | solution.py:19
  50.4 2.4 %shard_map.114 = (bf16[2,64,576]{2,1,0:T(8,128)(2,1)}, bf16[2,64,576]{2,1,0:T(8,128)(2,1)}) custom-call(s32[1,4]{1,0:T(1,128)} %moves, bf16[8,64,576]{2,1,0:T(8,128)(2,1)} %pool.1, bf16[8,64,576]{2,1,0:T(8,128)(2,1)} %pool.1), custom_call_target="tpu_custom_call" | custom-call | bytes 589824 | tf_op jit(solution)/shard_map/pallas_call | solution.py:99
  52.8 2.8 %collective-permute-start.1 = (bf16[2,64,576]{2,1,0:T(8,128)(2,1)}, bf16[2,64,576]{2,1,0:T(8,128)(2,1)S(1)}, u32[]{:S(2)}, u32[]{:S(2)}) collective-permute-start(bf16[2,64,576]{2,1,0:T(8,128)(2,1)} %get-tuple-element.23), channel_id=1, source_target_pairs={{0,1},{1,2},{2,3},{3,4},{4,5},{5,6},{6,7},{7,8},{8,9},{9,10},{10,1... | collective-permute-start | bytes 442376 | tf_op jit(solution)/shard_map/ppermute | solution.py:261
  55.6 0.0 copy-done.2
  55.6 1.9 %collective-permute-start.2 = (bf16[2,64,576]{2,1,0:T(8,128)(2,1)}, bf16[2,64,576]{2,1,0:T(8,128)(2,1)S(1)}, u32[]{:S(2)}, u32[]{:S(2)}) collective-permute-start(bf16[2,64,576]{2,1,0:T(8,128)(2,1)} %get-tuple-element.24), channel_id=1, source_target_pairs={{1,0},{2,1},{3,2},{4,3},{5,4},{6,5},{7,6},{8,7},{9,8},{10,9},{11,1... | collective-permute-start | bytes 442376 | tf_op jit(solution)/shard_map/ppermute | solution.py:262
  57.5 0.0 copy-done.5
  57.5 0.6 copy.34
  58.1 0.0 copy-start.1
  58.2 22.1 %all-to-all-done.1 = bf16[32,4,448]{2,1,0:T(4,128)(2,1)S(1)} async-done(((bf16[32,4,448]{2,1,0:T(4,128)(2,1)}), bf16[32,4,448]{2,1,0:T(4,128)(2,1)S(1)}, u32[]{:S(2)}, u32[]{:S(2)}) %all-to-all-start.1) | async-done | bytes 114720 | tf_op jit(solution)/shard_map/all_to_all | solution.py:19
  80.2 0.1 reshape.55
  80.3 0.0 collective-permute-done.1.low
  80.3 0.0 collective-permute-done.2.high
  80.3 0.1 copy.35
  80.4 0.1 broadcast_in_dim.24
  80.6 13.8 %all_to_all.34.values = bf16[8,448,128]{2,1,0:T(8,128)(2,1)S(1)} all-to-all(bf16[8,448,128]{2,1,0:T(8,128)(2,1)S(1)} %broadcast_in_dim.24), channel_id=1, replica_groups=mesh['z'=32,'h'=2,'y'=2,'x'=4,'c'=2] {'y','x'}, dimensions={0} | all-to-all | bytes 1835008 | tf_op jit(solution)/shard_map/all_to_all | solution.py:19
  94.3 0.0 copy-done.1
  94.3 1.5 copy-done.3
  95.8 0.8 shard_map.115
  96.6 5.8 %collective-permute-start.4 = (bf16[8,448,128]{2,1,0:T(8,128)(2,1)S(1)}, bf16[8,448,128]{2,1,0:T(8,128)(2,1)S(1)}, u32[]{:S(2)}, u32[]{:S(2)}) collective-permute-start(bf16[8,448,128]{2,1,0:T(8,128)(2,1)S(1)} %bitcast.18), channel_id=1, source_target_pairs={{0,1},{1,0},{2,3},{3,2},{4,5},{5,4},{6,7},{7,6},{8,9},{9,8},{10,11... | collective-permute-start | bytes 2752520 | tf_op jit(solution)/shard_map/ppermute | solution.py:269
  102.4 3.3 %collective-permute-start.3 = (bf16[128,512]{1,0:T(8,128)(2,1)S(1)}, bf16[128,512]{1,0:T(8,128)(2,1)S(1)}, u32[]{:S(2)}, u32[]{:S(2)}) collective-permute-start(bf16[128,512]{1,0:T(8,128)(2,1)S(1)} %get-tuple-element.31), channel_id=1, source_target_pairs={{0,16},{16,0},{1,17},{17,1},{2,18},{18,2},{3,19},{19,3},{4,20},{20... | collective-permute-start | bytes 393224 | tf_op jit(solution)/shard_map/ppermute | solution.py:268
  105.7 5.2 %collective-permute-done.3.partner = bf16[128,512]{1,0:T(8,128)(2,1)S(1)} collective-permute-done((bf16[128,512]{1,0:T(8,128)(2,1)S(1)}, bf16[128,512]{1,0:T(8,128)(2,1)S(1)}, u32[]{:S(2)}, u32[]{:S(2)}) %collective-permute-start.3) | collective-permute-done | bytes 131104 | tf_op jit(solution)/shard_map/ppermute | solution.py:268
  110.9 0.0 collective-permute-done.4.other
  110.9 0.6 shard_map.116
  111.6 0.0 copy-start.6
  111.6 0.0 copy-start
  111.6 0.0 copy-start.4
  111.6 16.3 %all_to_all.35.parts = bf16[8,448,128]{2,1,0:T(8,128)(2,1)S(1)} all-to-all(bf16[8,448,128]{2,1,0:T(8,128)(2,1)S(1)} %shard_map.116), channel_id=1, replica_groups=mesh['z'=32,'h'=2,'y'=2,'x'=4,'c'=2] {'y','x'}, dimensions={0} | all-to-all | bytes 1835008 | tf_op jit(solution)/shard_map/all_to_all | solution.py:19
  127.9 0.8 shard_map.117
  128.7 6.8 %all-to-all-start.4 = ((bf16[32,4,448]{2,1,0:T(4,128)(2,1)}), bf16[32,4,448]{2,1,0:T(4,128)(2,1)S(1)}, u32[]{:S(2)}, u32[]{:S(2)}) async-start(bf16[32,4,448]{2,1,0:T(4,128)(2,1)} %shard_map.117), calls=%async_computation.4 | async-start | bytes 262144 | tf_op jit(solution)/shard_map/all_to_all | solution.py:19
  135.6 0.0 copy-done.6
  135.6 0.2 copy.36.queries
  136.4 0.2 convert_reduce_fusion
  136.6 0.1 fusion.5
  136.7 0.2 select_reduce_fusion
  136.8 0.1 copy.37
  136.9 0.0 copy-done
  136.9 0.0 copy-done.4
  136.9 1.9 %shard_map.118 = bf16[1,128,512]{2,1,0:T(8,128)(2,1)} custom-call(s32[1,8]{1,0:T(1,128)S(1)} %copy-done.4, s32[1]{0:T(128)S(6)} %copy.47.lengths, bf16[1,128,576]{2,1,0:T(8,128)(2,1)S(1)} %copy.36.queries, bf16[8,64,576]{2,1,0:T(8,128)(2,1)S(1)} %copy-done, bf16[2,64,576]{2,1,0:T(8,128)(2,1)S(1)} %collective-permute-done.1.low, ...), custom_call_target="tpu_custom_call" | custom-call | flops 142606336 | bytes 884736 | tf_op jit(solution)/shard_map/pallas_call | solution.py:145
  138.8 25.3 %all-to-all-done.4 = bf16[32,4,448]{2,1,0:T(4,128)(2,1)S(1)} async-done(((bf16[32,4,448]{2,1,0:T(4,128)(2,1)}), bf16[32,4,448]{2,1,0:T(4,128)(2,1)S(1)}, u32[]{:S(2)}, u32[]{:S(2)}) %all-to-all-start.4) | async-done | bytes 114720 | tf_op jit(solution)/shard_map/all_to_all | solution.py:19
  164.1 0.1 reshape.57
  164.2 0.2 fusion
  164.4 0.5 broadcast.22
  164.9 0.7 reduce.2
  165.6 0.1 reshape.61
  165.7 13.8 %all_to_all.36 = bf16[32,2,224]{2,1,0:T(2,128)(2,1)S(1)} all-to-all(bf16[32,2,224]{2,1,0:T(2,128)(2,1)S(1)} %reshape.61), channel_id=1, replica_groups=mesh['z'=32,'h'=2,'y'=2,'x'=4,'c'=2] {'h','y','x','c'}, dimensions={0} | all-to-all | bytes 57344 | tf_op jit(solution)/shard_map/all_to_all | solution.py:19
  179.5 0.1 reshape.62
  179.6 0.2 reduce.1
  179.8 0.1 reduce_sum.32
  179.9 0.7 reshape.59
  (9 shorter events, 0.1 us)
Async XLA Ops:
  0.6 56.9 %copy-start.5 = (bf16[1,1,128,3584]{3,2,1,0:T(8,128)(2,1)S(1)}, bf16[1,1,128,3584]{3,2,1,0:T(8,128)(2,1)}, u32[]{:S(2)}) copy-start(bf16[1,1,128,3584]{3,2,1,0:T(8,128)(2,1)} %param.14) | copy-start | bytes 2752516
  0.6 28.7 %collective-permute-start = (bf16[8,448,256]{2,1,0:T(8,128)(2,1)}, bf16[8,448,256]{2,1,0:T(8,128)(2,1)S(1)}, u32[]{:S(2)}, u32[]{:S(2)}) collective-permute-start(bf16[8,448,256]{2,1,0:T(8,128)(2,1)} %bitcast.20), channel_id=1, source_target_pairs={{0,1},{1,0},{2,3},{3,2},{4,5},{5,4},{6,7},{7,6},{8,9},{9,8},{10,11... | collective-permute-start | bytes 5505032 | tf_op jit(solution)/shard_map/ppermute | solution.py:233
  18.4 10.9 %all-to-all-start = ((bf16[32,4,128]{2,1,0:T(4,128)(2,1)}), bf16[32,4,128]{2,1,0:T(4,128)(2,1)S(1)}, u32[]{:S(2)}, u32[]{:S(2)}) async-start(bf16[32,4,128]{2,1,0:T(4,128)(2,1)} %shard_map.113), calls=%async_computation | async-start | bytes 65536 | tf_op jit(solution)/shard_map/all_to_all | solution.py:19
  29.3 26.2 %copy-start.2 = (bf16[8,448,256]{2,1,0:T(8,128)(2,1)}, bf16[8,448,256]{2,1,0:T(8,128)(2,1)S(1)}, u32[]{:S(2)}) copy-start(bf16[8,448,256]{2,1,0:T(8,128)(2,1)S(1)} %collective-permute-done.other) | copy-start | bytes 5505028
  31.0 49.2 %all-to-all-start.1 = ((bf16[32,4,448]{2,1,0:T(4,128)(2,1)}), bf16[32,4,448]{2,1,0:T(4,128)(2,1)S(1)}, u32[]{:S(2)}, u32[]{:S(2)}) async-start(bf16[32,4,448]{2,1,0:T(4,128)(2,1)} %reshape.54), calls=%async_computation.1 | async-start | bytes 262144 | tf_op jit(solution)/shard_map/all_to_all | solution.py:19
  52.8 27.5 %collective-permute-start.1 = (bf16[2,64,576]{2,1,0:T(8,128)(2,1)}, bf16[2,64,576]{2,1,0:T(8,128)(2,1)S(1)}, u32[]{:S(2)}, u32[]{:S(2)}) collective-permute-start(bf16[2,64,576]{2,1,0:T(8,128)(2,1)} %get-tuple-element.23), channel_id=1, source_target_pairs={{0,1},{1,2},{2,3},{3,4},{4,5},{5,6},{6,7},{7,8},{8,9},{9,10},{10,1... | collective-permute-start | bytes 442376 | tf_op jit(solution)/shard_map/ppermute | solution.py:261
  55.6 24.7 %collective-permute-start.2 = (bf16[2,64,576]{2,1,0:T(8,128)(2,1)}, bf16[2,64,576]{2,1,0:T(8,128)(2,1)S(1)}, u32[]{:S(2)}, u32[]{:S(2)}) collective-permute-start(bf16[2,64,576]{2,1,0:T(8,128)(2,1)} %get-tuple-element.24), channel_id=1, source_target_pairs={{1,0},{2,1},{3,2},{4,3},{5,4},{6,5},{7,6},{8,7},{9,8},{10,9},{11,1... | collective-permute-start | bytes 442376 | tf_op jit(solution)/shard_map/ppermute | solution.py:262
  58.1 36.2 %copy-start.1 = (bf16[1,1,3584,256]{3,2,1,0:T(8,128)(2,1)S(1)}, bf16[1,1,3584,256]{3,2,1,0:T(8,128)(2,1)}, u32[]{:S(2)}) copy-start(bf16[1,1,3584,256]{3,2,1,0:T(8,128)(2,1)} %param.13) | copy-start | bytes 5505028
  94.3 1.5 copy-start.3
  96.6 14.3 %collective-permute-start.4 = (bf16[8,448,128]{2,1,0:T(8,128)(2,1)S(1)}, bf16[8,448,128]{2,1,0:T(8,128)(2,1)S(1)}, u32[]{:S(2)}, u32[]{:S(2)}) collective-permute-start(bf16[8,448,128]{2,1,0:T(8,128)(2,1)S(1)} %bitcast.18), channel_id=1, source_target_pairs={{0,1},{1,0},{2,3},{3,2},{4,5},{5,4},{6,7},{7,6},{8,9},{9,8},{10,11... | collective-permute-start | bytes 2752520 | tf_op jit(solution)/shard_map/ppermute | solution.py:269
  102.4 8.5 %collective-permute-start.3 = (bf16[128,512]{1,0:T(8,128)(2,1)S(1)}, bf16[128,512]{1,0:T(8,128)(2,1)S(1)}, u32[]{:S(2)}, u32[]{:S(2)}) collective-permute-start(bf16[128,512]{1,0:T(8,128)(2,1)S(1)} %get-tuple-element.31), channel_id=1, source_target_pairs={{0,16},{16,0},{1,17},{17,1},{2,18},{18,2},{3,19},{19,3},{4,20},{20... | collective-permute-start | bytes 393224 | tf_op jit(solution)/shard_map/ppermute | solution.py:268
  111.6 24.0 %copy-start.6 = (bf16[1,128,576]{1,2,0:T(8,128)(2,1)S(1)}, bf16[1,128,576]{1,2,0:T(8,128)(2,1)}, u32[]{:S(2)}) copy-start(bf16[1,128,576]{1,2,0:T(8,128)(2,1)} %param.15) | copy-start | bytes 442372
  111.6 25.3 %copy-start = (bf16[8,64,576]{2,1,0:T(8,128)(2,1)S(1)}, bf16[8,64,576]{2,1,0:T(8,128)(2,1)}, u32[]{:S(2)}) copy-start(bf16[8,64,576]{2,1,0:T(8,128)(2,1)} %pool.1) | copy-start | bytes 1769476
  111.6 25.3 %copy-start.4 = (s32[1,8]{1,0:T(1,128)S(1)}, s32[1,8]{1,0:T(1,128)}, u32[]{:S(2)}) copy-start(s32[1,8]{1,0:T(1,128)} %page_list.1) | copy-start | bytes 100
  128.7 35.4 %all-to-all-start.4 = ((bf16[32,4,448]{2,1,0:T(4,128)(2,1)}), bf16[32,4,448]{2,1,0:T(4,128)(2,1)S(1)}, u32[]{:S(2)}, u32[]{:S(2)}) async-start(bf16[32,4,448]{2,1,0:T(4,128)(2,1)} %shard_map.117), calls=%async_computation.4 | async-start | bytes 262144 | tf_op jit(solution)/shard_map/all_to_all | solution.py:19

commit v8 on v7

--- a/solution.py
+++ b/solution.py
@@ -231,8 +231,9 @@
     held = exchanged(prepared(tokens, expert_ids, affinity, members), EP)
     gate_up = gate_up_blocks.reshape(chips, width, 2 * units)
     other_gate_up = lax.ppermute(gate_up, "c", between_cores)
-    held, page_moves, other_gate_up, down_blocks = lax.optimization_barrier(
-        (held, page_moves, other_gate_up, down_blocks)
+    other_down = lax.ppermute(down_blocks, "c", between_cores)
+    held, page_moves, other_gate_up, down_blocks, other_down = lax.optimization_barrier(
+        (held, page_moves, other_gate_up, down_blocks, other_down)
     )
     held = held.reshape(members, -1)
     chosen = held[:, width : width + choices].astype(jnp.float32)
@@ -261,12 +262,13 @@
     low = lax.ppermute(to_higher, EP, forward)
     high = lax.ppermute(to_lower, EP, backward)
     down = down_blocks.reshape(units, chips, width).transpose(1, 2, 0)
-    arrived, low, high, down = lax.optimization_barrier((arrived, low, high, down))
+    other_down = other_down.reshape(units, chips, width).transpose(1, 2, 0)
+    arrived, low, high, down, other_down = lax.optimization_barrier(
+        (arrived, low, high, down, other_down)
+    )
     gathered = exchanged(jnp.broadcast_to(arrived.T[None], (chips, width, rows)), ("y", "x"))
     sums, rounded = gate_up_sums(gathered, gate_up, other_gate_up)
-    rounded, down = lax.optimization_barrier((rounded, down))
     partner = lax.ppermute(rounded, "h", [(0, 1), (1, 0)])
-    other_down = lax.ppermute(down, "c", between_cores)
     block_sums = down_sums(sums, partner, down, other_down)
     summed = added(exchanged(block_sums, ("y", "x")), groups)
     summed, low, high = lax.optimization_barrier((summed, low, high))
@@ -277,7 +279,8 @@
     mixed = jnp.einsum(
         "rn,rk->nk", weighted, returned.astype(jnp.float32), precision=lax.Precision.HIGHEST
     )
-    halves = exchanged(mixed.astype(jnp.bfloat16), EP).reshape(members // 2, 2, width)
+    mixed = mixed.astype(jnp.bfloat16).reshape(members, 2, width // 2)
+    halves = exchanged(mixed, EP).reshape(members // 2, 2, width)
     expert_mix = jnp.sum(halves.astype(jnp.float32), axis=1).astype(jnp.bfloat16).reshape(1, -1)
     return (attention_latent, expert_mix)
 

time: 181 us -> 179 us (0.989)
  waiting for transfers between devices: 59.7 us -> 54.7 us
  starting transfers between devices: 59.8 us -> 62.2 us
    all_to_all x3, starting transfers between devices: 29.8 us -> 36.2 us  [exchanged(): return lax.all_to_all(value, axes, split_axis=0, concat_axis=0, tiled=True)]
    ppermute x1, starting transfers between devices: 5.8 us -> 1.92 us  [shards(): other_down = lax.ppermute(down_blocks, 'c', between_cores)]
    all_to_all x3, waiting for transfers between devices: 54.5 us -> 50.7 us  [exchanged(): return lax.all_to_all(value, axes, split_axis=0, concat_axis=0, tiled=True)]
  transfers between devices with their start and end apart: 8 -> 8, of which waited for: 4 -> 4; matrix products, arithmetic and copies ran while one was open for 1% -> 2% of each run, Pallas kernels for 3% -> 3%
where the time goes in v8:
time: 179 us
  starting transfers between devices  62.2 us (35%)
  waiting for transfers between devices  54.7 us (31%)
  blocking collectives  44.3 us (25%)
  Pallas kernels  8.16 us (5%)
  local copies, waits for them, and re-layouts  6.27 us (4%)
    all_to_all x3, waiting for transfers between devices, exchanged(): return lax.all_to_all(value, axes, split_axis=0, concat_axis=0, tiled=True)  50.7 us
    all_to_all x3, blocking collectives, exchanged(): return lax.all_to_all(value, axes, split_axis=0, concat_axis=0, tiled=True)  44.3 us
    all_to_all x3, starting transfers between devices, exchanged(): return lax.all_to_all(value, axes, split_axis=0, concat_axis=0, tiled=True)  36.2 us
    ppermute x1, starting transfers between devices, shards(): other_gate_up = lax.ppermute(gate_up, 'c', between_cores)  16.2 us
    ppermute x1, waiting for transfers between devices, shards(): partner = lax.ppermute(rounded, 'h', [(0, 1), (1, 0)])  3.99 us
  transfers between devices with their start and end apart: 8, of which 4 were waited for; matrix products, arithmetic and copies ran while one was open for 2% of the time, Pallas kernels for 3%

profile of v8, /device:TPU:1, one launch (start us, length us, event | category | flops | bytes accessed | tf_op | source)
XLA Modules:
  0.0 178.6 jit_solution(507380543630738989)
XLA Ops:
  0.6 0.0 copy-start.5
  0.6 16.2 %collective-permute-start = (bf16[8,448,256]{2,1,0:T(8,128)(2,1)}, bf16[8,448,256]{2,1,0:T(8,128)(2,1)S(1)}, u32[]{:S(2)}, u32[]{:S(2)}) collective-permute-start(bf16[8,448,256]{2,1,0:T(8,128)(2,1)} %bitcast.21), channel_id=1, source_target_pairs={{0,1},{1,0},{2,3},{3,2},{4,5},{5,4},{6,7},{7,6},{8,9},{9,8},{10,11... | collective-permute-start | bytes 5505032 | tf_op jit(solution)/shard_map/ppermute | solution.py:233
  16.8 1.9 %collective-permute-start.1 = (bf16[1,1,128,3584]{3,2,1,0:T(8,128)(2,1)}, bf16[1,1,128,3584]{3,2,1,0:T(8,128)(2,1)}, u32[]{:S(2)}, u32[]{:S(2)}) collective-permute-start(bf16[1,1,128,3584]{3,2,1,0:T(8,128)(2,1)} %param.14), channel_id=1, source_target_pairs={{0,1},{1,0},{2,3},{3,2},{4,5},{5,4},{6,7},{7,6},{8,9},{9,8},{10,11... | collective-permute-start | bytes 2752520 | tf_op jit(solution)/shard_map/ppermute | solution.py:234
  18.8 1.6 shard_map.113
  20.4 4.0 %all-to-all-start = ((bf16[32,4,128]{2,1,0:T(4,128)(2,1)}), bf16[32,4,128]{2,1,0:T(4,128)(2,1)S(1)}, u32[]{:S(2)}, u32[]{:S(2)}) async-start(bf16[32,4,128]{2,1,0:T(4,128)(2,1)} %shard_map.113), calls=%async_computation | async-start | bytes 65536 | tf_op jit(solution)/shard_map/all_to_all | solution.py:19
  24.4 0.1 eq.40
  24.5 7.2 %all-to-all-done = bf16[32,4,128]{2,1,0:T(4,128)(2,1)S(1)} async-done(((bf16[32,4,128]{2,1,0:T(4,128)(2,1)}), bf16[32,4,128]{2,1,0:T(4,128)(2,1)S(1)}, u32[]{:S(2)}, u32[]{:S(2)}) %all-to-all-start) | async-done | bytes 32800 | tf_op jit(solution)/shard_map/all_to_all | solution.py:19
  31.7 0.0 collective-permute-done.1
  31.7 0.0 collective-permute-done.other
  31.8 0.0 copy-start.2
  31.8 0.1 slice_convert_fusion
  31.8 0.1 fusion
  32.0 0.2 fusion.5
  32.2 0.1 copy.22
  32.3 0.1 compare_and_fusion
  32.4 0.2 convolution_convert_fusion
  32.6 0.1 copy.23
  32.8 0.7 reshape.57
  33.5 19.3 %all-to-all-start.1 = ((bf16[32,4,448]{2,1,0:T(4,128)(2,1)}), bf16[32,4,448]{2,1,0:T(4,128)(2,1)S(1)}, u32[]{:S(2)}, u32[]{:S(2)}) async-start(bf16[32,4,448]{2,1,0:T(4,128)(2,1)} %reshape.57), calls=%async_computation.1 | async-start | bytes 262144 | tf_op jit(solution)/shard_map/all_to_all | solution.py:19
  52.7 2.4 %shard_map.114 = (bf16[2,64,576]{2,1,0:T(8,128)(2,1)}, bf16[2,64,576]{2,1,0:T(8,128)(2,1)}) custom-call(s32[1,4]{1,0:T(1,128)} %moves, bf16[8,64,576]{2,1,0:T(8,128)(2,1)} %pool.1, bf16[8,64,576]{2,1,0:T(8,128)(2,1)} %pool.1), custom_call_target="tpu_custom_call" | custom-call | bytes 589824 | tf_op jit(solution)/shard_map/pallas_call | solution.py:99
  55.1 2.8 %collective-permute-start.2 = (bf16[2,64,576]{2,1,0:T(8,128)(2,1)}, bf16[2,64,576]{2,1,0:T(8,128)(2,1)S(1)}, u32[]{:S(2)}, u32[]{:S(2)}) collective-permute-start(bf16[2,64,576]{2,1,0:T(8,128)(2,1)} %get-tuple-element.23), channel_id=1, source_target_pairs={{0,1},{1,2},{2,3},{3,4},{4,5},{5,6},{6,7},{7,8},{8,9},{9,10},{10,1... | collective-permute-start | bytes 442376 | tf_op jit(solution)/shard_map/ppermute | solution.py:262
  57.9 0.0 copy-done.2
  57.9 1.9 %collective-permute-start.3 = (bf16[2,64,576]{2,1,0:T(8,128)(2,1)}, bf16[2,64,576]{2,1,0:T(8,128)(2,1)S(1)}, u32[]{:S(2)}, u32[]{:S(2)}) collective-permute-start(bf16[2,64,576]{2,1,0:T(8,128)(2,1)} %get-tuple-element.24), channel_id=1, source_target_pairs={{1,0},{2,1},{3,2},{4,3},{5,4},{6,5},{7,6},{8,7},{9,8},{10,9},{11,1... | collective-permute-start | bytes 442376 | tf_op jit(solution)/shard_map/ppermute | solution.py:263
  59.8 0.0 copy-done.5
  59.8 0.6 copy.24
  60.5 1.6 copy.25
  62.0 20.5 %all-to-all-done.1 = bf16[32,4,448]{2,1,0:T(4,128)(2,1)S(1)} async-done(((bf16[32,4,448]{2,1,0:T(4,128)(2,1)}), bf16[32,4,448]{2,1,0:T(4,128)(2,1)S(1)}, u32[]{:S(2)}, u32[]{:S(2)}) %all-to-all-start.1) | async-done | bytes 114720 | tf_op jit(solution)/shard_map/all_to_all | solution.py:19
  82.5 0.1 reshape.58
  82.6 0.0 collective-permute-done.2.low
  82.6 0.0 collective-permute-done.3.high
  82.6 0.1 copy.26
  82.7 0.0 copy-start.1
  82.8 0.1 broadcast_in_dim.24
  82.9 13.9 %all_to_all.30.values = bf16[8,448,128]{2,1,0:T(8,128)(2,1)S(1)} all-to-all(bf16[8,448,128]{2,1,0:T(8,128)(2,1)S(1)} %broadcast_in_dim.24), channel_id=1, replica_groups=mesh['z'=32,'h'=2,'y'=2,'x'=4,'c'=2] {'y','x'}, dimensions={0} | all-to-all | bytes 1835008 | tf_op jit(solution)/shard_map/all_to_all | solution.py:19
  96.8 0.0 copy-done.1
  96.8 0.0 copy-start.3
  96.8 1.5 copy-done.3
  98.3 0.8 shard_map.115
  99.1 3.2 %collective-permute-start.4 = (bf16[128,512]{1,0:T(8,128)(2,1)S(1)}, bf16[128,512]{1,0:T(8,128)(2,1)S(1)}, u32[]{:S(2)}, u32[]{:S(2)}) collective-permute-start(bf16[128,512]{1,0:T(8,128)(2,1)S(1)} %get-tuple-element.30), channel_id=1, source_target_pairs={{0,16},{16,0},{1,17},{17,1},{2,18},{18,2},{3,19},{19,3},{4,20},{20... | collective-permute-start | bytes 393224 | tf_op jit(solution)/shard_map/ppermute | solution.py:271
  102.3 4.0 %collective-permute-done.4.partner = bf16[128,512]{1,0:T(8,128)(2,1)S(1)} collective-permute-done((bf16[128,512]{1,0:T(8,128)(2,1)S(1)}, bf16[128,512]{1,0:T(8,128)(2,1)S(1)}, u32[]{:S(2)}, u32[]{:S(2)}) %collective-permute-start.4) | collective-permute-done | bytes 131104 | tf_op jit(solution)/shard_map/ppermute | solution.py:271
  106.3 0.7 shard_map.116
  106.9 0.0 copy-start.6
  107.0 0.0 copy-start
  107.0 0.0 copy-start.4
  107.0 12.7 %all_to_all.31.parts = bf16[8,448,128]{2,1,0:T(8,128)(2,1)S(1)} all-to-all(bf16[8,448,128]{2,1,0:T(8,128)(2,1)S(1)} %shard_map.116), channel_id=1, replica_groups=mesh['z'=32,'h'=2,'y'=2,'x'=4,'c'=2] {'y','x'}, dimensions={0} | all-to-all | bytes 1835008 | tf_op jit(solution)/shard_map/all_to_all | solution.py:19
  119.7 0.8 shard_map.117
  120.5 12.9 %all-to-all-start.4 = ((bf16[32,4,448]{2,1,0:T(4,128)(2,1)}), bf16[32,4,448]{2,1,0:T(4,128)(2,1)S(1)}, u32[]{:S(2)}, u32[]{:S(2)}) async-start(bf16[32,4,448]{2,1,0:T(4,128)(2,1)} %shard_map.117), calls=%async_computation.4 | async-start | bytes 262144 | tf_op jit(solution)/shard_map/all_to_all | solution.py:19
  133.4 0.0 copy-done.6
  133.4 0.2 copy.27.queries
  134.3 0.2 convert_reduce_fusion
  134.4 0.1 fusion.4
  134.5 0.2 select_reduce_fusion
  134.7 0.1 copy.28
  134.8 0.0 copy-done
  134.8 0.0 copy-done.4
  134.8 1.9 %shard_map.118 = bf16[1,128,512]{2,1,0:T(8,128)(2,1)} custom-call(s32[1,8]{1,0:T(1,128)S(1)} %copy-done.4, s32[1]{0:T(128)S(6)} %copy.35.lengths, bf16[1,128,576]{2,1,0:T(8,128)(2,1)S(1)} %copy.27.queries, bf16[8,64,576]{2,1,0:T(8,128)(2,1)S(1)} %copy-done, bf16[2,64,576]{2,1,0:T(8,128)(2,1)S(1)} %collective-permute-done.2.low, ...), custom_call_target="tpu_custom_call" | custom-call | flops 142606336 | bytes 884736 | tf_op jit(solution)/shard_map/pallas_call | solution.py:145
  136.7 22.9 %all-to-all-done.4 = bf16[32,4,448]{2,1,0:T(4,128)(2,1)S(1)} async-done(((bf16[32,4,448]{2,1,0:T(4,128)(2,1)}), bf16[32,4,448]{2,1,0:T(4,128)(2,1)S(1)}, u32[]{:S(2)}, u32[]{:S(2)}) %all-to-all-start.4) | async-done | bytes 114720 | tf_op jit(solution)/shard_map/all_to_all | solution.py:19
  159.6 0.1 reshape.61
  159.7 0.2 convolution_convert_fusion.1
  159.9 0.1 reshape.62
  160.0 17.7 %all_to_all.32 = bf16[32,2,224]{2,1,0:T(2,128)(2,1)S(1)} all-to-all(bf16[32,2,224]{2,1,0:T(2,128)(2,1)S(1)} %reshape.62), channel_id=1, replica_groups=mesh['z'=32,'h'=2,'y'=2,'x'=4,'c'=2] {'h','y','x','c'}, dimensions={0} | all-to-all | bytes 57344 | tf_op jit(solution)/shard_map/all_to_all | solution.py:19
  177.7 0.1 reshape.63
  177.8 0.1 reduce_sum.32
  177.9 0.7 reshape.64
  (6 shorter events, 0.1 us)
Async XLA Ops:
  0.6 59.2 %copy-start.5 = (bf16[1,1,128,3584]{3,2,1,0:T(8,128)(2,1)S(1)}, bf16[1,1,128,3584]{3,2,1,0:T(8,128)(2,1)}, u32[]{:S(2)}) copy-start(bf16[1,1,128,3584]{3,2,1,0:T(8,128)(2,1)} %param.14) | copy-start | bytes 2752516
  0.6 31.1 %collective-permute-start = (bf16[8,448,256]{2,1,0:T(8,128)(2,1)}, bf16[8,448,256]{2,1,0:T(8,128)(2,1)S(1)}, u32[]{:S(2)}, u32[]{:S(2)}) collective-permute-start(bf16[8,448,256]{2,1,0:T(8,128)(2,1)} %bitcast.21), channel_id=1, source_target_pairs={{0,1},{1,0},{2,3},{3,2},{4,5},{5,4},{6,7},{7,6},{8,9},{9,8},{10,11... | collective-permute-start | bytes 5505032 | tf_op jit(solution)/shard_map/ppermute | solution.py:233
  16.8 14.9 %collective-permute-start.1 = (bf16[1,1,128,3584]{3,2,1,0:T(8,128)(2,1)}, bf16[1,1,128,3584]{3,2,1,0:T(8,128)(2,1)}, u32[]{:S(2)}, u32[]{:S(2)}) collective-permute-start(bf16[1,1,128,3584]{3,2,1,0:T(8,128)(2,1)} %param.14), channel_id=1, source_target_pairs={{0,1},{1,0},{2,3},{3,2},{4,5},{5,4},{6,7},{7,6},{8,9},{9,8},{10,11... | collective-permute-start | bytes 2752520 | tf_op jit(solution)/shard_map/ppermute | solution.py:234
  20.4 11.4 %all-to-all-start = ((bf16[32,4,128]{2,1,0:T(4,128)(2,1)}), bf16[32,4,128]{2,1,0:T(4,128)(2,1)S(1)}, u32[]{:S(2)}, u32[]{:S(2)}) async-start(bf16[32,4,128]{2,1,0:T(4,128)(2,1)} %shard_map.113), calls=%async_computation | async-start | bytes 65536 | tf_op jit(solution)/shard_map/all_to_all | solution.py:19
  31.8 26.1 %copy-start.2 = (bf16[8,448,256]{2,1,0:T(8,128)(2,1)}, bf16[8,448,256]{2,1,0:T(8,128)(2,1)S(1)}, u32[]{:S(2)}) copy-start(bf16[8,448,256]{2,1,0:T(8,128)(2,1)S(1)} %collective-permute-done.other) | copy-start | bytes 5505028
  33.5 49.1 %all-to-all-start.1 = ((bf16[32,4,448]{2,1,0:T(4,128)(2,1)}), bf16[32,4,448]{2,1,0:T(4,128)(2,1)S(1)}, u32[]{:S(2)}, u32[]{:S(2)}) async-start(bf16[32,4,448]{2,1,0:T(4,128)(2,1)} %reshape.57), calls=%async_computation.1 | async-start | bytes 262144 | tf_op jit(solution)/shard_map/all_to_all | solution.py:19
  55.1 27.5 %collective-permute-start.2 = (bf16[2,64,576]{2,1,0:T(8,128)(2,1)}, bf16[2,64,576]{2,1,0:T(8,128)(2,1)S(1)}, u32[]{:S(2)}, u32[]{:S(2)}) collective-permute-start(bf16[2,64,576]{2,1,0:T(8,128)(2,1)} %get-tuple-element.23), channel_id=1, source_target_pairs={{0,1},{1,2},{2,3},{3,4},{4,5},{5,6},{6,7},{7,8},{8,9},{9,10},{10,1... | collective-permute-start | bytes 442376 | tf_op jit(solution)/shard_map/ppermute | solution.py:262
  57.9 24.7 %collective-permute-start.3 = (bf16[2,64,576]{2,1,0:T(8,128)(2,1)}, bf16[2,64,576]{2,1,0:T(8,128)(2,1)S(1)}, u32[]{:S(2)}, u32[]{:S(2)}) collective-permute-start(bf16[2,64,576]{2,1,0:T(8,128)(2,1)} %get-tuple-element.24), channel_id=1, source_target_pairs={{1,0},{2,1},{3,2},{4,3},{5,4},{6,5},{7,6},{8,7},{9,8},{10,9},{11,1... | collective-permute-start | bytes 442376 | tf_op jit(solution)/shard_map/ppermute | solution.py:263
  82.7 14.0 %copy-start.1 = (bf16[1,1,3584,256]{3,2,1,0:T(8,128)(2,1)S(1)}, bf16[1,1,3584,256]{3,2,1,0:T(8,128)(2,1)}, u32[]{:S(2)}) copy-start(bf16[1,1,3584,256]{3,2,1,0:T(8,128)(2,1)} %param.13) | copy-start | bytes 5505028
  96.8 1.5 copy-start.3
  99.1 7.2 %collective-permute-start.4 = (bf16[128,512]{1,0:T(8,128)(2,1)S(1)}, bf16[128,512]{1,0:T(8,128)(2,1)S(1)}, u32[]{:S(2)}, u32[]{:S(2)}) collective-permute-start(bf16[128,512]{1,0:T(8,128)(2,1)S(1)} %get-tuple-element.30), channel_id=1, source_target_pairs={{0,16},{16,0},{1,17},{17,1},{2,18},{18,2},{3,19},{19,3},{4,20},{20... | collective-permute-start | bytes 393224 | tf_op jit(solution)/shard_map/ppermute | solution.py:271
  106.9 26.5 %copy-start.6 = (bf16[1,128,576]{1,2,0:T(8,128)(2,1)S(1)}, bf16[1,128,576]{1,2,0:T(8,128)(2,1)}, u32[]{:S(2)}) copy-start(bf16[1,128,576]{1,2,0:T(8,128)(2,1)} %param.15) | copy-start | bytes 442372
  107.0 27.8 %copy-start = (bf16[8,64,576]{2,1,0:T(8,128)(2,1)S(1)}, bf16[8,64,576]{2,1,0:T(8,128)(2,1)}, u32[]{:S(2)}) copy-start(bf16[8,64,576]{2,1,0:T(8,128)(2,1)} %pool.1) | copy-start | bytes 1769476
  107.0 27.8 %copy-start.4 = (s32[1,8]{1,0:T(1,128)S(1)}, s32[1,8]{1,0:T(1,128)}, u32[]{:S(2)}) copy-start(s32[1,8]{1,0:T(1,128)} %page_list.1) | copy-start | bytes 100
  120.5 39.1 %all-to-all-start.4 = ((bf16[32,4,448]{2,1,0:T(4,128)(2,1)}), bf16[32,4,448]{2,1,0:T(4,128)(2,1)S(1)}, u32[]{:S(2)}, u32[]{:S(2)}) async-start(bf16[32,4,448]{2,1,0:T(4,128)(2,1)} %shard_map.117), calls=%async_computation.4 | async-start | bytes 262144 | tf_op jit(solution)/shard_map/all_to_all | solution.py:19

commit v9 on v8

--- a/solution.py
+++ b/solution.py
@@ -190,14 +190,17 @@
     sums = parts[0].astype(jnp.float32)
     for n in range(1, parts.shape[0]):
         sums += parts[n].astype(jnp.float32)
-    out[...] = sums.T.reshape(out.shape).astype(out.dtype)
+    sums = sums.T
+    half = sums.shape[0] // 2
+    sums = jnp.concatenate([sums[:half], sums[half:]], axis=1)
+    out[...] = sums.reshape(out.shape).astype(out.dtype)
 
 
 def added(parts, groups):
     _, width, rows = parts.shape
     return pl.pallas_call(
         sum_kernel,
-        out_shape=jax.ShapeDtypeStruct((groups, rows // groups, width), jnp.bfloat16),
+        out_shape=jax.ShapeDtypeStruct((groups, rows // groups // 2, 2 * width), jnp.bfloat16),
         in_specs=whole(1),
         out_specs=pl.BlockSpec(memory_space=pltpu.VMEM),
         compiler_params=pltpu.CompilerParams(vmem_limit_bytes=24 << 20),
@@ -250,12 +253,19 @@
     )
     slot_number = (jnp.arange(slots) + lax.axis_index("c") * slots).astype(jnp.float32)
     selector = member.T[:, None, :] & (position.T[:, None, :] == slot_number[None, :, None])
-    sent_rows = jnp.dot(
-        selector.astype(jnp.bfloat16).reshape(rows, members),
-        held[:, :width],
-        preferred_element_type=jnp.float32,
-    ).astype(jnp.bfloat16)
-    arrived = exchanged(sent_rows.reshape(groups, slots, width), "z").reshape(rows, width)
+    selector = selector.reshape(groups, slots // 2, 2, members)
+    sides = [selector[:, :, n].reshape(rows // 2, members) for n in range(2)]
+    sent_rows = jnp.concatenate(
+        [
+            jnp.dot(
+                side.astype(jnp.bfloat16), held[:, :width], preferred_element_type=jnp.float32
+            ).astype(jnp.bfloat16)
+            for side in sides
+        ],
+        axis=1,
+    )
+    paired = (groups, slots // 2, 2 * width)
+    arrived = exchanged(sent_rows.reshape(paired), "z").reshape(rows // 2, 2 * width)
     to_lower, to_higher = departing_pages(latent_pool, page_moves)
     forward = [(i, (i + 1) % members) for i in range(members)]
     backward = [(target, source) for source, target in forward]
@@ -266,19 +276,22 @@
     arrived, low, high, down, other_down = lax.optimization_barrier(
         (arrived, low, high, down, other_down)
     )
-    gathered = exchanged(jnp.broadcast_to(arrived.T[None], (chips, width, rows)), ("y", "x"))
+    arrived = jnp.concatenate([arrived[:, :width].T, arrived[:, width:].T], axis=1)
+    gathered = exchanged(jnp.broadcast_to(arrived[None], (chips, width, rows)), ("y", "x"))
     sums, rounded = gate_up_sums(gathered, gate_up, other_gate_up)
     partner = lax.ppermute(rounded, "h", [(0, 1), (1, 0)])
     block_sums = down_sums(sums, partner, down, other_down)
     summed = added(exchanged(block_sums, ("y", "x")), groups)
     summed, low, high = lax.optimization_barrier((summed, low, high))
     attention_latent = attention(queries, latent_pool, low, high, page_list, lengths)
-    returned = exchanged(summed, "z").reshape(rows, width)
+    returned = exchanged(summed, "z").reshape(rows // 2, 2 * width)
     returned, attention_latent = lax.optimization_barrier((returned, attention_latent))
-    weighted = jnp.where(selector, weight_of.T[:, None, :], 0.0).reshape(rows, members)
-    mixed = jnp.einsum(
-        "rn,rk->nk", weighted, returned.astype(jnp.float32), precision=lax.Precision.HIGHEST
-    )
+    weight_rows = weight_of.T[:, None, :]
+    mixed = jnp.zeros((members, width), jnp.float32)
+    for n in range(2):
+        weighted = jnp.where(selector[:, :, n], weight_rows, 0.0).reshape(rows // 2, members)
+        values = returned[:, n * width : (n + 1) * width].astype(jnp.float32)
+        mixed += jnp.einsum("rn,rk->nk", weighted, values, precision=lax.Precision.HIGHEST)
     mixed = mixed.astype(jnp.bfloat16).reshape(members, 2, width // 2)
     halves = exchanged(mixed, EP).reshape(members // 2, 2, width)
     expert_mix = jnp.sum(halves.astype(jnp.float32), axis=1).astype(jnp.bfloat16).reshape(1, -1)

time: 179 us -> 177 us (0.989)
  no operation moved by 1% of the time
where the time goes in v9:
time: 177 us
  starting transfers between devices  62.1 us (35%)
  waiting for transfers between devices  53.6 us (30%)
  blocking collectives  43 us (24%)
  Pallas kernels  8.33 us (5%)
  local copies, waits for them, and re-layouts  6.17 us (3%)
    all_to_all x3, waiting for transfers between devices, exchanged(): return lax.all_to_all(value, axes, split_axis=0, concat_axis=0, tiled=True)  49.1 us
    all_to_all x3, blocking collectives, exchanged(): return lax.all_to_all(value, axes, split_axis=0, concat_axis=0, tiled=True)  43 us
    all_to_all x3, starting transfers between devices, exchanged(): return lax.all_to_all(value, axes, split_axis=0, concat_axis=0, tiled=True)  36.6 us
    ppermute x1, starting transfers between devices, shards(): other_gate_up = lax.ppermute(gate_up, 'c', between_cores)  16.2 us
    ppermute x1, waiting for transfers between devices, shards(): partner = lax.ppermute(rounded, 'h', [(0, 1), (1, 0)])  4.45 us
  transfers between devices with their start and end apart: 8, of which 4 were waited for; matrix products, arithmetic and copies ran while one was open for 2% of the time, Pallas kernels for 3%

profile of v9, /device:TPU:1, one launch (start us, length us, event | category | flops | bytes accessed | tf_op | source)
XLA Modules:
  0.0 176.7 jit_solution(16684901444362345690)
XLA Ops:
  0.6 0.0 copy-start.5
  0.6 16.2 %collective-permute-start = (bf16[8,448,256]{2,1,0:T(8,128)(2,1)}, bf16[8,448,256]{2,1,0:T(8,128)(2,1)S(1)}, u32[]{:S(2)}, u32[]{:S(2)}) collective-permute-start(bf16[8,448,256]{2,1,0:T(8,128)(2,1)} %bitcast.26), channel_id=1, source_target_pairs={{0,1},{1,0},{2,3},{3,2},{4,5},{5,4},{6,7},{7,6},{8,9},{9,8},{10,11... | collective-permute-start | bytes 5505032 | tf_op jit(solution)/shard_map/ppermute | solution.py:236
  16.8 1.9 %collective-permute-start.1 = (bf16[1,1,128,3584]{3,2,1,0:T(8,128)(2,1)}, bf16[1,1,128,3584]{3,2,1,0:T(8,128)(2,1)}, u32[]{:S(2)}, u32[]{:S(2)}) collective-permute-start(bf16[1,1,128,3584]{3,2,1,0:T(8,128)(2,1)} %param.14), channel_id=1, source_target_pairs={{0,1},{1,0},{2,3},{3,2},{4,5},{5,4},{6,7},{7,6},{8,9},{9,8},{10,11... | collective-permute-start | bytes 2752520 | tf_op jit(solution)/shard_map/ppermute | solution.py:237
  18.8 1.6 shard_map.113
  20.4 4.0 %all-to-all-start = ((bf16[32,4,128]{2,1,0:T(4,128)(2,1)}), bf16[32,4,128]{2,1,0:T(4,128)(2,1)S(1)}, u32[]{:S(2)}, u32[]{:S(2)}) async-start(bf16[32,4,128]{2,1,0:T(4,128)(2,1)} %shard_map.113), calls=%async_computation | async-start | bytes 65536 | tf_op jit(solution)/shard_map/all_to_all | solution.py:19
  24.4 7.3 %all-to-all-done = bf16[32,4,128]{2,1,0:T(4,128)(2,1)S(1)} async-done(((bf16[32,4,128]{2,1,0:T(4,128)(2,1)}), bf16[32,4,128]{2,1,0:T(4,128)(2,1)S(1)}, u32[]{:S(2)}, u32[]{:S(2)}) %all-to-all-start) | async-done | bytes 32800 | tf_op jit(solution)/shard_map/all_to_all | solution.py:19
  31.7 0.0 collective-permute-done.1
  31.7 0.0 collective-permute-done.other
  31.8 0.0 copy-start.2
  31.8 0.1 slice_convert_fusion
  31.8 0.1 fusion.1
  32.0 0.2 fusion.12
  32.2 0.1 copy.21
  32.2 0.1 compare_and_fusion
  32.4 0.1 convolution_convert_fusion.1
  32.6 0.1 convolution_convert_fusion
  32.8 0.1 pad_maximum_fusion.1
  32.9 0.7 reshape.57
  33.6 19.3 %all-to-all-start.1 = ((bf16[32,2,896]{2,1,0:T(2,128)(2,1)}), bf16[32,2,896]{2,1,0:T(2,128)(2,1)S(1)}, u32[]{:S(2)}, u32[]{:S(2)}) async-start(bf16[32,2,896]{2,1,0:T(2,128)(2,1)} %reshape.57), calls=%async_computation.1 | async-start | bytes 229376 | tf_op jit(solution)/shard_map/all_to_all | solution.py:19
  52.8 2.4 %shard_map.114 = (bf16[2,64,576]{2,1,0:T(8,128)(2,1)}, bf16[2,64,576]{2,1,0:T(8,128)(2,1)}) custom-call(s32[1,4]{1,0:T(1,128)} %moves, bf16[8,64,576]{2,1,0:T(8,128)(2,1)} %pool.1, bf16[8,64,576]{2,1,0:T(8,128)(2,1)} %pool.1), custom_call_target="tpu_custom_call" | custom-call | bytes 589824 | tf_op jit(solution)/shard_map/pallas_call | solution.py:99
  55.2 2.8 %collective-permute-start.2 = (bf16[2,64,576]{2,1,0:T(8,128)(2,1)}, bf16[2,64,576]{2,1,0:T(8,128)(2,1)S(1)}, u32[]{:S(2)}, u32[]{:S(2)}) collective-permute-start(bf16[2,64,576]{2,1,0:T(8,128)(2,1)} %get-tuple-element.23), channel_id=1, source_target_pairs={{0,1},{1,2},{2,3},{3,4},{4,5},{5,6},{6,7},{7,8},{8,9},{9,10},{10,1... | collective-permute-start | bytes 442376 | tf_op jit(solution)/shard_map/ppermute | solution.py:272
  58.0 0.0 copy-done.2
  58.0 1.9 %collective-permute-start.3 = (bf16[2,64,576]{2,1,0:T(8,128)(2,1)}, bf16[2,64,576]{2,1,0:T(8,128)(2,1)S(1)}, u32[]{:S(2)}, u32[]{:S(2)}) collective-permute-start(bf16[2,64,576]{2,1,0:T(8,128)(2,1)} %get-tuple-element.24), channel_id=1, source_target_pairs={{1,0},{2,1},{3,2},{4,3},{5,4},{6,5},{7,6},{8,7},{9,8},{10,9},{11,1... | collective-permute-start | bytes 442376 | tf_op jit(solution)/shard_map/ppermute | solution.py:273
  59.9 0.0 copy-done.5
  59.9 0.6 copy.22
  60.6 1.6 copy.23
  62.1 19.4 %all-to-all-done.1 = bf16[32,2,896]{2,1,0:T(2,128)(2,1)S(1)} async-done(((bf16[32,2,896]{2,1,0:T(2,128)(2,1)}), bf16[32,2,896]{2,1,0:T(2,128)(2,1)S(1)}, u32[]{:S(2)}, u32[]{:S(2)}) %all-to-all-start.1) | async-done | bytes 114720 | tf_op jit(solution)/shard_map/all_to_all | solution.py:19
  81.6 0.0 collective-permute-done.2.low
  81.6 0.0 collective-permute-done.3.high
  81.6 0.1 slice_bitcast_fusion.1
  81.8 0.1 copy.24
  81.9 0.0 copy-start.1
  81.9 0.1 broadcast_in_dim.46
  82.0 15.1 %all_to_all.30.values = bf16[8,448,128]{2,1,0:T(8,128)(2,1)S(1)} all-to-all(bf16[8,448,128]{2,1,0:T(8,128)(2,1)S(1)} %broadcast_in_dim.46), channel_id=1, replica_groups=mesh['z'=32,'h'=2,'y'=2,'x'=4,'c'=2] {'y','x'}, dimensions={0} | all-to-all | bytes 1835008 | tf_op jit(solution)/shard_map/all_to_all | solution.py:19
  97.1 0.0 copy-done.1
  97.1 0.0 copy-start.3
  97.1 1.5 copy-done.3
  98.6 0.8 shard_map.115
  99.4 2.8 %collective-permute-start.4 = (bf16[128,512]{1,0:T(8,128)(2,1)S(1)}, bf16[128,512]{1,0:T(8,128)(2,1)S(1)}, u32[]{:S(2)}, u32[]{:S(2)}) collective-permute-start(bf16[128,512]{1,0:T(8,128)(2,1)S(1)} %get-tuple-element.30), channel_id=1, source_target_pairs={{0,16},{16,0},{1,17},{17,1},{2,18},{18,2},{3,19},{19,3},{4,20},{20... | collective-permute-start | bytes 393224 | tf_op jit(solution)/shard_map/ppermute | solution.py:282
  102.1 4.4 %collective-permute-done.4.partner = bf16[128,512]{1,0:T(8,128)(2,1)S(1)} collective-permute-done((bf16[128,512]{1,0:T(8,128)(2,1)S(1)}, bf16[128,512]{1,0:T(8,128)(2,1)S(1)}, u32[]{:S(2)}, u32[]{:S(2)}) %collective-permute-start.4) | collective-permute-done | bytes 131104 | tf_op jit(solution)/shard_map/ppermute | solution.py:282
  106.6 0.6 shard_map.116
  107.2 0.0 copy-start.6
  107.3 0.0 copy-start
  107.3 0.0 copy-start.4
  107.3 12.2 %all_to_all.31.parts = bf16[8,448,128]{2,1,0:T(8,128)(2,1)S(1)} all-to-all(bf16[8,448,128]{2,1,0:T(8,128)(2,1)S(1)} %shard_map.116), channel_id=1, replica_groups=mesh['z'=32,'h'=2,'y'=2,'x'=4,'c'=2] {'y','x'}, dimensions={0} | all-to-all | bytes 1835008 | tf_op jit(solution)/shard_map/all_to_all | solution.py:19
  119.5 1.0 shard_map.117
  120.5 13.3 %all-to-all-start.4 = ((bf16[32,2,896]{2,1,0:T(2,128)(2,1)}), bf16[32,2,896]{2,1,0:T(2,128)(2,1)S(1)}, u32[]{:S(2)}, u32[]{:S(2)}) async-start(bf16[32,2,896]{2,1,0:T(2,128)(2,1)} %shard_map.117), calls=%async_computation.4 | async-start | bytes 229376 | tf_op jit(solution)/shard_map/all_to_all | solution.py:19
  133.8 0.0 copy-done.6
  133.8 0.2 copy.25.queries
  134.7 0.2 convert_reduce_fusion
  134.8 0.1 fusion.9
  134.9 0.2 select_reduce_fusion
  135.1 0.1 copy.26
  135.2 0.0 copy-done
  135.2 0.0 copy-done.4
  135.2 1.9 %shard_map.118 = bf16[1,128,512]{2,1,0:T(8,128)(2,1)} custom-call(s32[1,8]{1,0:T(1,128)S(1)} %copy-done.4, s32[1]{0:T(128)S(6)} %copy.34.lengths, bf16[1,128,576]{2,1,0:T(8,128)(2,1)S(1)} %copy.25.queries, bf16[8,64,576]{2,1,0:T(8,128)(2,1)S(1)} %copy-done, bf16[2,64,576]{2,1,0:T(8,128)(2,1)S(1)} %collective-permute-done.2.low, ...), custom_call_target="tpu_custom_call" | custom-call | flops 142606336 | bytes 884736 | tf_op jit(solution)/shard_map/pallas_call | solution.py:145
  137.1 22.4 %all-to-all-done.4 = bf16[32,2,896]{2,1,0:T(2,128)(2,1)S(1)} async-done(((bf16[32,2,896]{2,1,0:T(2,128)(2,1)}), bf16[32,2,896]{2,1,0:T(2,128)(2,1)S(1)}, u32[]{:S(2)}, u32[]{:S(2)}) %all-to-all-start.4) | async-done | bytes 114720 | tf_op jit(solution)/shard_map/all_to_all | solution.py:19
  159.5 0.2 fusion.3
  159.7 0.3 fusion
  160.0 0.1 reshape.62
  160.1 15.7 %all_to_all.32 = bf16[32,2,224]{2,1,0:T(2,128)(2,1)S(1)} all-to-all(bf16[32,2,224]{2,1,0:T(2,128)(2,1)S(1)} %reshape.62), channel_id=1, replica_groups=mesh['z'=32,'h'=2,'y'=2,'x'=4,'c'=2] {'h','y','x','c'}, dimensions={0} | all-to-all | bytes 57344 | tf_op jit(solution)/shard_map/all_to_all | solution.py:19
  175.8 0.1 reshape.63
  175.9 0.1 reduce_sum.32
  176.0 0.7 reshape.64
  (9 shorter events, 0.2 us)
Async XLA Ops:
  0.6 59.3 %copy-start.5 = (bf16[1,1,128,3584]{3,2,1,0:T(8,128)(2,1)S(1)}, bf16[1,1,128,3584]{3,2,1,0:T(8,128)(2,1)}, u32[]{:S(2)}) copy-start(bf16[1,1,128,3584]{3,2,1,0:T(8,128)(2,1)} %param.14) | copy-start | bytes 2752516
  0.6 31.1 %collective-permute-start = (bf16[8,448,256]{2,1,0:T(8,128)(2,1)}, bf16[8,448,256]{2,1,0:T(8,128)(2,1)S(1)}, u32[]{:S(2)}, u32[]{:S(2)}) collective-permute-start(bf16[8,448,256]{2,1,0:T(8,128)(2,1)} %bitcast.26), channel_id=1, source_target_pairs={{0,1},{1,0},{2,3},{3,2},{4,5},{5,4},{6,7},{7,6},{8,9},{9,8},{10,11... | collective-permute-start | bytes 5505032 | tf_op jit(solution)/shard_map/ppermute | solution.py:236
  16.8 14.9 %collective-permute-start.1 = (bf16[1,1,128,3584]{3,2,1,0:T(8,128)(2,1)}, bf16[1,1,128,3584]{3,2,1,0:T(8,128)(2,1)}, u32[]{:S(2)}, u32[]{:S(2)}) collective-permute-start(bf16[1,1,128,3584]{3,2,1,0:T(8,128)(2,1)} %param.14), channel_id=1, source_target_pairs={{0,1},{1,0},{2,3},{3,2},{4,5},{5,4},{6,7},{7,6},{8,9},{9,8},{10,11... | collective-permute-start | bytes 2752520 | tf_op jit(solution)/shard_map/ppermute | solution.py:237
  20.4 11.4 %all-to-all-start = ((bf16[32,4,128]{2,1,0:T(4,128)(2,1)}), bf16[32,4,128]{2,1,0:T(4,128)(2,1)S(1)}, u32[]{:S(2)}, u32[]{:S(2)}) async-start(bf16[32,4,128]{2,1,0:T(4,128)(2,1)} %shard_map.113), calls=%async_computation | async-start | bytes 65536 | tf_op jit(solution)/shard_map/all_to_all | solution.py:19
  31.8 26.3 %copy-start.2 = (bf16[8,448,256]{2,1,0:T(8,128)(2,1)}, bf16[8,448,256]{2,1,0:T(8,128)(2,1)S(1)}, u32[]{:S(2)}) copy-start(bf16[8,448,256]{2,1,0:T(8,128)(2,1)S(1)} %collective-permute-done.other) | copy-start | bytes 5505028
  33.6 48.0 %all-to-all-start.1 = ((bf16[32,2,896]{2,1,0:T(2,128)(2,1)}), bf16[32,2,896]{2,1,0:T(2,128)(2,1)S(1)}, u32[]{:S(2)}, u32[]{:S(2)}) async-start(bf16[32,2,896]{2,1,0:T(2,128)(2,1)} %reshape.57), calls=%async_computation.1 | async-start | bytes 229376 | tf_op jit(solution)/shard_map/all_to_all | solution.py:19
  55.2 26.4 %collective-permute-start.2 = (bf16[2,64,576]{2,1,0:T(8,128)(2,1)}, bf16[2,64,576]{2,1,0:T(8,128)(2,1)S(1)}, u32[]{:S(2)}, u32[]{:S(2)}) collective-permute-start(bf16[2,64,576]{2,1,0:T(8,128)(2,1)} %get-tuple-element.23), channel_id=1, source_target_pairs={{0,1},{1,2},{2,3},{3,4},{4,5},{5,6},{6,7},{7,8},{8,9},{9,10},{10,1... | collective-permute-start | bytes 442376 | tf_op jit(solution)/shard_map/ppermute | solution.py:272
  58.0 23.6 %collective-permute-start.3 = (bf16[2,64,576]{2,1,0:T(8,128)(2,1)}, bf16[2,64,576]{2,1,0:T(8,128)(2,1)S(1)}, u32[]{:S(2)}, u32[]{:S(2)}) collective-permute-start(bf16[2,64,576]{2,1,0:T(8,128)(2,1)} %get-tuple-element.24), channel_id=1, source_target_pairs={{1,0},{2,1},{3,2},{4,3},{5,4},{6,5},{7,6},{8,7},{9,8},{10,9},{11,1... | collective-permute-start | bytes 442376 | tf_op jit(solution)/shard_map/ppermute | solution.py:273
  81.9 15.2 %copy-start.1 = (bf16[1,1,3584,256]{3,2,1,0:T(8,128)(2,1)S(1)}, bf16[1,1,3584,256]{3,2,1,0:T(8,128)(2,1)}, u32[]{:S(2)}) copy-start(bf16[1,1,3584,256]{3,2,1,0:T(8,128)(2,1)} %param.13) | copy-start | bytes 5505028
  97.1 1.5 copy-start.3
  99.4 7.2 %collective-permute-start.4 = (bf16[128,512]{1,0:T(8,128)(2,1)S(1)}, bf16[128,512]{1,0:T(8,128)(2,1)S(1)}, u32[]{:S(2)}, u32[]{:S(2)}) collective-permute-start(bf16[128,512]{1,0:T(8,128)(2,1)S(1)} %get-tuple-element.30), channel_id=1, source_target_pairs={{0,16},{16,0},{1,17},{17,1},{2,18},{18,2},{3,19},{19,3},{4,20},{20... | collective-permute-start | bytes 393224 | tf_op jit(solution)/shard_map/ppermute | solution.py:282
  107.2 26.6 %copy-start.6 = (bf16[1,128,576]{1,2,0:T(8,128)(2,1)S(1)}, bf16[1,128,576]{1,2,0:T(8,128)(2,1)}, u32[]{:S(2)}) copy-start(bf16[1,128,576]{1,2,0:T(8,128)(2,1)} %param.15) | copy-start | bytes 442372
  107.3 27.9 %copy-start = (bf16[8,64,576]{2,1,0:T(8,128)(2,1)S(1)}, bf16[8,64,576]{2,1,0:T(8,128)(2,1)}, u32[]{:S(2)}) copy-start(bf16[8,64,576]{2,1,0:T(8,128)(2,1)} %pool.1) | copy-start | bytes 1769476
  107.3 27.9 %copy-start.4 = (s32[1,8]{1,0:T(1,128)S(1)}, s32[1,8]{1,0:T(1,128)}, u32[]{:S(2)}) copy-start(s32[1,8]{1,0:T(1,128)} %page_list.1) | copy-start | bytes 100
  120.5 38.9 %all-to-all-start.4 = ((bf16[32,2,896]{2,1,0:T(2,128)(2,1)}), bf16[32,2,896]{2,1,0:T(2,128)(2,1)S(1)}, u32[]{:S(2)}, u32[]{:S(2)}) async-start(bf16[32,2,896]{2,1,0:T(2,128)(2,1)} %shard_map.117), calls=%async_computation.4 | async-start | bytes 229376 | tf_op jit(solution)/shard_map/all_to_all | solution.py:19
